TPU v7x, 512 devices: a whole 4x4x16 slice. The times are simulated.
512 devices in a mesh: ctx: 32 (over z_lo, y, core), head: 16 (over x, z_hi).
Axes of the slice: x: 4, y: 4, z: 16 (z_hi: 4, z_lo: 4; z = z_hi * 4 + z_lo), core: 2. Of those that a mesh axis runs over, the one named last changes fastest.
Arguments:
- q_nope: bfloat16 [4096, 16384], P('ctx', 'head'), may hold values from -6 to 6
- q_rope: bfloat16 [4096, 8192], P('ctx', 'head'), may hold values from -250 to 250
- latent: bfloat16 [4096, 512], P('ctx'), may hold values from -6 to 6
- k_rope: bfloat16 [4096, 64], P('ctx'), may hold values from -5 to 5
- d_out: bfloat16 [4096, 16384], P('ctx', 'head'), may hold values from -6 to 6
- advantage: float32 [4096], P('ctx'), may hold values from -4 to 4
- segment: int32 [4096], replicated, may hold values from 0 to 31, never falling along the last dimension, each value on 1 to 512 neighbouring positions
- w_uk: bfloat16 [512, 16384], P('ctx', 'head'), may hold values from -0.5 to 0.5
- w_uv: bfloat16 [512, 16384], P('ctx', 'head'), may hold values from -0.5 to 0.5
Outputs:
- d_q_nope: bfloat16 [4096, 16384], P('ctx', 'head')
- d_q_rope: bfloat16 [4096, 8192], P('ctx', 'head')
- d_latent: float32 [4096, 512], P(('ctx', 'head'))
- d_k_rope: float32 [4096, 64], P(('ctx', 'head'))
- d_w_uk: float32 [512, 16384], P('ctx', 'head')
- d_w_uv: float32 [512, 16384], P('ctx', 'head')
Inputs may be any that keep to these rules, and one draw needn't show every extreme that they name: Segment numbers never fall; each segment holds 1 to 512 tokens and one holds exactly 512.
All inputs are finite; a program needn't handle non-finite values.
Results may differ from a plain program's by a relative error of at most 0.03.
Values may be sent and summed in bfloat16 or wider, within the bound.
No kernel may reach another device: no remote copies, remote signals or barrier semaphores. Data moves between devices by JAX's collectives and lax.ppermute only.
A program may use at most 64 MiB of HBM per device.

v0:
```python
import math

import jax
import jax.numpy as jnp
from jax import lax
from jax.sharding import PartitionSpec as P

LAT = 512
ROPE = 64
NOPE = 128
VDIM = 128


def passed_along(value, axis, steps):
    count = lax.axis_size(axis)
    leading, last = (max(0, -steps), min(count, count - steps))
    return lax.ppermute(value, axis, [(source, source + steps) for source in range(leading, last)])


def return_blocks(lat_blocks, rope_blocks, reach_blocks):
    total_lat = lat_blocks[reach_blocks]
    total_rope = rope_blocks[reach_blocks]
    for distance in range(1, reach_blocks + 1):
        arrived = (
            passed_along(
                lat_blocks[reach_blocks - distance].astype(jnp.bfloat16), "ctx", -distance
            ).astype(jnp.float32),
            passed_along(
                rope_blocks[reach_blocks - distance].astype(jnp.bfloat16), "ctx", -distance
            ).astype(jnp.float32),
        )
        total_lat = total_lat + arrived[0]
        total_rope = total_rope + arrived[1]
    return (total_lat, total_rope)


def on_device(q_nope, q_rope, latent, k_rope, d_out, advantage, segment, w_uk, w_uv):
    rows_here = latent.shape[0]
    head_count = q_nope.shape[1] // NOPE
    score_scale = 1.0 / math.sqrt(NOPE + ROPE)
    ctx_count = lax.axis_size("ctx")
    reach_blocks = min(4, ctx_count // 2)
    device_index = lax.axis_index("ctx")
    keys_full, values_full = (
        lax.all_gather(w_uk, "ctx", axis=0, tiled=True),
        lax.all_gather(w_uv, "ctx", axis=0, tiled=True),
    )
    up_keys = keys_full.reshape(LAT, head_count, NOPE)
    up_values = values_full.reshape(LAT, head_count, VDIM)
    queries = q_nope.reshape(rows_here, head_count, NOPE)
    rotated = q_rope.reshape(rows_here, head_count, ROPE)
    weighted = (
        advantage[:, None, None] * d_out.reshape(rows_here, head_count, VDIM).astype(jnp.float32)
    ).astype(jnp.bfloat16)
    absorbed = jnp.einsum(
        "thn,chn->htc", queries, up_keys, preferred_element_type=jnp.float32
    ).astype(jnp.bfloat16)
    back_lat = jnp.einsum(
        "thv,chv->htc", weighted, up_values, preferred_element_type=jnp.float32
    ).astype(jnp.bfloat16)
    earlier = []
    for distance in range(1, reach_blocks + 1):
        earlier.append(passed_along((latent, k_rope), "ctx", distance))
    ordered = earlier[::-1] + [(latent, k_rope)]
    key_lat = jnp.concatenate([piece[0] for piece in ordered], axis=0)
    key_rope = jnp.concatenate([piece[1] for piece in ordered], axis=0)
    key_span = (reach_blocks + 1) * rows_here
    padded = jnp.concatenate([jnp.full((reach_blocks * rows_here,), -1, jnp.int32), segment])
    key_seg = lax.dynamic_slice_in_dim(padded, device_index * rows_here, key_span)
    query_seg = lax.dynamic_slice_in_dim(segment, device_index * rows_here, rows_here)
    key_place = jnp.arange(key_span, dtype=jnp.int32)
    query_place = reach_blocks * rows_here + jnp.arange(rows_here, dtype=jnp.int32)
    allowed = (key_seg[None, :] == query_seg[:, None]) & (
        key_place[None, :] <= query_place[:, None]
    )
    scores = jnp.einsum("htc,kc->htk", absorbed, key_lat, preferred_element_type=jnp.float32)
    scores = (
        scores + jnp.einsum("thr,kr->htk", rotated, key_rope, preferred_element_type=jnp.float32)
    ) * score_scale
    scores = jnp.where(allowed[None], scores, -jnp.inf)
    row_max = jnp.max(scores, axis=-1, keepdims=True)
    exponent = jnp.exp(scores - row_max)
    probs = exponent / jnp.sum(exponent, axis=-1, keepdims=True)
    probs_low = probs.astype(jnp.bfloat16)
    grad_prob = jnp.einsum("htc,kc->htk", back_lat, key_lat, preferred_element_type=jnp.float32)
    row_delta = jnp.sum(probs * grad_prob, axis=-1, keepdims=True)
    grad_score = (probs * (grad_prob - row_delta) * score_scale).astype(jnp.bfloat16)
    out_lat = jnp.einsum(
        "htk,kc->htc", probs_low, key_lat, preferred_element_type=jnp.float32
    ).astype(jnp.bfloat16)
    grad_abs = jnp.einsum(
        "htk,kc->htc", grad_score, key_lat, preferred_element_type=jnp.float32
    ).astype(jnp.bfloat16)
    d_q_rope = jnp.einsum(
        "htk,kr->thr", grad_score, key_rope, preferred_element_type=jnp.float32
    ).astype(jnp.bfloat16)
    d_q_rope = d_q_rope.reshape(rows_here, head_count * ROPE)
    d_q_nope = jnp.einsum(
        "htc,chn->thn", grad_abs, up_keys, preferred_element_type=jnp.float32
    ).astype(jnp.bfloat16)
    d_q_nope = d_q_nope.reshape(rows_here, head_count * NOPE)
    grad_lat = jnp.einsum("htk,htc->kc", grad_score, absorbed, preferred_element_type=jnp.float32)
    grad_lat = grad_lat + jnp.einsum(
        "htk,htc->kc", probs_low, back_lat, preferred_element_type=jnp.float32
    )
    grad_rope = jnp.einsum("htk,thr->kr", grad_score, rotated, preferred_element_type=jnp.float32)
    term_keys = jnp.einsum("htc,thn->chn", grad_abs, queries, preferred_element_type=jnp.float32)
    term_values = jnp.einsum("htc,thv->chv", out_lat, weighted, preferred_element_type=jnp.float32)
    stacked = lax.psum_scatter(
        jnp.concatenate(
            [
                term_keys.reshape(LAT // ctx_count * lax.axis_size("ctx"), head_count * NOPE),
                term_values.reshape(LAT // ctx_count * lax.axis_size("ctx"), head_count * VDIM),
            ],
            axis=1,
        ).astype(jnp.bfloat16),
        "ctx",
        scatter_dimension=0,
        tiled=True,
    ).astype(jnp.float32)
    d_w_uk = stacked[:, : head_count * NOPE]
    d_w_uv = stacked[:, head_count * NOPE :]
    lat_blocks = grad_lat.reshape(reach_blocks + 1, rows_here, LAT)
    rope_blocks = grad_rope.reshape(reach_blocks + 1, rows_here, ROPE)
    own_lat, own_rope = return_blocks(lat_blocks, rope_blocks, reach_blocks)
    d_latent, d_k_rope = (
        lax.psum_scatter(
            own_lat.astype(jnp.bfloat16), "head", scatter_dimension=0, tiled=True
        ).astype(jnp.float32),
        lax.psum_scatter(
            own_rope.astype(jnp.bfloat16), "head", scatter_dimension=0, tiled=True
        ).astype(jnp.float32),
    )
    return (d_q_nope, d_q_rope, d_latent, d_k_rope, d_w_uk, d_w_uv)


def solution(mesh):
    placed = (
        P("ctx", "head"),
        P("ctx", "head"),
        P("ctx", None),
        P("ctx", None),
        P("ctx", "head"),
        P("ctx"),
        P(),
        P("ctx", "head"),
        P("ctx", "head"),
    )
    return jax.shard_map(
        on_device,
        mesh=mesh,
        in_specs=placed,
        out_specs=(
            P("ctx", "head"),
            P("ctx", "head"),
            P(("ctx", "head"), None),
            P(("ctx", "head"), None),
            P("ctx", "head"),
            P("ctx", "head"),
        ),
        check_vma=False,
    )
```

profile of v0, /device:TPU:2, one launch (start us, length us, event | category | flops | bytes accessed | tf_op | source)
XLA Modules:
  0.0 474.7 jit_solution(14518885723245536122)
XLA Ops:
  7.2 0.0 all-gather.3.cloned.1.call-start
  7.2 0.7 all-gather.3.cloned.1.call-update
  7.9 0.0 all-gather.5.cloned.1.call-start
  7.9 3.5 collective-permute-start.6
  11.4 2.6 collective-permute-start.5
  14.1 4.8 %collective-permute-start.4 = (bf16[128,64]{0,1:T(8,128)(2,1)}, bf16[128,64]{0,1:T(8,128)(2,1)S(1)}, u32[]{:S(2)}, u32[]{:S(2)}) collective-permute-start(bf16[128,64]{0,1:T(8,128)(2,1)} %param.12), channel_id=1, source_target_pairs={{0,64},{16,80},{32,96},{48,112},{64,128},{80,144},{96,160},{112,17... | collective-permute-start | bytes 49160 | tf_op jit(solution)/shard_map/ppermute | solution.py:17
  18.9 3.0 collective-permute-start.7
  21.9 3.5 collective-permute-start.2
  25.4 0.0 all-gather.5.cloned.1.call-update
  25.4 0.0 reduce-scatter.4.cloned.1.call-start
  25.5 0.8 dynamic_slice.7
  26.3 0.8 pad_dynamic-slice_fusion
  27.0 0.8 fusion.33
  27.8 1.0 copy.50
  28.9 1.2 copy.73
  30.0 1.1 copy.70
  31.2 2.5 collective-permute-start.1
  33.7 5.1 %collective-permute-start = (bf16[128,512]{1,0:T(8,128)(2,1)}, bf16[128,512]{1,0:T(8,128)(2,1)S(1)}, u32[]{:S(2)}, u32[]{:S(2)}) collective-permute-start(bf16[128,512]{1,0:T(8,128)(2,1)} %param.11), channel_id=1, source_target_pairs={{0,64},{16,80},{32,96},{48,112},{64,128},{80,144},{96,160},{112,17... | collective-permute-start | bytes 393224 | tf_op jit(solution)/shard_map/ppermute | solution.py:17
  38.9 2.8 collective-permute-start.3
  41.7 0.7 constant_dynamic-update-slice_fusion.5
  42.5 2.1 fusion.39
  44.7 36.2 %all-gather.3.cloned.1.call-done = bf16[512,1024]{1,0:T(8,128)(2,1)} async-done(((bf16[16,1024]{1,0:T(8,128)(2,1)}), bf16[512,1024]{1,0:T(8,128)(2,1)}) %all-gather.3.cloned.1.call-update) | async-done | bytes 1048592 | tf_op jit(solution)/shard_map/all_gather | solution.py:45
  80.9 1.5 copy.47
  82.4 1.5 convolution_convert_fusion.5
  83.8 63.4 %all-gather.5.cloned.1.call-done = bf16[512,1024]{1,0:T(8,128)(2,1)} async-done(((bf16[16,1024]{1,0:T(8,128)(2,1)}), bf16[512,1024]{1,0:T(8,128)(2,1)}) %all-gather.5.cloned.1.call-update) | async-done | bytes 1048592 | tf_op jit(solution)/shard_map/all_gather | solution.py:46
  147.2 1.5 copy.53
  148.7 0.5 convolution_convert_fusion.4
  149.2 0.9 copy-done.5
  150.2 2.5 fusion.27
  152.7 1.1 fusion.3
  153.8 2.0 fusion.56
  155.8 4.7 %convolution_bitcast_fusion = f32[640,512]{1,0:T(8,128)} fusion(bf16[8,128,512]{2,1,0:T(8,128)(2,1)} %copy-done.5, f32[8,128]{1,0:T(8,128)S(1)} %get-tuple-element.34, f32[8,128,640]{2,1,0:T(8,128)S(1)} %fusion.3), kind=kOutput, calls=%fused_computation.16 | convolution fusion | flops 673056384 | bytes 4984832 | tf_op jit(solution)/shard_map/htk,htc->kc/dot_general | solution.py:103
  160.5 9.9 %convolution_convert_fusion.3 = bf16[8,128,512]{2,1,0:T(8,128)(2,1)} fusion(f32[8,128,640]{2,1,0:T(8,128)} %fusion.27, bf16[640,512]{1,0:T(8,128)(2,1)S(1)} %constant_dynamic-update-slice_fusion, f32[8,128,640]{2,1,0:T(8,128)} %get-tuple-element.35, f32[8,128]{1,0:T(8,128)S(1)} %get-tuple-element.34), kind=kOutput, calls=%fused_computation.13 | convolution fusion | flops 676202112 | bytes 6950912 | tf_op jit(solution)/shard_map/htk,kc->htc/dot_general | solution.py:91
  170.4 12.0 %fusion.57 = (bf16[640,512]{1,0:T(8,128)(2,1)}, f32[640,512]{1,0:T(8,128)}) fusion(f32[640,512]{1,0:T(8,128)} %convolution_bitcast_fusion, bf16[8,128,512]{2,1,0:T(8,128)(2,1)} %convolution_convert_fusion.5, f32[8,128,640]{2,1,0:T(8,128)} %fusion.27, f32[8,128,640]{2,1,0:T(8,128)} %get-tuple-element.35, f32[8,128]{1,0:T(8,128)S(1)} %get-tuple-element.34), kind=kOutput, calls=%fused_computation.73 | convolution fusion | flops 676333184 | bytes 9572352 | tf_op jit(solution)/shard_map/htk,htc->kc/dot_general | solution.py:102
  182.5 2.7 convolution_convert_fusion
  185.2 0.8 fusion.53
  186.0 1.3 collective-permute-start.8
  187.3 1.3 collective-permute-start.11
  188.6 1.3 collective-permute-start.10
  189.9 1.5 collective-permute-start.9
  191.4 4.8 %convolution_convert_fusion.1 = bf16[8,128,512]{2,1,0:T(8,128)(2,1)} fusion(bf16[640,512]{1,0:T(8,128)(2,1)S(1)} %constant_dynamic-update-slice_fusion, f32[128,8,128]{0,2,1:T(8,128)} %bitcast.72, f32[128]{0:T(128)S(1)} %copy-done.15, f32[8,128]{1,0:T(8,128)S(1)} %get-tuple-element.34, f32[8,128,640]{2,1,0:T(8,128)S(1)} %fusion.3), kind=kOutput, calls=%fused_computation.11 | convolution fusion | flops 808584832 | bytes 4854272 | tf_op jit(solution)/shard_map/htc,thv->chv/dot_general | solution.py:108
  196.1 1.6 copy.59
  197.7 0.5 copy.60
  198.3 0.3 collective-permute-done.10
  198.6 3.3 collective-permute-done.9
  201.9 1.8 fusion.37
  203.7 0.0 reduce-scatter.6.cloned.1.call-start
  203.8 1.6 pad_maximum_fusion
  205.4 1.3 dynamic-slice
  207.3 9.3 %fusion.60 = (bf16[640,64]{0,1:T(8,128)(2,1)S(1)}, f32[640,64]{0,1:T(8,128)S(1)}) fusion(bf16[128,8,64]{0,2,1:T(8,128)(2,1)S(1)} %bitcast.76, f32[8,128,640]{2,1,0:T(8,128)} %fusion.27, f32[8,128,640]{2,1,0:T(8,128)} %get-tuple-element.35, f32[8,128]{1,0:T(8,128)S(1)} %get-tuple-element.34), kind=kOutput, calls=%fused_computation.74 | convolution fusion | flops 88516224 | bytes 5623808 | tf_op jit(solution)/shard_map/htk,thr->kr/dot_general | solution.py:106
  216.7 1.3 collective-permute-start.12
  218.0 1.3 collective-permute-start.15
  219.3 1.3 collective-permute-start.14
  220.6 1.3 collective-permute-start.13
  221.9 0.4 convolution_convert_fusion.6
  222.3 9.5 %fusion.18 = bf16[64,8,128]{2,0,1:T(8,128)(2,1)S(1)} fusion(f32[8,128,640]{2,1,0:T(8,128)} %fusion.27, bf16[640,64]{0,1:T(8,128)(2,1)S(1)} %copy-done.14, f32[8,128,640]{2,1,0:T(8,128)} %get-tuple-element.35, f32[8,128]{1,0:T(8,128)S(1)} %get-tuple-element.34), kind=kOutput, calls=%fused_computation.23 | convolution fusion | flops 88540800 | bytes 5459968 | tf_op jit(solution)/shard_map/htk,kr->thr/dot_general | solution.py:94
  231.9 0.8 copy.62
  232.6 0.8 copy.61
  233.5 93.6 %all-reduce.1 = bf16[128,64]{0,1:T(8,128)(2,1)S(1)} all-reduce(bf16[128,64]{0,1:T(8,128)(2,1)S(1)} %fusion.44), channel_id=3, replica_groups=mesh['ctx'=32,'head'=16] {'head'}, use_global_device_ids=true, to_apply=%region_4.5.clone | all-reduce | flops 8192 | bytes 32768
  327.2 0.1 dynamic-slice_convert_fusion
  327.2 0.7 copy.63
  327.9 1.3 convert_element_type.104
  329.2 137.6 %reduce-scatter.6.cloned.1.call-done = bf16[16,2048]{1,0:T(8,128)(2,1)} async-done(((bf16[512,2048]{1,0:T(8,128)(2,1)}), bf16[16,2048]{1,0:T(8,128)(2,1)}) %reduce-scatter.6.cloned.1.call-update) | async-done | bytes 65552 | tf_op jit(solution)/shard_map/reduce_scatter | solution.py:109
  466.8 1.4 fusion.55
  (60 shorter events, 0.3 us)
Async XLA Ops:
  7.2 73.7 %all-gather.3.cloned.1.call-start = ((), (), s32[]{:S(2)}) async-start(), calls=%async_computation.2 | async-start | bytes 1081344 | tf_op jit(solution)/shard_map/all_gather | solution.py:45
  7.9 139.3 %all-gather.5.cloned.1.call-start = ((), (), s32[]{:S(2)}) async-start(), calls=%async_computation.3 | async-start | bytes 1081344 | tf_op jit(solution)/shard_map/all_gather | solution.py:46
  7.9 30.9 %collective-permute-start.6 = (bf16[128,64]{0,1:T(8,128)(2,1)}, bf16[128,64]{0,1:T(8,128)(2,1)S(1)}, u32[]{:S(2)}, u32[]{:S(2)}) collective-permute-start(bf16[128,64]{0,1:T(8,128)(2,1)} %param.12), channel_id=1, source_target_pairs={{0,32},{16,48},{32,64},{48,80},{64,96},{80,112},{96,128},{112,144}... | collective-permute-start | bytes 49160 | tf_op jit(solution)/shard_map/ppermute | solution.py:17
  11.4 22.3 %collective-permute-start.5 = (bf16[128,64]{0,1:T(8,128)(2,1)}, bf16[128,64]{0,1:T(8,128)(2,1)S(1)}, u32[]{:S(2)}, u32[]{:S(2)}) collective-permute-start(bf16[128,64]{0,1:T(8,128)(2,1)} %param.12), channel_id=1, source_target_pairs={{0,48},{16,64},{32,80},{48,96},{64,112},{80,128},{96,144},{112,160... | collective-permute-start | bytes 49160 | tf_op jit(solution)/shard_map/ppermute | solution.py:17
  14.1 17.1 %collective-permute-start.4 = (bf16[128,64]{0,1:T(8,128)(2,1)}, bf16[128,64]{0,1:T(8,128)(2,1)S(1)}, u32[]{:S(2)}, u32[]{:S(2)}) collective-permute-start(bf16[128,64]{0,1:T(8,128)(2,1)} %param.12), channel_id=1, source_target_pairs={{0,64},{16,80},{32,96},{48,112},{64,128},{80,144},{96,160},{112,17... | collective-permute-start | bytes 49160 | tf_op jit(solution)/shard_map/ppermute | solution.py:17
  18.9 22.8 %collective-permute-start.7 = (bf16[128,64]{0,1:T(8,128)(2,1)}, bf16[128,64]{0,1:T(8,128)(2,1)S(1)}, u32[]{:S(2)}, u32[]{:S(2)}) collective-permute-start(bf16[128,64]{0,1:T(8,128)(2,1)} %param.12), channel_id=1, source_target_pairs={{0,16},{16,32},{32,48},{48,64},{64,80},{80,96},{96,112},{112,128},... | collective-permute-start | bytes 49160 | tf_op jit(solution)/shard_map/ppermute | solution.py:17
  21.9 22.7 %collective-permute-start.2 = (bf16[128,512]{1,0:T(8,128)(2,1)}, bf16[128,512]{1,0:T(8,128)(2,1)S(1)}, u32[]{:S(2)}, u32[]{:S(2)}) collective-permute-start(bf16[128,512]{1,0:T(8,128)(2,1)} %param.11), channel_id=1, source_target_pairs={{0,32},{16,48},{32,64},{48,80},{64,96},{80,112},{96,128},{112,144}... | collective-permute-start | bytes 393224 | tf_op jit(solution)/shard_map/ppermute | solution.py:17
  25.4 302.5 %reduce-scatter.4.cloned.1.call-start = ((), (), s32[]{:S(2)}) async-start(), calls=%async_computation.4 | async-start | bytes 139264 | tf_op jit(solution)/shard_map/reduce_scatter | solution.py:127
  28.8 15.7 %copy-start.8 = (bf16[128,512]{0,1:T(8,128)(2,1)}, bf16[128,512]{0,1:T(8,128)(2,1)S(1)}, u32[]{:S(2)}) copy-start(bf16[128,512]{0,1:T(8,128)(2,1)S(1)} %copy.50) | copy-start | bytes 393220
  28.8 15.8 %copy-start.12 = (bf16[128,512]{1,0:T(8,128)(2,1)S(1)}, bf16[128,512]{1,0:T(8,128)(2,1)}, u32[]{:S(2)}) copy-start(bf16[128,512]{1,0:T(8,128)(2,1)} %param.11) | copy-start | bytes 393220
  31.1 117.6 %copy-start.6 = (f32[128,1024]{0,1:T(8,128)}, f32[128,1024]{0,1:T(8,128)S(1)}, u32[]{:S(2)}) copy-start(f32[128,1024]{0,1:T(8,128)S(1)} %copy.70) | copy-start | bytes 1572868
  31.2 13.4 %collective-permute-start.1 = (bf16[128,512]{1,0:T(8,128)(2,1)}, bf16[128,512]{1,0:T(8,128)(2,1)S(1)}, u32[]{:S(2)}, u32[]{:S(2)}) collective-permute-start(bf16[128,512]{1,0:T(8,128)(2,1)} %param.11), channel_id=1, source_target_pairs={{0,48},{16,64},{32,80},{48,96},{64,112},{80,128},{96,144},{112,160... | collective-permute-start | bytes 393224 | tf_op jit(solution)/shard_map/ppermute | solution.py:17
  33.7 10.8 %collective-permute-start = (bf16[128,512]{1,0:T(8,128)(2,1)}, bf16[128,512]{1,0:T(8,128)(2,1)S(1)}, u32[]{:S(2)}, u32[]{:S(2)}) collective-permute-start(bf16[128,512]{1,0:T(8,128)(2,1)} %param.11), channel_id=1, source_target_pairs={{0,64},{16,80},{32,96},{48,112},{64,128},{80,144},{96,160},{112,17... | collective-permute-start | bytes 393224 | tf_op jit(solution)/shard_map/ppermute | solution.py:17
  38.9 5.8 %collective-permute-start.3 = (bf16[128,512]{1,0:T(8,128)(2,1)}, bf16[128,512]{1,0:T(8,128)(2,1)S(1)}, u32[]{:S(2)}, u32[]{:S(2)}) collective-permute-start(bf16[128,512]{1,0:T(8,128)(2,1)} %param.11), channel_id=1, source_target_pairs={{0,16},{16,32},{32,48},{48,64},{64,80},{80,96},{96,112},{112,128},... | collective-permute-start | bytes 393224 | tf_op jit(solution)/shard_map/ppermute | solution.py:17
  42.5 2.1 copy-start.13
  82.4 66.9 %copy-start.1 = (bf16[512,1024]{0,1:T(8,128)(2,1)}, bf16[512,1024]{0,1:T(8,128)(2,1)S(1)}, u32[]{:S(2)}) copy-start(bf16[512,1024]{0,1:T(8,128)(2,1)S(1)} %copy.47) | copy-start | bytes 3145732
  82.4 66.4 %copy-start.15 = (f32[128]{0:T(128)S(1)}, f32[128]{0:T(128)}, u32[]{:S(2)}) copy-start(f32[128]{0:T(128)} %param.14) | copy-start | bytes 1540
  149.2 1.0 copy-start.5
  150.2 2.5 copy-start
  150.2 2.5 copy-start.4
  150.2 2.5 copy-start.11
  182.5 2.7 copy-start.10
  186.0 12.3 %collective-permute-start.8 = (bf16[128,512]{1,0:T(8,128)(2,1)}, bf16[128,512]{1,0:T(8,128)(2,1)S(1)}, u32[]{:S(2)}, u32[]{:S(2)}) collective-permute-start(bf16[128,512]{1,0:T(8,128)(2,1)} %get-tuple-element.24), channel_id=1, source_target_pairs={{16,0},{32,16},{48,32},{64,48},{80,64},{96,80},{112,96},{128,112},... | collective-permute-start | bytes 393224 | tf_op jit(solution)/shard_map/ppermute | solution.py:17
  187.3 11.0 %collective-permute-start.11 = (bf16[128,512]{1,0:T(8,128)(2,1)}, bf16[128,512]{1,0:T(8,128)(2,1)S(1)}, u32[]{:S(2)}, u32[]{:S(2)}) collective-permute-start(bf16[128,512]{1,0:T(8,128)(2,1)} %get-tuple-element.25), channel_id=1, source_target_pairs={{64,0},{80,16},{96,32},{112,48},{128,64},{144,80},{160,96},{176,11... | collective-permute-start | bytes 393224 | tf_op jit(solution)/shard_map/ppermute | solution.py:17
  188.6 10.0 %collective-permute-start.10 = (bf16[128,512]{1,0:T(8,128)(2,1)}, bf16[128,512]{1,0:T(8,128)(2,1)}, u32[]{:S(2)}, u32[]{:S(2)}) collective-permute-start(bf16[128,512]{1,0:T(8,128)(2,1)} %get-tuple-element.26), channel_id=1, source_target_pairs={{48,0},{64,16},{80,32},{96,48},{112,64},{128,80},{144,96},{160,112... | collective-permute-start | bytes 393224 | tf_op jit(solution)/shard_map/ppermute | solution.py:17
  189.9 12.0 %collective-permute-start.9 = (bf16[128,512]{1,0:T(8,128)(2,1)}, bf16[128,512]{1,0:T(8,128)(2,1)}, u32[]{:S(2)}, u32[]{:S(2)}) collective-permute-start(bf16[128,512]{1,0:T(8,128)(2,1)} %get-tuple-element.27), channel_id=1, source_target_pairs={{32,0},{48,16},{64,32},{80,48},{96,64},{112,80},{128,96},{144,112}... | collective-permute-start | bytes 393224 | tf_op jit(solution)/shard_map/ppermute | solution.py:17
  196.1 1.6 copy-start.7
  203.7 3.6 copy-start.9
  203.7 263.0 %reduce-scatter.6.cloned.1.call-start = ((), (), s32[]{:S(2)}) async-start(), calls=%async_computation.5 | async-start | bytes 2162688 | tf_op jit(solution)/shard_map/reduce_scatter | solution.py:109
  207.3 14.6 %copy-start.2 = (bf16[512,1024]{0,1:T(8,128)(2,1)S(1)}, bf16[512,1024]{0,1:T(8,128)(2,1)}, u32[]{:S(2)}) copy-start(bf16[512,1024]{0,1:T(8,128)(2,1)} %copy-done.1) | copy-start | bytes 3145732
  207.3 14.6 %copy-start.3 = (bf16[8,128,512]{2,1,0:T(8,128)(2,1)S(1)}, bf16[8,128,512]{2,1,0:T(8,128)(2,1)}, u32[]{:S(2)}) copy-start(bf16[8,128,512]{2,1,0:T(8,128)(2,1)} %convolution_convert_fusion.3) | copy-start | bytes 3145732
  207.3 15.0 %copy-start.14 = (bf16[640,64]{0,1:T(8,128)(2,1)S(1)}, bf16[640,64]{0,1:T(8,128)(2,1)}, u32[]{:S(2)}) copy-start(bf16[640,64]{0,1:T(8,128)(2,1)} %copy-done.13) | copy-start | bytes 245764
  216.7 16.8 %collective-permute-start.12 = (bf16[128,64]{0,1:T(8,128)(2,1)S(1)}, bf16[128,64]{0,1:T(8,128)(2,1)S(1)}, u32[]{:S(2)}, u32[]{:S(2)}) collective-permute-start(bf16[128,64]{0,1:T(8,128)(2,1)S(1)} %get-tuple-element.28), channel_id=1, source_target_pairs={{16,0},{32,16},{48,32},{64,48},{80,64},{96,80},{112,96},{128,112},... | collective-permute-start | bytes 49160 | tf_op jit(solution)/shard_map/ppermute | solution.py:17
  218.0 15.5 %collective-permute-start.15 = (bf16[128,64]{0,1:T(8,128)(2,1)S(1)}, bf16[128,64]{0,1:T(8,128)(2,1)S(1)}, u32[]{:S(2)}, u32[]{:S(2)}) collective-permute-start(bf16[128,64]{0,1:T(8,128)(2,1)S(1)} %get-tuple-element.29), channel_id=1, source_target_pairs={{64,0},{80,16},{96,32},{112,48},{128,64},{144,80},{160,96},{176,11... | collective-permute-start | bytes 49160 | tf_op jit(solution)/shard_map/ppermute | solution.py:17
  219.3 14.2 %collective-permute-start.14 = (bf16[128,64]{0,1:T(8,128)(2,1)S(1)}, bf16[128,64]{0,1:T(8,128)(2,1)S(1)}, u32[]{:S(2)}, u32[]{:S(2)}) collective-permute-start(bf16[128,64]{0,1:T(8,128)(2,1)S(1)} %get-tuple-element.30), channel_id=1, source_target_pairs={{48,0},{64,16},{80,32},{96,48},{112,64},{128,80},{144,96},{160,112... | collective-permute-start | bytes 49160 | tf_op jit(solution)/shard_map/ppermute | solution.py:17
  220.6 12.9 %collective-permute-start.13 = (bf16[128,64]{0,1:T(8,128)(2,1)S(1)}, bf16[128,64]{0,1:T(8,128)(2,1)S(1)}, u32[]{:S(2)}, u32[]{:S(2)}) collective-permute-start(bf16[128,64]{0,1:T(8,128)(2,1)S(1)} %get-tuple-element.31), channel_id=1, source_target_pairs={{32,0},{48,16},{64,32},{80,48},{96,64},{112,80},{128,96},{144,112}... | collective-permute-start | bytes 49160 | tf_op jit(solution)/shard_map/ppermute | solution.py:17
Sparse Core Ops, SparseCore 0:
  10.1 70.6 all-gather.2
  83.0 64.1 all-gather.4
  203.8 112.4 reduce-scatter.3
  319.2 147.5 reduce-scatter.5
where the time goes:
time: 476 us; the launch traced here: 475 us
  waiting for transfers between devices  241 us (51%)
  blocking collectives  93.6 us (20%)
  matrix products  61 us (13%)
  starting transfers between devices  38.6 us (8%)
  local copies, waits for them, and re-layouts  17.6 us (4%)
  between operations  15 us (3%)
  other arithmetic  7.55 us (2%)
    reduce_scatter x1, waiting for transfers between devices, on_device(): lax.psum_scatter(jnp.concatenate([term_keys.reshape(LAT // ctx_count * la...  138 us
    unnamed x1, blocking collectives  93.6 us
    all_gather x1, waiting for transfers between devices, on_device(): lax.all_gather(w_uv, 'ctx', axis=0, tiled=True)  63.4 us
    ppermute x16, starting transfers between devices, passed_along(): lax.ppermute(value, axis, [(source, source + steps) for source in range(l...  38.4 us
    all_gather x1, waiting for transfers between devices, on_device(): lax.all_gather(w_uk, 'ctx', axis=0, tiled=True)  36.2 us
    dot_general x1, matrix products, on_device(): jnp.einsum('htk,htc->kc', grad_score, absorbed, preferred_element_type=jn...  12 us
    dot_general x1, matrix products, on_device(): jnp.einsum('htk,kc->htc', grad_score, key_lat, preferred_element_type=jnp...  9.89 us
    dot_general x1, matrix products, on_device(): jnp.einsum('htk,kr->thr', grad_score, key_rope, preferred_element_type=jn...  9.54 us
  transfers between devices with their start and end apart: 20, of which 5 were waited for; matrix products, arithmetic and copies ran while one was open for 9% of the time, Pallas kernels for 0%

commit v1 on v0

v1 whole, which is shorter than its diff:
```python
import functools
import math

import jax
import jax.numpy as jnp
from jax import lax
from jax.experimental import pallas as pl
from jax.experimental.pallas import tpu as pltpu
from jax.sharding import PartitionSpec as P

LAT = 512
ROPE = 64
NOPE = 128
VDIM = 128
FAR = -1e30


def dot_nt(left, right):
    return lax.dot_general(
        left, right, (((1,), (1,)), ((), ())), preferred_element_type=jnp.float32
    )


def dot_nn(left, right):
    return lax.dot_general(
        left, right, (((1,), (0,)), ((), ())), preferred_element_type=jnp.float32
    )


def dot_tn(left, right):
    return lax.dot_general(
        left, right, (((0,), (0,)), ((), ())), preferred_element_type=jnp.float32
    )


def column_of(row, count):
    return jnp.transpose(jnp.broadcast_to(row, (count, count)))


def core_rows(value, side):
    pieces = value.reshape(value.shape[0] // 32, 2, 16, value.shape[1])
    return pieces[:, side].reshape(value.shape[0] // 2, value.shape[1])


def layer_kernel(
    place,
    advantage,
    segment,
    queries,
    rotated,
    cotangent,
    key4,
    key3,
    key2,
    key1,
    key0,
    weights_mine,
    weights_theirs,
    d_q_nope,
    d_q_rope,
    grad_earlier,
    grad_own,
    d_weights_mine,
    d_weights_theirs,
    weights,
    keys,
    keys_t,
    bias,
    absorbed,
    back_lat,
    probs_low,
    grad_score,
):
    rows = queries.shape[0]
    width = queries.shape[1]
    heads = width // NOPE
    span = keys.shape[0]
    reach = span // rows - 1
    scale = 1.0 / math.sqrt(NOPE + ROPE)
    index = place[0]
    core = lax.rem(index, 2)

    for piece in range(weights_mine.shape[0] // 16):
        source = slice(piece * 16, piece * 16 + 16)
        mine_at = pl.multiple_of(piece * 32 + core * 16, 16)
        theirs_at = pl.multiple_of(piece * 32 + 16 - core * 16, 16)
        weights[pl.ds(mine_at, 16), :] = weights_mine[source, :]
        weights[pl.ds(theirs_at, 16), :] = weights_theirs[source, :]

    for block, piece in enumerate((key4, key3, key2, key1, key0)):
        keys[block * rows : (block + 1) * rows, :] = piece[...]
        keys_t[:, block * rows : (block + 1) * rows] = jnp.transpose(piece[...])

    query_segment = segment[pl.ds(index, 1), :]
    query_at = lax.broadcasted_iota(jnp.int32, (rows, rows), 1)
    key_at = lax.broadcasted_iota(jnp.int32, (rows, rows), 0)
    for block in range(reach + 1):
        owner = index - (reach - block)
        key_row = segment[pl.ds(jnp.maximum(owner, 0), 1), :]
        key_segment = column_of(key_row, rows)
        allowed = (key_segment == query_segment) & (owner >= 0)
        if block == reach:
            allowed = allowed & (key_at <= query_at)
        bias[block * rows : (block + 1) * rows, :] = jnp.where(allowed, 0.0, FAR)

    advantage_column = column_of(advantage[...], rows)
    bias_pair = jnp.concatenate([bias[...], bias[...]], axis=1)

    for pair in range(heads // 2):
        both = slice(pair * 2 * rows, (pair + 1) * 2 * rows)
        weighted = []
        for head in (2 * pair, 2 * pair + 1):
            here = slice(head * rows, (head + 1) * rows)
            nope = slice(head * NOPE, (head + 1) * NOPE)
            values = slice(width + head * VDIM, width + (head + 1) * VDIM)
            absorbed[here, :LAT] = dot_nt(queries[:, nope], weights[:, nope]).astype(jnp.bfloat16)
            absorbed[here, LAT:] = rotated[:, head * ROPE : (head + 1) * ROPE]
            weighted.append(
                (advantage_column * cotangent[:, nope].astype(jnp.float32)).astype(jnp.bfloat16)
            )
            back_lat[here, :] = dot_nt(weighted[-1], weights[:, values]).astype(jnp.bfloat16)
        scores = dot_nt(keys[...], absorbed[both, :]) * scale + bias_pair
        exponent = jnp.exp(scores - jnp.max(scores, axis=0, keepdims=True))
        probs = exponent * (1.0 / jnp.sum(exponent, axis=0, keepdims=True))
        low = probs.astype(jnp.bfloat16)
        probs_low[:, both] = low
        grad_prob = dot_nt(keys[:, :LAT], back_lat[both, :])
        row_delta = jnp.sum(probs * grad_prob, axis=0, keepdims=True)
        score = (probs * (grad_prob - row_delta) * scale).astype(jnp.bfloat16)
        grad_score[:, both] = score
        out_lat = dot_nn(keys_t[:LAT, :], low).astype(jnp.bfloat16)
        grad_abs = dot_nn(keys_t[...], score).astype(jnp.bfloat16)
        rope_rows = grad_abs[LAT:, :].astype(jnp.float32)
        rope_rows = jnp.concatenate([rope_rows[:, :rows], rope_rows[:, rows:]], axis=0)
        d_q_rope[:, pair * 2 * ROPE : (pair + 1) * 2 * ROPE] = jnp.transpose(rope_rows).astype(
            jnp.bfloat16
        )
        for side, head in enumerate((2 * pair, 2 * pair + 1)):
            nope = slice(head * NOPE, (head + 1) * NOPE)
            values = slice(width + head * VDIM, width + (head + 1) * VDIM)
            mine = slice(side * rows, (side + 1) * rows)
            d_q_nope[:, nope] = dot_tn(grad_abs[:LAT, mine], weights[:, nope]).astype(jnp.bfloat16)
            term_keys = dot_nn(grad_abs[:LAT, mine], queries[:, nope]).astype(jnp.bfloat16)
            term_values = dot_nn(out_lat[:, mine], weighted[side]).astype(jnp.bfloat16)
            for columns, term in ((nope, term_keys), (values, term_values)):
                even, odd = core_rows(term, 0), core_rows(term, 1)
                d_weights_mine[:, columns] = jnp.where(core == 0, even, odd)
                d_weights_theirs[:, columns] = jnp.where(core == 0, odd, even)

    for block in range(reach + 1):
        here = slice(block * rows, (block + 1) * rows)
        total = dot_nn(grad_score[here, :], absorbed[...])
        total_lat = total[:, :LAT] + dot_nn(probs_low[here, :], back_lat[...])
        if block < reach:
            grad_earlier[here, :LAT] = total_lat.astype(jnp.bfloat16)
            grad_earlier[here, LAT:] = total[:, LAT:].astype(jnp.bfloat16)
        else:
            grad_own[:, :LAT] = total_lat
            grad_own[:, LAT:] = total[:, LAT:]


def layer(place, advantage, segment, queries, rotated, cotangent, key_blocks, mine, theirs):
    rows, width = queries.shape
    heads = width // NOPE
    span = len(key_blocks) * rows
    wide = LAT + ROPE
    whole = pl.BlockSpec(memory_space=pltpu.VMEM)
    return pl.pallas_call(
        layer_kernel,
        out_shape=(
            jax.ShapeDtypeStruct((rows, width), jnp.bfloat16),
            jax.ShapeDtypeStruct((rows, heads * ROPE), jnp.bfloat16),
            jax.ShapeDtypeStruct((span - rows, wide), jnp.bfloat16),
            jax.ShapeDtypeStruct((rows, wide), jnp.float32),
            jax.ShapeDtypeStruct(mine.shape, jnp.bfloat16),
            jax.ShapeDtypeStruct(theirs.shape, jnp.bfloat16),
        ),
        in_specs=[pl.BlockSpec(memory_space=pltpu.SMEM)] + [whole] * (7 + len(key_blocks)),
        out_specs=(whole,) * 6,
        scratch_shapes=[
            pltpu.VMEM((LAT, 2 * width), jnp.bfloat16),
            pltpu.VMEM((span, wide), jnp.bfloat16),
            pltpu.VMEM((wide, span), jnp.bfloat16),
            pltpu.VMEM((span, rows), jnp.float32),
            pltpu.VMEM((heads * rows, wide), jnp.bfloat16),
            pltpu.VMEM((heads * rows, LAT), jnp.bfloat16),
            pltpu.VMEM((span, heads * rows), jnp.bfloat16),
            pltpu.VMEM((span, heads * rows), jnp.bfloat16),
        ],
        compiler_params=pltpu.CompilerParams(vmem_limit_bytes=48 * 1024 * 1024),
        cost_estimate=pl.CostEstimate(
            flops=5_000_000_000, bytes_accessed=8_000_000, transcendentals=700_000
        ),
    )(place, advantage, segment, queries, rotated, cotangent, *key_blocks, mine, theirs)


def passed_along(value, steps):
    count = lax.axis_size("ctx")
    leading, last = (max(0, -steps), min(count, count - steps))
    return lax.ppermute(value, "ctx", [(source, source + steps) for source in range(leading, last)])


def on_device(q_nope, q_rope, latent, k_rope, d_out, advantage, segment, w_uk, w_uv):
    rows, width = q_nope.shape
    count = lax.axis_size("ctx")
    chips = count // 2
    reach = 4
    index = lax.axis_index("ctx")
    same_core = [[2 * chip + core for chip in range(chips)] for core in range(2)]
    swap = [(device, device ^ 1) for device in range(count)]

    up = jnp.concatenate([w_uk, w_uv], axis=1)
    mine = lax.all_to_all(
        jnp.broadcast_to(up[None], (chips,) + up.shape).reshape(chips * up.shape[0], up.shape[1]),
        "ctx",
        0,
        0,
        axis_index_groups=same_core,
        tiled=True,
    )
    theirs = lax.ppermute(mine, "ctx", swap)
    keys = jnp.concatenate([latent, k_rope], axis=1)
    blocks = [passed_along(keys, distance) for distance in range(reach, 0, -1)] + [keys]

    d_q_nope, d_q_rope, grad_earlier, grad_own, d_mine, d_theirs = layer(
        index.reshape(1),
        advantage.reshape(1, rows),
        segment.reshape(count, rows),
        q_nope,
        q_rope,
        d_out,
        blocks,
        mine,
        theirs,
    )

    total = grad_own
    for block in range(reach):
        piece = grad_earlier[block * rows : (block + 1) * rows]
        total = total + passed_along(piece, block - reach).astype(jnp.float32)
    heads_over = lax.axis_size("head")
    key_terms = lax.all_to_all(
        total.astype(jnp.bfloat16), "head", 0, 0, tiled=True
    ).reshape(heads_over, rows // heads_over, LAT + ROPE)
    d_keys = jnp.sum(key_terms.astype(jnp.float32), axis=0)

    arrived = lax.ppermute(d_theirs, "ctx", swap)
    chip_sum = (d_mine.astype(jnp.float32) + arrived.astype(jnp.float32)).astype(jnp.bfloat16)
    up_terms = lax.all_to_all(
        chip_sum, "ctx", 0, 0, axis_index_groups=same_core, tiled=True
    ).reshape(chips, LAT // count, 2 * width)
    d_up = jnp.sum(up_terms.astype(jnp.float32), axis=0)
    return (
        d_q_nope,
        d_q_rope,
        d_keys[:, :LAT],
        d_keys[:, LAT:],
        d_up[:, :width],
        d_up[:, width:],
    )


def solution(mesh):
    placed = (
        P("ctx", "head"),
        P("ctx", "head"),
        P("ctx", None),
        P("ctx", None),
        P("ctx", "head"),
        P("ctx"),
        P(),
        P("ctx", "head"),
        P("ctx", "head"),
    )
    return jax.shard_map(
        on_device,
        mesh=mesh,
        in_specs=placed,
        out_specs=(
            P("ctx", "head"),
            P("ctx", "head"),
            P(("ctx", "head"), None),
            P(("ctx", "head"), None),
            P("ctx", "head"),
            P("ctx", "head"),
        ),
        check_vma=False,
    )
```

time: 476 us -> 165 us (0.35)
  the two profiles are of different devices: /device:TPU:2 before, /device:TPU:24 now
where the time goes in v1:
time: 165 us; the launch traced here: 162 us
  waiting for transfers between devices  52.4 us (32%)
  starting transfers between devices  50.4 us (31%)
  blocking collectives  33.4 us (20%)
  Pallas kernels  12.5 us (8%)
  local copies, waits for them, and re-layouts  9.71 us (6%)
  other arithmetic  3.14 us (2%)
    all_to_all x1, blocking collectives, on_device(): lax.all_to_all(jnp.broadcast_to(up[None], (chips,) + up.shape).reshape(ch...  33.4 us
    ppermute x8, starting transfers between devices, passed_along(): lax.ppermute(value, 'ctx', [(source, source + steps) for source in range(...  23.1 us
    all_to_all x1, waiting for transfers between devices, on_device(): lax.all_to_all(chip_sum, 'ctx', 0, 0, axis_index_groups=same_core, tiled=...  22.8 us
    ppermute x8, waiting for transfers between devices, passed_along(): lax.ppermute(value, 'ctx', [(source, source + steps) for source in range(...  15.2 us
    all_to_all x1, starting transfers between devices, on_device(): lax.all_to_all(total.astype(jnp.bfloat16), 'head', 0, 0, tiled=True)  15 us
    all_to_all x1, waiting for transfers between devices, on_device(): lax.all_to_all(total.astype(jnp.bfloat16), 'head', 0, 0, tiled=True)  14.4 us
    pallas_call x1, Pallas kernels, layer(): pl.pallas_call(layer_kernel, out_shape=(jax.ShapeDtypeStruct((rows, width...  12.5 us
    all_to_all x1, starting transfers between devices, on_device(): lax.all_to_all(chip_sum, 'ctx', 0, 0, axis_index_groups=same_core, tiled=...  8.53 us
  transfers between devices with their start and end apart: 12, of which 6 were waited for; matrix products, arithmetic and copies ran while one was open for 2% of the time, Pallas kernels for 0%

profile of v1, /device:TPU:24, one launch (start us, length us, event | category | flops | bytes accessed | tf_op | source)
XLA Modules:
  0.0 162.4 jit_solution(7811222609945350243)
XLA Ops:
  0.6 0.8 pad_maximum_fusion.1
  1.4 0.1 broadcast_in_dim.2
  1.5 0.0 copy-start.12
  1.5 0.0 copy-start.11
  1.6 0.0 copy-start.9
  1.6 0.0 copy-start.10
  1.6 33.4 %all_to_all.26 = bf16[16,16,2048]{2,1,0:T(8,128)(2,1)S(1)} all-to-all(bf16[16,16,2048]{2,1,0:T(8,128)(2,1)S(1)} %broadcast_in_dim.2), channel_id=1, replica_groups={{0,32,64,96,128,160,192,224,256,288,320,352,384,416,448,480},{16,48,80,..., dimensions={0} | all-to-all | bytes 2097152 | tf_op jit(solution)/shard_map/all_to_all | solution.py:213
  35.0 1.9 %collective-permute-start.4 = (bf16[256,2048]{1,0:T(8,128)(2,1)S(1)}, bf16[256,2048]{1,0:T(8,128)(2,1)}, u32[]{:S(2)}, u32[]{:S(2)}) collective-permute-start(bf16[256,2048]{1,0:T(8,128)(2,1)S(1)} %bitcast.7), channel_id=1, source_target_pairs={{0,16},{16,0},{32,48},{48,32},{64,80},{80,64},{96,112},{112,96},{1... | collective-permute-start | bytes 3145736 | tf_op jit(solution)/shard_map/ppermute | solution.py:221
  36.9 0.0 copy-done.12
  37.0 0.1 copy.15
  37.1 0.0 copy-done.11
  37.1 2.4 %collective-permute-start.3 = (bf16[128,576]{1,0:T(8,128)(2,1)S(1)}, bf16[128,576]{1,0:T(8,128)(2,1)S(1)}, u32[]{:S(2)}, u32[]{:S(2)}) collective-permute-start(bf16[128,576]{1,0:T(8,128)(2,1)S(1)} %pad_maximum_fusion.key0), channel_id=1, source_target_pairs={{0,16},{16,32},{32,48},{48,64},{64,80},{80,96},{96,112},{112,128},... | collective-permute-start | bytes 442376 | tf_op jit(solution)/shard_map/ppermute | solution.py:200
  39.5 4.6 %collective-permute-start.2 = (bf16[128,576]{1,0:T(8,128)(2,1)S(1)}, bf16[128,576]{1,0:T(8,128)(2,1)S(1)}, u32[]{:S(2)}, u32[]{:S(2)}) collective-permute-start(bf16[128,576]{1,0:T(8,128)(2,1)S(1)} %pad_maximum_fusion.key0), channel_id=1, source_target_pairs={{0,32},{16,48},{32,64},{48,80},{64,96},{80,112},{96,128},{112,144}... | collective-permute-start | bytes 442376 | tf_op jit(solution)/shard_map/ppermute | solution.py:200
  44.2 2.6 %collective-permute-start.1 = (bf16[128,576]{1,0:T(8,128)(2,1)S(1)}, bf16[128,576]{1,0:T(8,128)(2,1)S(1)}, u32[]{:S(2)}, u32[]{:S(2)}) collective-permute-start(bf16[128,576]{1,0:T(8,128)(2,1)S(1)} %pad_maximum_fusion.key0), channel_id=1, source_target_pairs={{0,48},{16,64},{32,80},{48,96},{64,112},{80,128},{96,144},{112,160... | collective-permute-start | bytes 442376 | tf_op jit(solution)/shard_map/ppermute | solution.py:200
  46.8 4.9 %collective-permute-start = (bf16[128,576]{1,0:T(8,128)(2,1)S(1)}, bf16[128,576]{1,0:T(8,128)(2,1)S(1)}, u32[]{:S(2)}, u32[]{:S(2)}) collective-permute-start(bf16[128,576]{1,0:T(8,128)(2,1)S(1)} %pad_maximum_fusion.key0), channel_id=1, source_target_pairs={{0,64},{16,80},{32,96},{48,112},{64,128},{80,144},{96,160},{112,17... | collective-permute-start | bytes 442376 | tf_op jit(solution)/shard_map/ppermute | solution.py:200
  51.7 0.0 collective-permute-done.3.key1
  51.7 0.0 collective-permute-done.2.key2
  51.7 0.0 copy-start.2
  51.7 0.7 copy-done.2
  52.4 0.0 collective-permute-done.1.key3
  52.4 0.0 copy-start.4
  52.4 0.7 copy-done.4
  53.0 3.9 %collective-permute-done.key4 = bf16[128,576]{1,0:T(8,128)(2,1)S(1)} collective-permute-done((bf16[128,576]{1,0:T(8,128)(2,1)S(1)}, bf16[128,576]{1,0:T(8,128)(2,1)S(1)}, u32[]{:S(2)}, u32[]{:S(2)}) %collective-permute-start) | collective-permute-done | bytes 147488 | tf_op jit(solution)/shard_map/ppermute | solution.py:200
  56.9 0.0 copy-start.6
  56.9 0.7 copy-done.6
  57.6 0.0 collective-permute-done.4.weights_theirs
  57.6 0.0 copy-done.9
  57.6 0.0 copy-done.10
  57.6 0.0 copy-start
  57.6 0.9 copy-done
  58.5 0.0 copy-start.1
  58.5 0.9 copy-done.1
  59.5 0.0 copy-start.3
  59.5 0.9 copy-done.3
  60.4 0.0 copy-start.5
  60.4 0.9 copy-done.5
  61.3 0.0 copy-start.7
  61.3 0.9 copy-done.7
  62.2 0.0 copy-start.8
  62.2 0.9 copy-done.8
  63.1 12.5 %shard_map.136 = (bf16[128,1024]{1,0:T(8,128)(2,1)}, bf16[128,512]{1,0:T(8,128)(2,1)}, bf16[512,576]{1,0:T(8,128)(2,1)S(1)}, f32[128,576]{1,0:T(8,128)S(1)}, bf1...) custom-call(s32[1]{0:T(128)} %bitcast.place, f32[1,128]{1,0:T(1,128)S(1)} %bitcast.10, s32[32,128]{1,0:T(8,128)S(1)} %bitcast.9, ...), custom_call_target="tpu_custom_call" | custom-call | flops 5000000000 | bytes 8000000 | tf_op jit(solution)/shard_map/pallas_call | solution.py:168
  75.6 1.9 %collective-permute-start.9 = (bf16[256,2048]{1,0:T(8,128)(2,1)S(1)}, bf16[256,2048]{1,0:T(8,128)(2,1)S(1)}, u32[]{:S(2)}, u32[]{:S(2)}) collective-permute-start(bf16[256,2048]{1,0:T(8,128)(2,1)S(1)} %get-tuple-element.17), channel_id=1, source_target_pairs={{0,16},{16,0},{32,48},{48,32},{64,80},{80,64},{96,112},{112,96},{1... | collective-permute-start | bytes 3145736 | tf_op jit(solution)/shard_map/ppermute | solution.py:247
  77.5 0.1 fusion.1
  77.6 2.6 %collective-permute-start.5 = (bf16[128,576]{1,0:T(8,128)(2,1)S(1)}, bf16[128,576]{1,0:T(8,128)(2,1)S(1)}, u32[]{:S(2)}, u32[]{:S(2)}) collective-permute-start(bf16[128,576]{1,0:T(8,128)(2,1)S(1)} %get-tuple-element.18), channel_id=1, source_target_pairs={{64,0},{80,16},{96,32},{112,48},{128,64},{144,80},{160,96},{176,11... | collective-permute-start | bytes 442376 | tf_op jit(solution)/shard_map/ppermute | solution.py:200
  80.2 1.9 %collective-permute-start.8 = (bf16[128,576]{1,0:T(8,128)(2,1)S(1)}, bf16[128,576]{1,0:T(8,128)(2,1)S(1)}, u32[]{:S(2)}, u32[]{:S(2)}) collective-permute-start(bf16[128,576]{1,0:T(8,128)(2,1)S(1)} %get-tuple-element.19), channel_id=1, source_target_pairs={{16,0},{32,16},{48,32},{64,48},{80,64},{96,80},{112,96},{128,112},... | collective-permute-start | bytes 442376 | tf_op jit(solution)/shard_map/ppermute | solution.py:200
  82.1 2.1 %collective-permute-start.7 = (bf16[128,576]{1,0:T(8,128)(2,1)S(1)}, bf16[128,576]{1,0:T(8,128)(2,1)S(1)}, u32[]{:S(2)}, u32[]{:S(2)}) collective-permute-start(bf16[128,576]{1,0:T(8,128)(2,1)S(1)} %get-tuple-element.20), channel_id=1, source_target_pairs={{32,0},{48,16},{64,32},{80,48},{96,64},{112,80},{128,96},{144,112}... | collective-permute-start | bytes 442376 | tf_op jit(solution)/shard_map/ppermute | solution.py:200
  84.2 1.9 %collective-permute-start.6 = (bf16[128,576]{1,0:T(8,128)(2,1)S(1)}, bf16[128,576]{1,0:T(8,128)(2,1)S(1)}, u32[]{:S(2)}, u32[]{:S(2)}) collective-permute-start(bf16[128,576]{1,0:T(8,128)(2,1)S(1)} %get-tuple-element.21), channel_id=1, source_target_pairs={{48,0},{64,16},{80,32},{96,48},{112,64},{128,80},{144,96},{160,112... | collective-permute-start | bytes 442376 | tf_op jit(solution)/shard_map/ppermute | solution.py:200
  86.2 3.0 %collective-permute-done.5 = bf16[128,576]{1,0:T(8,128)(2,1)S(1)} collective-permute-done((bf16[128,576]{1,0:T(8,128)(2,1)S(1)}, bf16[128,576]{1,0:T(8,128)(2,1)S(1)}, u32[]{:S(2)}, u32[]{:S(2)}) %collective-permute-start.5) | collective-permute-done | bytes 147488 | tf_op jit(solution)/shard_map/ppermute | solution.py:200
  89.2 0.0 collective-permute-done.8
  89.2 7.0 %collective-permute-done.7 = bf16[128,576]{1,0:T(8,128)(2,1)S(1)} collective-permute-done((bf16[128,576]{1,0:T(8,128)(2,1)S(1)}, bf16[128,576]{1,0:T(8,128)(2,1)S(1)}, u32[]{:S(2)}, u32[]{:S(2)}) %collective-permute-start.7) | collective-permute-done | bytes 147488 | tf_op jit(solution)/shard_map/ppermute | solution.py:200
  96.2 1.3 collective-permute-done.6
  97.5 0.8 fusion
  98.2 15.0 %all-to-all-start.1 = ((bf16[16,8,576]{2,1,0:T(8,128)(2,1)}), bf16[16,8,576]{2,1,0:T(8,128)(2,1)S(1)}, u32[]{:S(2)}, u32[]{:S(2)}) async-start(bf16[16,8,576]{2,1,0:T(8,128)(2,1)} %fusion), calls=%async_computation.1 | async-start | bytes 327680 | tf_op jit(solution)/shard_map/all_to_all | solution.py:242
  113.2 0.0 collective-permute-done.9
  113.2 1.4 add_convert_fusion
  114.6 14.4 %all-to-all-done.1 = bf16[16,8,576]{2,1,0:T(8,128)(2,1)S(1)} async-done(((bf16[16,8,576]{2,1,0:T(8,128)(2,1)}), bf16[16,8,576]{2,1,0:T(8,128)(2,1)S(1)}, u32[]{:S(2)}, u32[]{:S(2)}) %all-to-all-start.1) | async-done | bytes 147488 | tf_op jit(solution)/shard_map/all_to_all | solution.py:242
  129.0 8.5 %all-to-all-start.2 = ((bf16[16,16,2048]{2,1,0:T(8,128)(2,1)}), bf16[16,16,2048]{2,1,0:T(8,128)(2,1)S(1)}, u32[]{:S(2)}, u32[]{:S(2)}) async-start(bf16[16,16,2048]{2,1,0:T(8,128)(2,1)} %bitcast.5), calls=%async_computation.2 | async-start | bytes 2097152 | tf_op jit(solution)/shard_map/all_to_all | solution.py:249
  137.6 0.6 slice.33
  138.2 0.6 slice.32
  138.8 22.8 %all-to-all-done.2 = bf16[16,16,2048]{2,1,0:T(8,128)(2,1)S(1)} async-done(((bf16[16,16,2048]{2,1,0:T(8,128)(2,1)}), bf16[16,16,2048]{2,1,0:T(8,128)(2,1)S(1)}, u32[]{:S(2)}, u32[]{:S(2)}) %all-to-all-start.2) | async-done | bytes 1048608 | tf_op jit(solution)/shard_map/all_to_all | solution.py:249
  161.6 0.1 convert_reduce_fusion
  161.7 0.7 fusion.2
  (2 shorter events, 0.0 us)
Async XLA Ops:
  1.5 35.4 %copy-start.12 = (bf16[128,64]{0,1:T(8,128)(2,1)S(1)}, bf16[128,64]{0,1:T(8,128)(2,1)}, u32[]{:S(2)}) copy-start(bf16[128,64]{0,1:T(8,128)(2,1)} %param.12) | copy-start | bytes 49156
  1.5 35.5 %copy-start.11 = (bf16[128,512]{1,0:T(8,128)(2,1)S(1)}, bf16[128,512]{1,0:T(8,128)(2,1)}, u32[]{:S(2)}) copy-start(bf16[128,512]{1,0:T(8,128)(2,1)} %param.11) | copy-start | bytes 393220
  1.6 56.0 %copy-start.9 = (s32[4096]{0:T(1024)S(1)}, s32[4096]{0:T(1024)}, u32[]{:S(2)}) copy-start(s32[4096]{0:T(1024)} %param.15) | copy-start | bytes 49156
  1.6 56.0 %copy-start.10 = (f32[128]{0:T(128)S(1)}, f32[128]{0:T(128)}, u32[]{:S(2)}) copy-start(f32[128]{0:T(128)} %param.14) | copy-start | bytes 1540
  35.0 22.6 %collective-permute-start.4 = (bf16[256,2048]{1,0:T(8,128)(2,1)S(1)}, bf16[256,2048]{1,0:T(8,128)(2,1)}, u32[]{:S(2)}, u32[]{:S(2)}) collective-permute-start(bf16[256,2048]{1,0:T(8,128)(2,1)S(1)} %bitcast.7), channel_id=1, source_target_pairs={{0,16},{16,0},{32,48},{48,32},{64,80},{80,64},{96,112},{112,96},{1... | collective-permute-start | bytes 3145736 | tf_op jit(solution)/shard_map/ppermute | solution.py:221
  37.1 14.6 %collective-permute-start.3 = (bf16[128,576]{1,0:T(8,128)(2,1)S(1)}, bf16[128,576]{1,0:T(8,128)(2,1)S(1)}, u32[]{:S(2)}, u32[]{:S(2)}) collective-permute-start(bf16[128,576]{1,0:T(8,128)(2,1)S(1)} %pad_maximum_fusion.key0), channel_id=1, source_target_pairs={{0,16},{16,32},{32,48},{48,64},{64,80},{80,96},{96,112},{112,128},... | collective-permute-start | bytes 442376 | tf_op jit(solution)/shard_map/ppermute | solution.py:200
  39.5 12.2 %collective-permute-start.2 = (bf16[128,576]{1,0:T(8,128)(2,1)S(1)}, bf16[128,576]{1,0:T(8,128)(2,1)S(1)}, u32[]{:S(2)}, u32[]{:S(2)}) collective-permute-start(bf16[128,576]{1,0:T(8,128)(2,1)S(1)} %pad_maximum_fusion.key0), channel_id=1, source_target_pairs={{0,32},{16,48},{32,64},{48,80},{64,96},{80,112},{96,128},{112,144}... | collective-permute-start | bytes 442376 | tf_op jit(solution)/shard_map/ppermute | solution.py:200
  44.2 8.2 %collective-permute-start.1 = (bf16[128,576]{1,0:T(8,128)(2,1)S(1)}, bf16[128,576]{1,0:T(8,128)(2,1)S(1)}, u32[]{:S(2)}, u32[]{:S(2)}) collective-permute-start(bf16[128,576]{1,0:T(8,128)(2,1)S(1)} %pad_maximum_fusion.key0), channel_id=1, source_target_pairs={{0,48},{16,64},{32,80},{48,96},{64,112},{80,128},{96,144},{112,160... | collective-permute-start | bytes 442376 | tf_op jit(solution)/shard_map/ppermute | solution.py:200
  46.8 10.1 %collective-permute-start = (bf16[128,576]{1,0:T(8,128)(2,1)S(1)}, bf16[128,576]{1,0:T(8,128)(2,1)S(1)}, u32[]{:S(2)}, u32[]{:S(2)}) collective-permute-start(bf16[128,576]{1,0:T(8,128)(2,1)S(1)} %pad_maximum_fusion.key0), channel_id=1, source_target_pairs={{0,64},{16,80},{32,96},{48,112},{64,128},{80,144},{96,160},{112,17... | collective-permute-start | bytes 442376 | tf_op jit(solution)/shard_map/ppermute | solution.py:200
  51.7 0.7 copy-start.2
  52.4 0.7 copy-start.4
  56.9 0.7 copy-start.6
  57.6 1.0 copy-start
  58.5 0.9 copy-start.1
  59.5 0.9 copy-start.3
  60.4 0.9 copy-start.5
  61.3 0.9 copy-start.7
  62.2 0.9 copy-start.8
  75.6 37.6 %collective-permute-start.9 = (bf16[256,2048]{1,0:T(8,128)(2,1)S(1)}, bf16[256,2048]{1,0:T(8,128)(2,1)S(1)}, u32[]{:S(2)}, u32[]{:S(2)}) collective-permute-start(bf16[256,2048]{1,0:T(8,128)(2,1)S(1)} %get-tuple-element.17), channel_id=1, source_target_pairs={{0,16},{16,0},{32,48},{48,32},{64,80},{80,64},{96,112},{112,96},{1... | collective-permute-start | bytes 3145736 | tf_op jit(solution)/shard_map/ppermute | solution.py:247
  77.6 11.6 %collective-permute-start.5 = (bf16[128,576]{1,0:T(8,128)(2,1)S(1)}, bf16[128,576]{1,0:T(8,128)(2,1)S(1)}, u32[]{:S(2)}, u32[]{:S(2)}) collective-permute-start(bf16[128,576]{1,0:T(8,128)(2,1)S(1)} %get-tuple-element.18), channel_id=1, source_target_pairs={{64,0},{80,16},{96,32},{112,48},{128,64},{144,80},{160,96},{176,11... | collective-permute-start | bytes 442376 | tf_op jit(solution)/shard_map/ppermute | solution.py:200
  80.2 9.0 %collective-permute-start.8 = (bf16[128,576]{1,0:T(8,128)(2,1)S(1)}, bf16[128,576]{1,0:T(8,128)(2,1)S(1)}, u32[]{:S(2)}, u32[]{:S(2)}) collective-permute-start(bf16[128,576]{1,0:T(8,128)(2,1)S(1)} %get-tuple-element.19), channel_id=1, source_target_pairs={{16,0},{32,16},{48,32},{64,48},{80,64},{96,80},{112,96},{128,112},... | collective-permute-start | bytes 442376 | tf_op jit(solution)/shard_map/ppermute | solution.py:200
  82.1 14.1 %collective-permute-start.7 = (bf16[128,576]{1,0:T(8,128)(2,1)S(1)}, bf16[128,576]{1,0:T(8,128)(2,1)S(1)}, u32[]{:S(2)}, u32[]{:S(2)}) collective-permute-start(bf16[128,576]{1,0:T(8,128)(2,1)S(1)} %get-tuple-element.20), channel_id=1, source_target_pairs={{32,0},{48,16},{64,32},{80,48},{96,64},{112,80},{128,96},{144,112}... | collective-permute-start | bytes 442376 | tf_op jit(solution)/shard_map/ppermute | solution.py:200
  84.2 13.2 %collective-permute-start.6 = (bf16[128,576]{1,0:T(8,128)(2,1)S(1)}, bf16[128,576]{1,0:T(8,128)(2,1)S(1)}, u32[]{:S(2)}, u32[]{:S(2)}) collective-permute-start(bf16[128,576]{1,0:T(8,128)(2,1)S(1)} %get-tuple-element.21), channel_id=1, source_target_pairs={{48,0},{64,16},{80,32},{96,48},{112,64},{128,80},{144,96},{160,112... | collective-permute-start | bytes 442376 | tf_op jit(solution)/shard_map/ppermute | solution.py:200
  98.2 30.8 %all-to-all-start.1 = ((bf16[16,8,576]{2,1,0:T(8,128)(2,1)}), bf16[16,8,576]{2,1,0:T(8,128)(2,1)S(1)}, u32[]{:S(2)}, u32[]{:S(2)}) async-start(bf16[16,8,576]{2,1,0:T(8,128)(2,1)} %fusion), calls=%async_computation.1 | async-start | bytes 327680 | tf_op jit(solution)/shard_map/all_to_all | solution.py:242
  129.0 32.5 %all-to-all-start.2 = ((bf16[16,16,2048]{2,1,0:T(8,128)(2,1)}), bf16[16,16,2048]{2,1,0:T(8,128)(2,1)S(1)}, u32[]{:S(2)}, u32[]{:S(2)}) async-start(bf16[16,16,2048]{2,1,0:T(8,128)(2,1)} %bitcast.5), calls=%async_computation.2 | async-start | bytes 2097152 | tf_op jit(solution)/shard_map/all_to_all | solution.py:249

commit v2 on v1

v2 whole, which is shorter than its diff:
```python
import functools
import math

import jax
import jax.numpy as jnp
from jax import lax
from jax.experimental import pallas as pl
from jax.experimental.pallas import tpu as pltpu
from jax.sharding import PartitionSpec as P

LAT = 512
ROPE = 64
NOPE = 128
VDIM = 128
FAR = -1e30


def dot_nt(left, right):
    return lax.dot_general(
        left, right, (((1,), (1,)), ((), ())), preferred_element_type=jnp.float32
    )


def dot_nn(left, right):
    return lax.dot_general(
        left, right, (((1,), (0,)), ((), ())), preferred_element_type=jnp.float32
    )


def dot_tn(left, right):
    return lax.dot_general(
        left, right, (((0,), (0,)), ((), ())), preferred_element_type=jnp.float32
    )


def column_of(row, count):
    return jnp.transpose(jnp.broadcast_to(row, (count, count)))


def layer_kernel(
    place,
    advantage,
    segment,
    queries_in,
    rotated_in,
    cotangent_in,
    keys_near,
    keys_far,
    weights_mine,
    weights_theirs,
    d_q_nope,
    d_q_rope,
    grad_kept,
    grad_given,
    grad_own,
    d_weights_mine,
    d_weights_theirs,
    queries,
    rotated,
    cotangent,
    weights,
    key_blocks,
    keys,
    keys_t,
    bias,
    absorbed,
    back_lat,
    probs_low,
    grad_score,
    d_weights,
    in_sems,
    out_sems,
):
    rows, width = queries.shape
    heads = width // NOPE
    span = keys.shape[0]
    reach = span // rows - 1
    ring = weights.shape[1]
    scale = 1.0 / math.sqrt(NOPE + ROPE)
    index = place[0]
    core = lax.rem(index, 2)

    loads = []

    def load(source, target):
        copy = pltpu.make_async_copy(source, target, in_sems.at[len(loads)])
        copy.start()
        loads.append(copy)

    load(keys_near, key_blocks.at[:, core])
    load(keys_far, key_blocks.at[:, 1 - core])
    key_loads = len(loads)
    load(queries_in, queries)
    load(cotangent_in, cotangent)
    load(rotated_in, rotated)
    for step in range(ring):
        load(weights_mine.at[step], weights.at[:, step, core])
        load(weights_theirs.at[step], weights.at[:, step, 1 - core])

    query_segment = segment[pl.ds(index, 1), :]
    query_at = lax.broadcasted_iota(jnp.int32, (rows, rows), 1)
    key_at = lax.broadcasted_iota(jnp.int32, (rows, rows), 0)
    for block in range(reach + 1):
        owner = index - (reach - block)
        key_row = segment[pl.ds(jnp.maximum(owner, 0), 1), :]
        key_segment = column_of(key_row, rows)
        allowed = (key_segment == query_segment) & (owner >= 0)
        if block == reach:
            allowed = allowed & (key_at <= query_at)
        bias[block * rows : (block + 1) * rows, :] = jnp.where(allowed, 0.0, FAR)
    advantage_column = column_of(advantage[...], rows)
    bias_pair = jnp.concatenate([bias[...], bias[...]], axis=1)

    for copy in loads[:key_loads]:
        copy.wait()
    for block in range(reach + 1):
        here = slice(block * rows, (block + 1) * rows)
        piece = key_blocks[(block + core) // 2, (block + core) % 2]
        keys[here, :] = piece
        keys_t[:, here] = jnp.transpose(piece)
    for copy in loads[key_loads:]:
        copy.wait()

    stores = []

    def store(source, target):
        copy = pltpu.make_async_copy(source, target, out_sems.at[len(stores)])
        copy.start()
        stores.append(copy)

    for pair in range(heads // 2):
        both = slice(pair * 2 * rows, (pair + 1) * 2 * rows)
        weighted = []
        for head in (2 * pair, 2 * pair + 1):
            here = slice(head * rows, (head + 1) * rows)
            nope = slice(head * NOPE, (head + 1) * NOPE)
            values = slice(width + head * VDIM, width + (head + 1) * VDIM)
            up_keys = weights[:, :, :, :, nope].reshape(LAT, NOPE)
            up_values = weights[:, :, :, :, values].reshape(LAT, VDIM)
            absorbed[here, :LAT] = dot_nt(queries[:, nope], up_keys).astype(jnp.bfloat16)
            absorbed[here, LAT:] = rotated[:, head * ROPE : (head + 1) * ROPE]
            weighted.append(
                (advantage_column * cotangent[:, nope].astype(jnp.float32)).astype(jnp.bfloat16)
            )
            back_lat[here, :] = dot_nt(weighted[-1], up_values).astype(jnp.bfloat16)
        scores = dot_nt(keys[...], absorbed[both, :]) * scale + bias_pair
        exponent = jnp.exp(scores - jnp.max(scores, axis=0, keepdims=True))
        probs = exponent * (1.0 / jnp.sum(exponent, axis=0, keepdims=True))
        low = probs.astype(jnp.bfloat16)
        probs_low[:, both] = low
        grad_prob = dot_nt(keys[:, :LAT], back_lat[both, :])
        row_delta = jnp.sum(probs * grad_prob, axis=0, keepdims=True)
        score = (probs * (grad_prob - row_delta) * scale).astype(jnp.bfloat16)
        grad_score[:, both] = score
        out_lat = dot_nn(keys_t[:LAT, :], low).astype(jnp.bfloat16)
        grad_abs = dot_nn(keys_t[...], score).astype(jnp.bfloat16)
        rope_rows = grad_abs[LAT:, :].astype(jnp.float32)
        rope_rows = jnp.concatenate([rope_rows[:, :rows], rope_rows[:, rows:]], axis=0)
        d_q_rope[:, pair * 2 * ROPE : (pair + 1) * 2 * ROPE] = jnp.transpose(rope_rows).astype(
            jnp.bfloat16
        )
        for side, head in enumerate((2 * pair, 2 * pair + 1)):
            nope = slice(head * NOPE, (head + 1) * NOPE)
            values = slice(width + head * VDIM, width + (head + 1) * VDIM)
            mine = slice(side * rows, (side + 1) * rows)
            up_keys = weights[:, :, :, :, nope].reshape(LAT, NOPE)
            d_q_nope[:, nope] = dot_tn(grad_abs[:LAT, mine], up_keys).astype(jnp.bfloat16)
            term_keys = dot_nn(grad_abs[:LAT, mine], queries[:, nope]).astype(jnp.bfloat16)
            term_values = dot_nn(out_lat[:, mine], weighted[side]).astype(jnp.bfloat16)
            shape = weights.shape[:4] + (NOPE,)
            d_weights[:, :, :, :, nope] = term_keys.reshape(shape)
            d_weights[:, :, :, :, values] = term_values.reshape(shape)
        if pair % 2 == 1:
            half = width // 2
            for start in (pair // 2 * half, width + pair // 2 * half):
                columns = pl.ds(start, half)
                for step in range(ring):
                    store(
                        d_weights.at[:, step, core, :, columns],
                        d_weights_mine.at[step, :, :, columns],
                    )
                    store(
                        d_weights.at[:, step, 1 - core, :, columns],
                        d_weights_theirs.at[step, :, :, columns],
                    )

    outs = (grad_kept.at[0], grad_given.at[0], grad_kept.at[1], grad_given.at[1], grad_own)
    for block, out in enumerate(outs):
        here = slice(block * rows, (block + 1) * rows)
        total = dot_nn(grad_score[here, :], absorbed[...])
        total_lat = total[:, :LAT] + dot_nn(probs_low[here, :], back_lat[...])
        out[:, :LAT] = total_lat.astype(out.dtype)
        out[:, LAT:] = total[:, LAT:].astype(out.dtype)
    for copy in stores:
        copy.wait()


def layer(place, advantage, segment, queries, rotated, cotangent, near, far, mine, theirs):
    rows, width = queries.shape
    heads = width // NOPE
    span = 5 * rows
    wide = LAT + ROPE
    whole = pl.BlockSpec(memory_space=pltpu.VMEM)
    apart = pl.BlockSpec(memory_space=pl.ANY)
    ring, steps = mine.shape[:2]
    parts = (steps, ring, 2, mine.shape[2], 2 * width)
    return pl.pallas_call(
        layer_kernel,
        out_shape=(
            jax.ShapeDtypeStruct((rows, width), jnp.bfloat16),
            jax.ShapeDtypeStruct((rows, heads * ROPE), jnp.bfloat16),
            jax.ShapeDtypeStruct((2, rows, wide), jnp.bfloat16),
            jax.ShapeDtypeStruct((2, rows, wide), jnp.bfloat16),
            jax.ShapeDtypeStruct((rows, wide), jnp.float32),
            jax.ShapeDtypeStruct(mine.shape, jnp.bfloat16),
            jax.ShapeDtypeStruct(theirs.shape, jnp.bfloat16),
        ),
        in_specs=[pl.BlockSpec(memory_space=pltpu.SMEM), whole, whole]
        + [apart] * 7,
        out_specs=(whole,) * 5 + (apart, apart),
        scratch_shapes=[
            pltpu.VMEM((rows, width), jnp.bfloat16),
            pltpu.VMEM((rows, heads * ROPE), jnp.bfloat16),
            pltpu.VMEM((rows, width), jnp.bfloat16),
            pltpu.VMEM(parts, jnp.bfloat16),
            pltpu.VMEM((3, 2, rows, wide), jnp.bfloat16),
            pltpu.VMEM((span, wide), jnp.bfloat16),
            pltpu.VMEM((wide, span), jnp.bfloat16),
            pltpu.VMEM((span, rows), jnp.float32),
            pltpu.VMEM((heads * rows, wide), jnp.bfloat16),
            pltpu.VMEM((heads * rows, LAT), jnp.bfloat16),
            pltpu.VMEM((span, heads * rows), jnp.bfloat16),
            pltpu.VMEM((span, heads * rows), jnp.bfloat16),
            pltpu.VMEM(parts, jnp.bfloat16),
            pltpu.SemaphoreType.DMA((5 + 2 * ring,)),
            pltpu.SemaphoreType.DMA((8 * ring,)),
        ],
        compiler_params=pltpu.CompilerParams(vmem_limit_bytes=56 * 1024 * 1024),
        cost_estimate=pl.CostEstimate(
            flops=5_000_000_000, bytes_accessed=8_000_000, transcendentals=700_000
        ),
    )(place, advantage, segment, queries, rotated, cotangent, near, far, mine, theirs)


def sum_kernel(shares, left, right):
    total = jnp.sum(shares[...].astype(jnp.float32), axis=0)
    left[...] = total[:, : left.shape[1]]
    right[...] = total[:, left.shape[1] :]


def summed(shares, cut):
    rows, width = shares.shape[1:]
    whole = pl.BlockSpec(memory_space=pltpu.VMEM)
    return pl.pallas_call(
        sum_kernel,
        out_shape=(
            jax.ShapeDtypeStruct((rows, cut), jnp.float32),
            jax.ShapeDtypeStruct((rows, width - cut), jnp.float32),
        ),
        in_specs=[whole],
        out_specs=(whole, whole),
        compiler_params=pltpu.CompilerParams(vmem_limit_bytes=8 * 1024 * 1024),
        cost_estimate=pl.CostEstimate(flops=1_000_000, bytes_accessed=500_000, transcendentals=0),
    )(shares)


def to_all(value, groups):
    spread = jnp.broadcast_to(value[None], (len(groups[0]),) + value.shape)
    return lax.all_to_all(spread, "ctx", 0, 0, axis_index_groups=groups, tiled=True)


def on_device(q_nope, q_rope, latent, k_rope, d_out, advantage, segment, w_uk, w_uv):
    rows, width = q_nope.shape
    count = lax.axis_size("ctx")
    ring = 4
    steps = count // (2 * ring)
    index = lax.axis_index("ctx")
    core = lax.rem(index, 2)
    place = index.reshape(1)

    def device(step, place, core):
        return (step * ring + place) * 2 + core

    along_y = [
        [device(step, place, core) for place in range(ring)]
        for step in range(steps)
        for core in range(2)
    ]
    along_z = [
        [device(step, place, core) for step in range(steps)]
        for place in range(ring)
        for core in range(2)
    ]

    def swapped(value):
        return lax.ppermute(value, "ctx", [(source, source ^ 1) for source in range(count)])

    def to_chip(value, chips):
        pairs = [(source, source + 2 * chips) for source in range(count)]
        return lax.ppermute(value, "ctx", [pair for pair in pairs if 0 <= pair[1] < count])

    up = jnp.concatenate([w_uk, w_uv], axis=1)
    column = to_all(up, along_z)
    keys = jnp.concatenate([latent, k_rope], axis=1)
    near = jnp.stack([to_chip(keys, 2), to_chip(keys, 1), keys])
    column, near = lax.optimization_barrier((column, near))
    mine = to_all(column, along_y)
    far = swapped(near)
    mine, near, far = lax.optimization_barrier((mine, near, far))
    theirs = swapped(mine)

    d_q_nope, d_q_rope, kept, given, own, d_mine, d_theirs = layer(
        place,
        advantage.reshape(1, rows),
        segment.reshape(count, rows),
        q_nope,
        q_rope,
        d_out,
        near,
        far,
        mine,
        theirs,
    )

    got = swapped(given).astype(jnp.float32)
    arrived = swapped(d_theirs)
    chip_sum = (d_mine.astype(jnp.float32) + arrived.astype(jnp.float32)).astype(jnp.bfloat16)
    far_sum = kept[0].astype(jnp.float32) + jnp.where(core == 1, got[0], 0.0)
    near_sum = kept[1].astype(jnp.float32) + jnp.where(core == 1, got[1], got[0])
    own_sum = own + jnp.where(core == 1, 0.0, got[1])
    far_sum = far_sum.astype(jnp.bfloat16)
    chip_sum, far_sum = lax.optimization_barrier((chip_sum, far_sum))
    shares = lax.all_to_all(chip_sum, "ctx", 0, 0, axis_index_groups=along_y, tiled=True)
    near_sum = (near_sum + to_chip(far_sum, -1).astype(jnp.float32)).astype(jnp.bfloat16)
    shares, near_sum = lax.optimization_barrier((shares, near_sum))
    d_column = jnp.sum(shares.astype(jnp.float32), axis=0).astype(jnp.bfloat16)
    d_shares = lax.all_to_all(d_column, "ctx", 0, 0, axis_index_groups=along_z, tiled=True)
    total = (own_sum + to_chip(near_sum, -1).astype(jnp.float32)).astype(jnp.bfloat16)
    d_shares, total = lax.optimization_barrier((d_shares, total))
    d_uk, d_uv = summed(d_shares, width)
    heads_over = lax.axis_size("head")
    key_terms = lax.all_to_all(total, "head", 0, 0, tiled=True)
    key_terms = key_terms.reshape(heads_over, rows // heads_over, LAT + ROPE)
    d_latent, d_k_rope = summed(key_terms, LAT)
    return (d_q_nope, d_q_rope, d_latent, d_k_rope, d_uk, d_uv)


def solution(mesh):
    placed = (
        P("ctx", "head"),
        P("ctx", "head"),
        P("ctx", None),
        P("ctx", None),
        P("ctx", "head"),
        P("ctx"),
        P(),
        P("ctx", "head"),
        P("ctx", "head"),
    )
    return jax.shard_map(
        on_device,
        mesh=mesh,
        in_specs=placed,
        out_specs=(
            P("ctx", "head"),
            P("ctx", "head"),
            P(("ctx", "head"), None),
            P(("ctx", "head"), None),
            P("ctx", "head"),
            P("ctx", "head"),
        ),
        check_vma=False,
    )
```

time: 165 us -> 147 us (0.89); the launches traced: 162 us -> 146 us
  blocking collectives: 33.4 us -> 0 us
  starting transfers between devices: 50.4 us -> 62.9 us
  local copies, waits for them, and re-layouts: 9.71 us -> 3.65 us
  waiting for transfers between devices: 52.4 us -> 57.2 us
  Pallas kernels: 12.5 us -> 16.5 us
  other arithmetic: 3.14 us -> 5.04 us
    all_to_all x1 -> x0, blocking collectives: 33.4 us -> none  [on_device(): lax.all_to_all(jnp.broadcast_to(up[None], (chips,) + up.shape).reshape(ch...]
    ppermute x10 -> x8, waiting for transfers between devices: 15.2 us -> 32.6 us  [the longest x4 26.7 us: to_chip(): lax.ppermute(value, 'ctx', [pair for pair in pairs if 0 <= pair[1] < count])]
    all_to_all x2 -> x5, starting transfers between devices: 23.5 us -> 39.1 us  [the longest x1 15 us: on_device(): key_terms = lax.all_to_all(total, 'head', 0, 0, tiled=True)]
    all_to_all x2 -> x5, waiting for transfers between devices: 37.2 us -> 24.7 us  [the longest x1 16.7 us: on_device(): key_terms = lax.all_to_all(total, 'head', 0, 0, tiled=True)]
    unnamed x27 -> x17, local copies, waits for them, and re-layouts: 7.68 us -> 1.79 us
    ppermute x10 -> x8, starting transfers between devices: 26.9 us -> 23.8 us  [the longest x4 15.5 us: to_chip(): lax.ppermute(value, 'ctx', [pair for pair in pairs if 0 <= pair[1] < count])]
    pallas_call x1, Pallas kernels: 12.5 us -> 15.2 us  [layer(): pl.pallas_call(layer_kernel, out_shape=(jax.ShapeDtypeStruct((rows, width...]
    slice x4 -> x0, local copies, waits for them, and re-layouts: 1.92 us -> none  [the longest x1 0.66 us: on_device(): d_up[:, width:]]
  transfers between devices with their start and end apart: 12 -> 13, of which waited for: 6 -> 10; matrix products, arithmetic and copies ran while one was open for 2% -> 2% of each run, Pallas kernels for 0% -> 0%
where the time goes in v2:
time: 147 us; the launch traced here: 146 us
  starting transfers between devices  62.9 us (43%)
  waiting for transfers between devices  57.2 us (39%)
  Pallas kernels  16.5 us (11%)
  other arithmetic  5.04 us (3%)
  local copies, waits for them, and re-layouts  3.65 us (2%)
    ppermute x4, waiting for transfers between devices, to_chip(): lax.ppermute(value, 'ctx', [pair for pair in pairs if 0 <= pair[1] < count])  26.7 us
    all_to_all x1, waiting for transfers between devices, on_device(): key_terms = lax.all_to_all(total, 'head', 0, 0, tiled=True)  16.7 us
    ppermute x4, starting transfers between devices, to_chip(): lax.ppermute(value, 'ctx', [pair for pair in pairs if 0 <= pair[1] < count])  15.5 us
    pallas_call x1, Pallas kernels, layer(): pl.pallas_call(layer_kernel, out_shape=(jax.ShapeDtypeStruct((rows, width...  15.2 us
    all_to_all x1, starting transfers between devices, on_device(): key_terms = lax.all_to_all(total, 'head', 0, 0, tiled=True)  15 us
    all_to_all x2, starting transfers between devices, to_all(): lax.all_to_all(spread, 'ctx', 0, 0, axis_index_groups=groups, tiled=True)  11.4 us
    ppermute x4, starting transfers between devices, swapped(): lax.ppermute(value, 'ctx', [(source, source ^ 1) for source in range(coun...  8.28 us
    all_to_all x1, starting transfers between devices, on_device(): lax.all_to_all(d_column, 'ctx', 0, 0, axis_index_groups=along_z, tiled=True)  7.13 us
  transfers between devices with their start and end apart: 13, of which 10 were waited for; matrix products, arithmetic and copies ran while one was open for 2% of the time, Pallas kernels for 0%

profile of v2, /device:TPU:24, one launch (start us, length us, event | category | flops | bytes accessed | tf_op | source)
XLA Modules:
  0.0 146.1 jit_solution(1029144153480740266)
XLA Ops:
  0.6 0.0 copy-start.5
  0.6 0.8 pad_maximum_fusion.2
  1.5 0.7 broadcast_in_dim.8
  2.2 5.9 %all-to-all-start = ((bf16[4,16,2048]{2,1,0:T(8,128)(2,1)}), bf16[4,16,2048]{2,1,0:T(8,128)(2,1)S(1)}, u32[]{:S(2)}, u32[]{:S(2)}) async-start(bf16[4,16,2048]{2,1,0:T(8,128)(2,1)} %broadcast_in_dim.8), calls=%async_computation | async-start | bytes 524288 | tf_op jit(solution)/shard_map/all_to_all | solution.py:269
  8.1 0.8 copy.15
  8.9 0.0 copy-done.5
  8.9 4.6 %collective-permute-start = (bf16[128,576]{1,0:T(8,128)(2,1)S(1)}, bf16[128,576]{1,0:T(8,128)(2,1)S(1)}, u32[]{:S(2)}, u32[]{:S(2)}) collective-permute-start(bf16[128,576]{1,0:T(8,128)(2,1)S(1)} %get-tuple-element.50), channel_id=1, source_target_pairs={{0,64},{16,80},{32,96},{48,112},{64,128},{80,144},{96,160},{112,17... | collective-permute-start | bytes 442376 | tf_op jit(solution)/shard_map/ppermute | solution.py:300
  13.6 4.1 %collective-permute-start.1 = (bf16[128,576]{1,0:T(8,128)(2,1)S(1)}, bf16[128,576]{1,0:T(8,128)(2,1)S(1)}, u32[]{:S(2)}, u32[]{:S(2)}) collective-permute-start(bf16[128,576]{1,0:T(8,128)(2,1)S(1)} %get-tuple-element.50), channel_id=1, source_target_pairs={{0,32},{16,48},{32,64},{48,80},{64,96},{80,112},{96,128},{112,144}... | collective-permute-start | bytes 442376 | tf_op jit(solution)/shard_map/ppermute | solution.py:300
  17.7 0.3 collective-permute-done
  18.0 3.9 %collective-permute-done.1 = bf16[128,576]{1,0:T(8,128)(2,1)S(1)} collective-permute-done((bf16[128,576]{1,0:T(8,128)(2,1)S(1)}, bf16[128,576]{1,0:T(8,128)(2,1)S(1)}, u32[]{:S(2)}, u32[]{:S(2)}) %collective-permute-start.1) | collective-permute-done | bytes 147488 | tf_op jit(solution)/shard_map/ppermute | solution.py:300
  21.9 0.1 pad_maximum_fusion.keys_near
  22.0 0.0 copy-start.2
  22.1 0.0 all-to-all-done
  22.1 1.1 broadcast_in_dim.10
  23.2 5.5 %all-to-all-start.1 = ((bf16[4,4,16,2048]{3,2,1,0:T(8,128)(2,1)}), bf16[4,4,16,2048]{3,2,1,0:T(8,128)(2,1)S(1)}, u32[]{:S(2)}, u32[]{:S(2)}) async-start(bf16[4,4,16,2048]{3,2,1,0:T(8,128)(2,1)} %broadcast_in_dim.10), calls=%async_computation.1 | async-start | bytes 2097152 | tf_op jit(solution)/shard_map/all_to_all | solution.py:269
  28.7 0.0 copy-done.2
  28.7 1.9 %collective-permute-start.2 = (bf16[3,128,576]{2,1,0:T(8,128)(2,1)S(1)}, bf16[3,128,576]{2,1,0:T(8,128)(2,1)S(1)}, u32[]{:S(2)}, u32[]{:S(2)}) collective-permute-start(bf16[3,128,576]{2,1,0:T(8,128)(2,1)S(1)} %pad_maximum_fusion.keys_near), channel_id=1, source_target_pairs={{0,16},{16,0},{32,48},{48,32},{64,80},{80,64},{96,112},{112,96},{1... | collective-permute-start | bytes 1327112 | tf_op jit(solution)/shard_map/ppermute | solution.py:296
  30.6 1.8 %collective-permute-done.2.keys_far = bf16[3,128,576]{2,1,0:T(8,128)(2,1)S(1)} collective-permute-done((bf16[3,128,576]{2,1,0:T(8,128)(2,1)S(1)}, bf16[3,128,576]{2,1,0:T(8,128)(2,1)S(1)}, u32[]{:S(2)}, u32[]{:S(2)}) %collective-permute-start.2) | collective-permute-done | bytes 442400 | tf_op jit(solution)/shard_map/ppermute | solution.py:296
  32.4 0.0 copy-start.7
  32.4 6.4 %all-to-all-done.1.weights_mine = bf16[4,4,16,2048]{3,2,1,0:T(8,128)(2,1)S(1)} async-done(((bf16[4,4,16,2048]{3,2,1,0:T(8,128)(2,1)}), bf16[4,4,16,2048]{3,2,1,0:T(8,128)(2,1)S(1)}, u32[]{:S(2)}, u32[]{:S(2)}) %all-to-all-start.1) | async-done | bytes 1048608 | tf_op jit(solution)/shard_map/all_to_all | solution.py:269
  38.8 0.0 copy-start.1
  38.8 1.9 %collective-permute-start.3 = (bf16[4,4,16,2048]{3,2,1,0:T(8,128)(2,1)S(1)}, bf16[4,4,16,2048]{3,2,1,0:T(8,128)(2,1)S(1)}, u32[]{:S(2)}, u32[]{:S(2)}) collective-permute-start(bf16[4,4,16,2048]{3,2,1,0:T(8,128)(2,1)S(1)} %all-to-all-done.1.weights_mine), channel_id=1, source_target_pairs={{0,16},{16,0},{32,48},{48,32},{64,80},{80,64},{96,112},{112,96},{1... | collective-permute-start | bytes 3145736 | tf_op jit(solution)/shard_map/ppermute | solution.py:296
  40.7 2.6 %collective-permute-done.3.weights_theirs = bf16[4,4,16,2048]{3,2,1,0:T(8,128)(2,1)S(1)} collective-permute-done((bf16[4,4,16,2048]{3,2,1,0:T(8,128)(2,1)S(1)}, bf16[4,4,16,2048]{3,2,1,0:T(8,128)(2,1)S(1)}, u32[]{:S(2)}, u32[]{:S(2)}) %collective-permute-start.3) | collective-permute-done | bytes 1048608 | tf_op jit(solution)/shard_map/ppermute | solution.py:296
  43.4 0.0 copy-start.6
  43.4 0.0 copy-done.7
  43.4 0.0 copy-done.1
  43.4 0.9 copy-done.6
  44.3 15.2 %shard_map.136 = (bf16[128,1024]{1,0:T(8,128)(2,1)}, bf16[128,512]{1,0:T(8,128)(2,1)}, bf16[2,128,576]{2,1,0:T(8,128)(2,1)}, bf16[2,128,576]{2,1,0:T(8,128)(2,1)...) custom-call(s32[1]{0:T(128)} %bitcast.place, f32[1,128]{1,0:T(1,128)} %bitcast.23, ...), custom_call_target="tpu_custom_call" | custom-call | flops 5000000000 | bytes 8000000 | tf_op jit(solution)/shard_map/pallas_call | solution.py:207
  59.5 0.0 copy-start
  59.5 2.2 %collective-permute-start.4 = (bf16[4,4,16,2048]{3,2,1,0:T(8,128)(2,1)}, bf16[4,4,16,2048]{3,2,1,0:T(8,128)(2,1)S(1)}, u32[]{:S(2)}, u32[]{:S(2)}) collective-permute-start(bf16[4,4,16,2048]{3,2,1,0:T(8,128)(2,1)} %get-tuple-element.36), channel_id=1, source_target_pairs={{0,16},{16,0},{32,48},{48,32},{64,80},{80,64},{96,112},{112,96},{1... | collective-permute-start | bytes 3145736 | tf_op jit(solution)/shard_map/ppermute | solution.py:296
  61.7 2.3 %collective-permute-start.5 = (bf16[2,128,576]{2,1,0:T(8,128)(2,1)}, bf16[2,128,576]{2,1,0:T(8,128)(2,1)S(1)}, u32[]{:S(2)}, u32[]{:S(2)}) collective-permute-start(bf16[2,128,576]{2,1,0:T(8,128)(2,1)} %get-tuple-element.38), channel_id=1, source_target_pairs={{0,16},{16,0},{32,48},{48,32},{64,80},{80,64},{96,112},{112,96},{1... | collective-permute-start | bytes 884744 | tf_op jit(solution)/shard_map/ppermute | solution.py:296
  64.0 1.4 collective-permute-done.5
  65.4 1.0 fusion.3
  66.4 0.0 collective-permute-done.4
  66.4 0.0 copy-done
  66.4 1.4 add_convert_fusion
  67.8 0.0 copy-start.4
  67.8 5.6 %all-to-all-start.2 = ((bf16[4,4,16,2048]{3,2,1,0:T(8,128)(2,1)}), bf16[4,4,16,2048]{3,2,1,0:T(8,128)(2,1)S(1)}, u32[]{:S(2)}, u32[]{:S(2)}) async-start(bf16[4,4,16,2048]{3,2,1,0:T(8,128)(2,1)} %add_convert_fusion), calls=%async_computation.2 | async-start | bytes 2097152 | tf_op jit(solution)/shard_map/all_to_all | solution.py:333
  73.4 2.8 %collective-permute-start.6 = (bf16[128,576]{1,0:T(8,128)(2,1)S(1)}, bf16[128,576]{1,0:T(8,128)(2,1)S(1)}, u32[]{:S(2)}, u32[]{:S(2)}) collective-permute-start(bf16[128,576]{1,0:T(8,128)(2,1)S(1)} %fusion.3), channel_id=1, source_target_pairs={{32,0},{48,16},{64,32},{80,48},{96,64},{112,80},{128,96},{144,112}... | collective-permute-start | bytes 442376 | tf_op jit(solution)/shard_map/ppermute | solution.py:300
  76.2 12.7 %collective-permute-done.6 = bf16[128,576]{1,0:T(8,128)(2,1)S(1)} collective-permute-done((bf16[128,576]{1,0:T(8,128)(2,1)S(1)}, bf16[128,576]{1,0:T(8,128)(2,1)S(1)}, u32[]{:S(2)}, u32[]{:S(2)}) %collective-permute-start.6) | collective-permute-done | bytes 147488 | tf_op jit(solution)/shard_map/ppermute | solution.py:300
  88.9 0.0 copy-done.4
  88.9 0.1 fusion.2
  89.0 0.0 copy-start.3
  89.0 1.6 %all-to-all-done.2 = bf16[4,4,16,2048]{3,2,1,0:T(8,128)(2,1)S(1)} async-done(((bf16[4,4,16,2048]{3,2,1,0:T(8,128)(2,1)}), bf16[4,4,16,2048]{3,2,1,0:T(8,128)(2,1)S(1)}, u32[]{:S(2)}, u32[]{:S(2)}) %all-to-all-start.2) | async-done | bytes 1048608 | tf_op jit(solution)/shard_map/all_to_all | solution.py:333
  90.5 0.9 reduce_sum.12
  91.5 7.1 %all-to-all-start.3 = ((bf16[4,16,2048]{2,1,0:T(8,128)(2,1)}), bf16[4,16,2048]{2,1,0:T(8,128)(2,1)S(1)}, u32[]{:S(2)}, u32[]{:S(2)}) async-start(bf16[4,16,2048]{2,1,0:T(8,128)(2,1)} %reduce_sum.12), calls=%async_computation.3 | async-start | bytes 524288 | tf_op jit(solution)/shard_map/all_to_all | solution.py:337
  98.6 4.1 %collective-permute-start.7 = (bf16[128,576]{1,0:T(8,128)(2,1)S(1)}, bf16[128,576]{1,0:T(8,128)(2,1)S(1)}, u32[]{:S(2)}, u32[]{:S(2)}) collective-permute-start(bf16[128,576]{1,0:T(8,128)(2,1)S(1)} %fusion.2), channel_id=1, source_target_pairs={{32,0},{48,16},{64,32},{80,48},{96,64},{112,80},{128,96},{144,112}... | collective-permute-start | bytes 442376 | tf_op jit(solution)/shard_map/ppermute | solution.py:300
  102.7 9.7 %collective-permute-done.7 = bf16[128,576]{1,0:T(8,128)(2,1)S(1)} collective-permute-done((bf16[128,576]{1,0:T(8,128)(2,1)S(1)}, bf16[128,576]{1,0:T(8,128)(2,1)S(1)}, u32[]{:S(2)}, u32[]{:S(2)}) %collective-permute-start.7) | collective-permute-done | bytes 147488 | tf_op jit(solution)/shard_map/ppermute | solution.py:300
  112.3 0.0 copy-done.3
  112.3 0.7 fusion.1
  113.1 0.0 all-to-all-done.3.shares
  113.1 15.0 %all-to-all-start.4 = ((bf16[16,8,576]{2,1,0:T(8,128)(2,1)}), bf16[16,8,576]{2,1,0:T(8,128)(2,1)S(1)}, u32[]{:S(2)}, u32[]{:S(2)}) async-start(bf16[16,8,576]{2,1,0:T(8,128)(2,1)} %bitcast.9), calls=%async_computation.4 | async-start | bytes 327680 | tf_op jit(solution)/shard_map/all_to_all | solution.py:342
  128.1 0.7 shard_map.138
  128.7 16.7 %all-to-all-done.4.shares = bf16[16,8,576]{2,1,0:T(8,128)(2,1)S(1)} async-done(((bf16[16,8,576]{2,1,0:T(8,128)(2,1)}), bf16[16,8,576]{2,1,0:T(8,128)(2,1)S(1)}, u32[]{:S(2)}, u32[]{:S(2)}) %all-to-all-start.4) | async-done | bytes 147488 | tf_op jit(solution)/shard_map/all_to_all | solution.py:342
  145.4 0.6 shard_map.137
  (2 shorter events, 0.1 us)
Async XLA Ops:
  0.6 8.3 %copy-start.5 = (bf16[128,512]{1,0:T(8,128)(2,1)S(1)}, bf16[128,512]{1,0:T(8,128)(2,1)}, u32[]{:S(2)}) copy-start(bf16[128,512]{1,0:T(8,128)(2,1)} %param.11) | copy-start | bytes 393220
  2.2 19.9 %all-to-all-start = ((bf16[4,16,2048]{2,1,0:T(8,128)(2,1)}), bf16[4,16,2048]{2,1,0:T(8,128)(2,1)S(1)}, u32[]{:S(2)}, u32[]{:S(2)}) async-start(bf16[4,16,2048]{2,1,0:T(8,128)(2,1)} %broadcast_in_dim.8), calls=%async_computation | async-start | bytes 524288 | tf_op jit(solution)/shard_map/all_to_all | solution.py:269
  8.9 9.1 %collective-permute-start = (bf16[128,576]{1,0:T(8,128)(2,1)S(1)}, bf16[128,576]{1,0:T(8,128)(2,1)S(1)}, u32[]{:S(2)}, u32[]{:S(2)}) collective-permute-start(bf16[128,576]{1,0:T(8,128)(2,1)S(1)} %get-tuple-element.50), channel_id=1, source_target_pairs={{0,64},{16,80},{32,96},{48,112},{64,128},{80,144},{96,160},{112,17... | collective-permute-start | bytes 442376 | tf_op jit(solution)/shard_map/ppermute | solution.py:300
  13.6 8.4 %collective-permute-start.1 = (bf16[128,576]{1,0:T(8,128)(2,1)S(1)}, bf16[128,576]{1,0:T(8,128)(2,1)S(1)}, u32[]{:S(2)}, u32[]{:S(2)}) collective-permute-start(bf16[128,576]{1,0:T(8,128)(2,1)S(1)} %get-tuple-element.50), channel_id=1, source_target_pairs={{0,32},{16,48},{32,64},{48,80},{64,96},{80,112},{96,128},{112,144}... | collective-permute-start | bytes 442376 | tf_op jit(solution)/shard_map/ppermute | solution.py:300
  22.0 6.6 %copy-start.2 = (bf16[3,128,576]{2,1,0:T(8,128)(2,1)}, bf16[3,128,576]{2,1,0:T(8,128)(2,1)S(1)}, u32[]{:S(2)}) copy-start(bf16[3,128,576]{2,1,0:T(8,128)(2,1)S(1)} %pad_maximum_fusion.keys_near) | copy-start | bytes 1327108
  23.2 15.6 %all-to-all-start.1 = ((bf16[4,4,16,2048]{3,2,1,0:T(8,128)(2,1)}), bf16[4,4,16,2048]{3,2,1,0:T(8,128)(2,1)S(1)}, u32[]{:S(2)}, u32[]{:S(2)}) async-start(bf16[4,4,16,2048]{3,2,1,0:T(8,128)(2,1)} %broadcast_in_dim.10), calls=%async_computation.1 | async-start | bytes 2097152 | tf_op jit(solution)/shard_map/all_to_all | solution.py:269
  28.7 3.7 %collective-permute-start.2 = (bf16[3,128,576]{2,1,0:T(8,128)(2,1)S(1)}, bf16[3,128,576]{2,1,0:T(8,128)(2,1)S(1)}, u32[]{:S(2)}, u32[]{:S(2)}) collective-permute-start(bf16[3,128,576]{2,1,0:T(8,128)(2,1)S(1)} %pad_maximum_fusion.keys_near), channel_id=1, source_target_pairs={{0,16},{16,0},{32,48},{48,32},{64,80},{80,64},{96,112},{112,96},{1... | collective-permute-start | bytes 1327112 | tf_op jit(solution)/shard_map/ppermute | solution.py:296
  32.4 10.9 %copy-start.7 = (bf16[3,128,576]{2,1,0:T(8,128)(2,1)}, bf16[3,128,576]{2,1,0:T(8,128)(2,1)S(1)}, u32[]{:S(2)}) copy-start(bf16[3,128,576]{2,1,0:T(8,128)(2,1)S(1)} %collective-permute-done.2.keys_far) | copy-start | bytes 1327108
  38.8 4.6 %copy-start.1 = (bf16[4,4,16,2048]{3,2,1,0:T(8,128)(2,1)}, bf16[4,4,16,2048]{3,2,1,0:T(8,128)(2,1)S(1)}, u32[]{:S(2)}) copy-start(bf16[4,4,16,2048]{3,2,1,0:T(8,128)(2,1)S(1)} %all-to-all-done.1.weights_mine) | copy-start | bytes 3145732
  38.8 4.5 %collective-permute-start.3 = (bf16[4,4,16,2048]{3,2,1,0:T(8,128)(2,1)S(1)}, bf16[4,4,16,2048]{3,2,1,0:T(8,128)(2,1)S(1)}, u32[]{:S(2)}, u32[]{:S(2)}) collective-permute-start(bf16[4,4,16,2048]{3,2,1,0:T(8,128)(2,1)S(1)} %all-to-all-done.1.weights_mine), channel_id=1, source_target_pairs={{0,16},{16,0},{32,48},{48,32},{64,80},{80,64},{96,112},{112,96},{1... | collective-permute-start | bytes 3145736 | tf_op jit(solution)/shard_map/ppermute | solution.py:296
  43.4 0.9 copy-start.6
  59.5 7.0 %copy-start = (bf16[4,4,16,2048]{3,2,1,0:T(8,128)(2,1)S(1)}, bf16[4,4,16,2048]{3,2,1,0:T(8,128)(2,1)}, u32[]{:S(2)}) copy-start(bf16[4,4,16,2048]{3,2,1,0:T(8,128)(2,1)} %get-tuple-element.35) | copy-start | bytes 3145732
  59.5 6.9 %collective-permute-start.4 = (bf16[4,4,16,2048]{3,2,1,0:T(8,128)(2,1)}, bf16[4,4,16,2048]{3,2,1,0:T(8,128)(2,1)S(1)}, u32[]{:S(2)}, u32[]{:S(2)}) collective-permute-start(bf16[4,4,16,2048]{3,2,1,0:T(8,128)(2,1)} %get-tuple-element.36), channel_id=1, source_target_pairs={{0,16},{16,0},{32,48},{48,32},{64,80},{80,64},{96,112},{112,96},{1... | collective-permute-start | bytes 3145736 | tf_op jit(solution)/shard_map/ppermute | solution.py:296
  61.7 3.7 %collective-permute-start.5 = (bf16[2,128,576]{2,1,0:T(8,128)(2,1)}, bf16[2,128,576]{2,1,0:T(8,128)(2,1)S(1)}, u32[]{:S(2)}, u32[]{:S(2)}) collective-permute-start(bf16[2,128,576]{2,1,0:T(8,128)(2,1)} %get-tuple-element.38), channel_id=1, source_target_pairs={{0,16},{16,0},{32,48},{48,32},{64,80},{80,64},{96,112},{112,96},{1... | collective-permute-start | bytes 884744 | tf_op jit(solution)/shard_map/ppermute | solution.py:296
  67.8 21.1 %copy-start.4 = (bf16[2,128,576]{2,1,0:T(8,128)(2,1)S(1)}, bf16[2,128,576]{2,1,0:T(8,128)(2,1)}, u32[]{:S(2)}) copy-start(bf16[2,128,576]{2,1,0:T(8,128)(2,1)} %get-tuple-element.37) | copy-start | bytes 884740
  67.8 22.7 %all-to-all-start.2 = ((bf16[4,4,16,2048]{3,2,1,0:T(8,128)(2,1)}), bf16[4,4,16,2048]{3,2,1,0:T(8,128)(2,1)S(1)}, u32[]{:S(2)}, u32[]{:S(2)}) async-start(bf16[4,4,16,2048]{3,2,1,0:T(8,128)(2,1)} %add_convert_fusion), calls=%async_computation.2 | async-start | bytes 2097152 | tf_op jit(solution)/shard_map/all_to_all | solution.py:333
  73.4 15.5 %collective-permute-start.6 = (bf16[128,576]{1,0:T(8,128)(2,1)S(1)}, bf16[128,576]{1,0:T(8,128)(2,1)S(1)}, u32[]{:S(2)}, u32[]{:S(2)}) collective-permute-start(bf16[128,576]{1,0:T(8,128)(2,1)S(1)} %fusion.3), channel_id=1, source_target_pairs={{32,0},{48,16},{64,32},{80,48},{96,64},{112,80},{128,96},{144,112}... | collective-permute-start | bytes 442376 | tf_op jit(solution)/shard_map/ppermute | solution.py:300
  89.0 23.4 %copy-start.3 = (f32[128,576]{1,0:T(8,128)S(1)}, f32[128,576]{1,0:T(8,128)}, u32[]{:S(2)}) copy-start(f32[128,576]{1,0:T(8,128)} %get-tuple-element.42) | copy-start | bytes 884740
  91.5 21.6 %all-to-all-start.3 = ((bf16[4,16,2048]{2,1,0:T(8,128)(2,1)}), bf16[4,16,2048]{2,1,0:T(8,128)(2,1)S(1)}, u32[]{:S(2)}, u32[]{:S(2)}) async-start(bf16[4,16,2048]{2,1,0:T(8,128)(2,1)} %reduce_sum.12), calls=%async_computation.3 | async-start | bytes 524288 | tf_op jit(solution)/shard_map/all_to_all | solution.py:337
  98.6 13.8 %collective-permute-start.7 = (bf16[128,576]{1,0:T(8,128)(2,1)S(1)}, bf16[128,576]{1,0:T(8,128)(2,1)S(1)}, u32[]{:S(2)}, u32[]{:S(2)}) collective-permute-start(bf16[128,576]{1,0:T(8,128)(2,1)S(1)} %fusion.2), channel_id=1, source_target_pairs={{32,0},{48,16},{64,32},{80,48},{96,64},{112,80},{128,96},{144,112}... | collective-permute-start | bytes 442376 | tf_op jit(solution)/shard_map/ppermute | solution.py:300
  113.1 32.4 %all-to-all-start.4 = ((bf16[16,8,576]{2,1,0:T(8,128)(2,1)}), bf16[16,8,576]{2,1,0:T(8,128)(2,1)S(1)}, u32[]{:S(2)}, u32[]{:S(2)}) async-start(bf16[16,8,576]{2,1,0:T(8,128)(2,1)} %bitcast.9), calls=%async_computation.4 | async-start | bytes 327680 | tf_op jit(solution)/shard_map/all_to_all | solution.py:342

commit v3 on v2

v3 whole, which is shorter than its diff:
```python
import math

import jax
import jax.numpy as jnp
from jax import lax
from jax.experimental import pallas as pl
from jax.experimental.pallas import tpu as pltpu
from jax.sharding import PartitionSpec as P

LAT = 512
ROPE = 64
NOPE = 128
VDIM = 128
FAR = -1e30
MIB = 1024 * 1024


def dot_nt(left, right):
    return lax.dot_general(
        left, right, (((1,), (1,)), ((), ())), preferred_element_type=jnp.float32
    )


def dot_nn(left, right):
    return lax.dot_general(
        left, right, (((1,), (0,)), ((), ())), preferred_element_type=jnp.float32
    )


def dot_tn(left, right):
    return lax.dot_general(
        left, right, (((0,), (0,)), ((), ())), preferred_element_type=jnp.float32
    )


def column_of(row, count):
    return jnp.transpose(jnp.broadcast_to(row, (count, count)))


def split_kernel(place, advantage, queries, rotated, cotangent, kept, lent):
    rows, width = queries.shape
    half, rope_half = width // 2, rotated.shape[1] // 2
    core = lax.rem(place[0], 2)
    column = column_of(advantage[...], rows)[:, :1]
    for side, out in ((core, kept), (1 - core, lent)):
        here = pl.ds(pl.multiple_of(side * half, half), half)
        rope = pl.ds(pl.multiple_of(side * rope_half, rope_half), rope_half)
        out[:, :half] = queries[:, here]
        out[:, half:width] = (column * cotangent[:, here].astype(jnp.float32)).astype(jnp.bfloat16)
        out[:, width:] = rotated[:, rope]


def join_kernel(place, kept, returned, d_q_nope, d_q_rope):
    width, rope_width = d_q_nope.shape[1], d_q_rope.shape[1]
    half, rope_half = width // 2, rope_width // 2
    core = lax.rem(place[0], 2)
    for side, part in ((core, kept), (1 - core, returned)):
        here = pl.ds(pl.multiple_of(side * half, half), half)
        rope = pl.ds(pl.multiple_of(side * rope_half, rope_half), rope_half)
        d_q_nope[:, here] = part[:, :half]
        d_q_rope[:, rope] = part[:, half:]


def layer_kernel(
    place,
    segment,
    rows_kept,
    rows_lent,
    keys_near,
    keys_far,
    weights_in,
    d_rows_kept,
    d_rows_lent,
    grad_kept,
    grad_given,
    d_weights_out,
    tokens,
    weights,
    key_blocks,
    keys_t,
    bias,
    absorbed,
    back_lat,
    probs_low,
    grad_score,
    d_tokens,
    d_keys,
    d_weights,
    in_sems,
    out_sems,
):
    rows = tokens.shape[1]
    half = weights.shape[4] // 2
    heads = half // NOPE
    blocks = 2 * key_blocks.shape[0]
    span = (blocks - 1) * rows
    ring = weights.shape[1]
    scale = 1.0 / math.sqrt(NOPE + ROPE)
    core = lax.rem(place[0], 2)
    first = place[0] - core

    loads = []

    def load(source, target):
        copy = pltpu.make_async_copy(source, target, in_sems.at[len(loads)])
        copy.start()
        loads.append(copy)

    load(keys_near, key_blocks.at[:, core])
    load(keys_far, key_blocks.at[:, 1 - core])
    load(rows_kept, tokens.at[core])
    load(rows_lent, tokens.at[1 - core])
    for step in range(ring):
        load(weights_in.at[step], weights.at[:, step])

    query_at = lax.broadcasted_iota(jnp.int32, (rows, rows), 1)
    key_at = lax.broadcasted_iota(jnp.int32, (rows, rows), 0)
    query_segments = [segment[pl.ds(first + block, 1), :] for block in range(2)]
    for slot in range(blocks):
        owner = first - (blocks - 2) + slot
        key_row = segment[pl.ds(jnp.maximum(owner, 0), 1), :]
        key_segment = column_of(key_row, rows)
        for block in range(2):
            at = slot - block
            if not 0 <= at < blocks - 1:
                continue
            allowed = (key_segment == query_segments[block]) & (owner >= 0)
            if at == blocks - 2:
                allowed = allowed & (key_at <= query_at)
            bias[block, at * rows : (at + 1) * rows, :] = jnp.where(allowed, 0.0, FAR)

    loads[0].wait()
    loads[1].wait()
    for slot in range(blocks):
        here = slice(slot * rows, (slot + 1) * rows)
        keys_t[:, here] = jnp.transpose(key_blocks[slot // 2, slot % 2])
    for copy in loads[2:]:
        copy.wait()

    stores = []

    def store(source, target):
        copy = pltpu.make_async_copy(source, target, out_sems.at[len(stores)])
        copy.start()
        stores.append(copy)

    def head_weights(start):
        return weights[:, :, :, :, start : start + NOPE].reshape(LAT, NOPE)

    def keys_of(block, wide):
        return key_blocks[:, :, :, :wide].reshape(blocks * rows, wide)[
            block * rows : block * rows + span
        ]

    wide = LAT + ROPE
    units = [(pair, block) for pair in range(heads // 2) for block in range(2)]

    def columns_of(unit):
        pair, block = unit
        start = (block * heads + 2 * pair) * rows
        return slice(start, start + 2 * rows)

    def project(pair):
        for head in (2 * pair, 2 * pair + 1):
            nope = slice(head * NOPE, (head + 1) * NOPE)
            values = slice(half + head * VDIM, half + (head + 1) * VDIM)
            rope = slice(2 * half + head * ROPE, 2 * half + (head + 1) * ROPE)
            up = dot_nt(tokens[:, :, nope].reshape(2 * rows, NOPE), head_weights(nope.start))
            back = dot_nt(tokens[:, :, values].reshape(2 * rows, VDIM), head_weights(values.start))
            for block in range(2):
                here = slice((block * heads + head) * rows, (block * heads + head + 1) * rows)
                there = slice(block * rows, (block + 1) * rows)
                absorbed[here, :LAT] = up[there].astype(jnp.bfloat16)
                absorbed[here, LAT:] = tokens[block, :, rope]
                back_lat[here, :] = back[there].astype(jnp.bfloat16)

    def products(unit):
        here = columns_of(unit)
        scores = dot_nt(keys_of(unit[1], wide), absorbed[here, :])
        grad_prob = dot_nt(keys_of(unit[1], LAT), back_lat[here, :])
        return scores, grad_prob

    def soften(unit, scores, grad_prob):
        block = unit[1]
        mask = bias[block]
        scores = scores * scale + jnp.concatenate([mask, mask], axis=1)
        exponent = jnp.exp(scores - jnp.max(scores, axis=0, keepdims=True))
        probs = exponent * (1.0 / jnp.sum(exponent, axis=0, keepdims=True))
        low = probs.astype(jnp.bfloat16)
        row_delta = jnp.sum(probs * grad_prob, axis=0, keepdims=True)
        score = (probs * (grad_prob - row_delta) * scale).astype(jnp.bfloat16)
        here = columns_of(unit)
        probs_low[block * rows : block * rows + span, here] = low
        grad_score[block * rows : block * rows + span, here] = score
        there = slice(block * rows, block * rows + span)
        out_lat = dot_nn(keys_t[:LAT, there], low).astype(jnp.bfloat16)
        grad_abs = dot_nn(keys_t[:, there], score).astype(jnp.bfloat16)
        return out_lat, grad_abs

    def finish(pair, results):
        for block in range(2):
            rope_rows = results[block][1][LAT:, :].astype(jnp.float32)
            rope_rows = jnp.concatenate([rope_rows[:, :rows], rope_rows[:, rows:]], axis=0)
            start = half + 2 * pair * ROPE
            d_tokens[block, :, start : start + 2 * ROPE] = jnp.transpose(rope_rows).astype(
                jnp.bfloat16
            )
        for side, head in enumerate((2 * pair, 2 * pair + 1)):
            nope = slice(head * NOPE, (head + 1) * NOPE)
            values = slice(half + head * VDIM, half + (head + 1) * VDIM)
            mine = slice(side * rows, (side + 1) * rows)
            out_lat = jnp.concatenate([results[0][0][:, mine], results[1][0][:, mine]], axis=1)
            grad_abs = jnp.concatenate(
                [results[0][1][:LAT, mine], results[1][1][:LAT, mine]], axis=1
            )
            d_query = dot_tn(grad_abs, head_weights(nope.start)).astype(jnp.bfloat16)
            for block in range(2):
                d_tokens[block, :, nope] = d_query[block * rows : (block + 1) * rows]
            shape = weights.shape[:4] + (NOPE,)
            for columns, lead in ((nope, grad_abs), (values, out_lat)):
                term = dot_nn(lead, tokens[:, :, columns].reshape(2 * rows, NOPE))
                d_weights[:, :, :, :, columns] = term.astype(jnp.bfloat16).reshape(shape)
        for start in (2 * pair * NOPE, half + 2 * pair * VDIM):
            columns = pl.ds(start, 2 * NOPE)
            for step in range(ring):
                store(d_weights.at[:, step, :, :, columns], d_weights_out.at[step, :, :, :, columns])

    project(0)
    ahead = products(units[0])
    results = []
    for at, unit in enumerate(units):
        now = ahead
        if at + 1 < len(units):
            if units[at + 1][1] == 0:
                project(units[at + 1][0])
            ahead = products(units[at + 1])
        results.append(soften(unit, *now))
        if unit[1] == 1:
            finish(unit[0], results[-2:])
    store(d_tokens.at[core], d_rows_kept)
    store(d_tokens.at[1 - core], d_rows_lent)

    many = heads * rows
    for slot in range(blocks):
        here = slice(slot * rows, (slot + 1) * rows)
        low, high = (0, 2 * many)
        if slot == 0:
            high = many
        if slot == blocks - 1:
            low = many
        total = dot_nn(grad_score[here, low:high], absorbed[low:high, :])
        total_lat = total[:, :LAT] + dot_nn(probs_low[here, low:high], back_lat[low:high, :])
        d_keys[slot // 2, slot % 2, :, :LAT] = total_lat.astype(jnp.bfloat16)
        d_keys[slot // 2, slot % 2, :, LAT:] = total[:, LAT:].astype(jnp.bfloat16)
        if slot % 2 == 1:
            chip = slot // 2
            store(d_keys.at[chip, 1 - core], grad_given.at[chip])
            store(d_keys.at[chip, core], grad_kept.at[chip])
    for copy in stores:
        copy.wait()


WHOLE = pl.BlockSpec(memory_space=pltpu.VMEM)
SCALAR = pl.BlockSpec(memory_space=pltpu.SMEM)
APART = pl.BlockSpec(memory_space=pl.ANY)


def cost(flops, moved):
    return pl.CostEstimate(flops=flops, bytes_accessed=moved, transcendentals=0)


def layer(place, segment, kept, lent, near, far, weights):
    rows, packed = kept.shape
    chips, wide = near.shape[0], near.shape[2]
    ring, steps, cores, piece, width = weights.shape
    half = width // 2
    heads = half // NOPE
    span = (2 * chips - 1) * rows
    d_packed = half + heads * ROPE
    parts = (steps, ring, cores, piece, width)
    bf16 = jnp.bfloat16
    return pl.pallas_call(
        layer_kernel,
        out_shape=(
            jax.ShapeDtypeStruct((rows, d_packed), bf16),
            jax.ShapeDtypeStruct((rows, d_packed), bf16),
            jax.ShapeDtypeStruct(near.shape, bf16),
            jax.ShapeDtypeStruct(near.shape, bf16),
            jax.ShapeDtypeStruct(weights.shape, bf16),
        ),
        in_specs=[SCALAR, WHOLE] + [APART] * 5,
        out_specs=(APART,) * 5,
        scratch_shapes=[
            pltpu.VMEM((2, rows, packed), bf16),
            pltpu.VMEM(parts, bf16),
            pltpu.VMEM((chips, 2, rows, wide), bf16),
            pltpu.VMEM((wide, 2 * chips * rows), bf16),
            pltpu.VMEM((2, span, rows), jnp.float32),
            pltpu.VMEM((2 * heads * rows, wide), bf16),
            pltpu.VMEM((2 * heads * rows, LAT), bf16),
            pltpu.VMEM((2 * chips * rows, 2 * heads * rows), bf16),
            pltpu.VMEM((2 * chips * rows, 2 * heads * rows), bf16),
            pltpu.VMEM((2, rows, d_packed), bf16),
            pltpu.VMEM((chips, 2, rows, wide), bf16),
            pltpu.VMEM(parts, bf16),
            pltpu.SemaphoreType.DMA((4 + ring,)),
            pltpu.SemaphoreType.DMA((heads * ring + 2 + 2 * chips,)),
        ],
        compiler_params=pltpu.CompilerParams(vmem_limit_bytes=56 * MIB),
        cost_estimate=cost(5_000_000_000, 8_000_000),
    )(place, segment, kept, lent, near, far, weights)


def split_heads(place, advantage, queries, rotated, cotangent):
    rows, width = queries.shape
    packed = jax.ShapeDtypeStruct((rows, width + rotated.shape[1] // 2), jnp.bfloat16)
    return pl.pallas_call(
        split_kernel,
        out_shape=(packed, packed),
        in_specs=[SCALAR] + [WHOLE] * 4,
        out_specs=(WHOLE, WHOLE),
        compiler_params=pltpu.CompilerParams(vmem_limit_bytes=8 * MIB),
        cost_estimate=cost(1_000_000, 1_300_000),
    )(place, advantage, queries, rotated, cotangent)


def join_heads(place, kept, returned, width, rope_width):
    rows = kept.shape[0]
    return pl.pallas_call(
        join_kernel,
        out_shape=(
            jax.ShapeDtypeStruct((rows, width), jnp.bfloat16),
            jax.ShapeDtypeStruct((rows, rope_width), jnp.bfloat16),
        ),
        in_specs=[SCALAR, WHOLE, WHOLE],
        out_specs=(WHOLE, WHOLE),
        compiler_params=pltpu.CompilerParams(vmem_limit_bytes=8 * MIB),
        cost_estimate=cost(1_000_000, 800_000),
    )(place, kept, returned)


def key_sum_kernel(shares, left, right):
    total = jnp.sum(shares[...].astype(jnp.float32), axis=0)
    left[...] = total[:, : left.shape[1]]
    right[...] = total[:, left.shape[1] :]


def up_sum_kernel(shares, left, right):
    half = shares.shape[3] // 2
    for core in range(2):
        total = jnp.sum(shares[:, core].astype(jnp.float32), axis=0)
        left[:, core * half : (core + 1) * half] = total[:, :half]
        right[:, core * half : (core + 1) * half] = total[:, half:]


def summed(kernel, shares, rows, widths):
    return pl.pallas_call(
        kernel,
        out_shape=tuple(jax.ShapeDtypeStruct((rows, width), jnp.float32) for width in widths),
        in_specs=[WHOLE],
        out_specs=(WHOLE, WHOLE),
        compiler_params=pltpu.CompilerParams(vmem_limit_bytes=8 * MIB),
        cost_estimate=cost(1_000_000, 500_000),
    )(shares)


def on_device(q_nope, q_rope, latent, k_rope, d_out, advantage, segment, w_uk, w_uv):
    rows, width = q_nope.shape
    piece = w_uk.shape[0]
    half = width // 2
    count = lax.axis_size("ctx")
    ring = 4
    steps = count // (2 * ring)
    place = lax.axis_index("ctx").reshape(1)

    def device(step, place, core):
        return (step * ring + place) * 2 + core

    along_y = [
        [device(step, place, core) for place in range(ring)]
        for step in range(steps)
        for core in range(2)
    ]
    along_z = [
        [device(step, place, core) for step in range(steps) for core in range(2)]
        for place in range(ring)
    ]

    def swapped(value):
        return lax.ppermute(value, "ctx", [(source, source ^ 1) for source in range(count)])

    def to_chip(value, chips):
        pairs = [(source, source + 2 * chips) for source in range(count)]
        return lax.ppermute(value, "ctx", [pair for pair in pairs if 0 <= pair[1] < count])

    def exchanged(value, groups):
        return lax.all_to_all(value, "ctx", 0, 0, axis_index_groups=groups, tiled=True)

    up = jnp.stack([w_uk.reshape(piece, 2, half), w_uv.reshape(piece, 2, half)], axis=2)
    up = up.reshape(piece, 2, width).transpose(1, 0, 2)
    up = jnp.broadcast_to(up[None], (steps, 2, piece, width)).reshape(2 * steps, piece, width)
    column = exchanged(up, along_z)
    keys = jnp.concatenate([latent, k_rope], axis=1)
    near = jnp.stack([to_chip(keys, 2), to_chip(keys, 1), keys])
    column, near = lax.optimization_barrier((column, near))
    spread = jnp.broadcast_to(column[None], (ring,) + column.shape)
    weights = exchanged(spread, along_y).reshape(ring, steps, 2, piece, width)
    far = swapped(near)
    kept, lent = split_heads(place, advantage.reshape(1, rows), q_nope, q_rope, d_out)
    borrowed = swapped(lent)

    d_kept, d_lent, grad_kept, grad_given, d_weights = layer(
        place, segment.reshape(count, rows), kept, borrowed, near, far, weights
    )

    got = swapped(grad_given)
    sums = grad_kept.astype(jnp.float32) + got.astype(jnp.float32)
    far_sum = sums[0].astype(jnp.bfloat16)
    d_weights, far_sum = lax.optimization_barrier((d_weights, far_sum))
    shares = exchanged(d_weights, along_y)
    near_sum = (sums[1] + to_chip(far_sum, -1).astype(jnp.float32)).astype(jnp.bfloat16)
    returned = swapped(d_lent)
    d_q_nope, d_q_rope = join_heads(place, d_kept, returned, width, q_rope.shape[1])
    shares, near_sum, d_q_nope = lax.optimization_barrier((shares, near_sum, d_q_nope))
    d_column = jnp.sum(shares.astype(jnp.float32), axis=0).astype(jnp.bfloat16)
    d_shares = exchanged(d_column.reshape(2 * steps, piece, width), along_z)
    total = (sums[2] + to_chip(near_sum, -1).astype(jnp.float32)).astype(jnp.bfloat16)
    d_shares, total = lax.optimization_barrier((d_shares, total))
    d_uk, d_uv = summed(
        up_sum_kernel, d_shares.reshape(steps, 2, piece, width), piece, (width, width)
    )
    heads_over = lax.axis_size("head")
    key_terms = lax.all_to_all(total, "head", 0, 0, tiled=True)
    key_terms = key_terms.reshape(heads_over, rows // heads_over, LAT + ROPE)
    d_latent, d_k_rope = summed(key_sum_kernel, key_terms, rows // heads_over, (LAT, ROPE))
    return (d_q_nope, d_q_rope, d_latent, d_k_rope, d_uk, d_uv)


def solution(mesh):
    placed = (
        P("ctx", "head"),
        P("ctx", "head"),
        P("ctx", None),
        P("ctx", None),
        P("ctx", "head"),
        P("ctx"),
        P(),
        P("ctx", "head"),
        P("ctx", "head"),
    )
    return jax.shard_map(
        on_device,
        mesh=mesh,
        in_specs=placed,
        out_specs=(
            P("ctx", "head"),
            P("ctx", "head"),
            P(("ctx", "head"), None),
            P(("ctx", "head"), None),
            P("ctx", "head"),
            P("ctx", "head"),
        ),
        check_vma=False,
    )
```

time: 147 us -> 140 us (0.952)
  starting transfers between devices: 62.9 us -> 59.7 us
  Pallas kernels: 16.5 us -> 13.6 us
  local copies, waits for them, and re-layouts: 3.65 us -> 5.97 us
  waiting for transfers between devices: 57.2 us -> 55.2 us
  other arithmetic: 5.04 us -> 3.06 us
    all_to_all x4, starting transfers between devices: 24.1 us -> 20.9 us  [exchanged(): lax.all_to_all(value, 'ctx', 0, 0, axis_index_groups=groups, tiled=True)]
    pallas_call x3 -> x5, Pallas kernels: 16.5 us -> 13.6 us  [the longest x1 11.4 us: layer(): pl.pallas_call(layer_kernel, out_shape=(jax.ShapeDtypeStruct((rows, d_pac...]
    ppermute x4, waiting for transfers between devices: 5.9 us -> 3.28 us  [swapped(): lax.ppermute(value, 'ctx', [(source, source ^ 1) for source in range(coun...]
    convert_element_type x5 -> x2, other arithmetic: 3.19 us -> 0.73 us  [the longest x1 0.69 us: on_device(): (sums[2] + to_chip(near_sum, -1).astype(jnp.float32)).astype(jnp.bfloat16)]
    all_to_all x4, waiting for transfers between devices: 7.96 us -> 6.18 us  [exchanged(): lax.all_to_all(value, 'ctx', 0, 0, axis_index_groups=groups, tiled=True)]
    ppermute x4, waiting for transfers between devices: 26.7 us -> 28.3 us  [to_chip(): lax.ppermute(value, 'ctx', [pair for pair in pairs if 0 <= pair[1] < count])]
    unnamed x17 -> x29, local copies, waits for them, and re-layouts: 1.79 us -> 3.17 us
  transfers between devices with their start and end apart: 13 -> 13, of which waited for: 10 -> 9; matrix products, arithmetic and copies ran while one was open for 2% -> 1% of each run, Pallas kernels for 0% -> 1%
where the time goes in v3:
time: 140 us; the launch traced here: 139 us
  starting transfers between devices  59.7 us (43%)
  waiting for transfers between devices  55.2 us (39%)
  Pallas kernels  13.6 us (10%)
  local copies, waits for them, and re-layouts  5.97 us (4%)
  other arithmetic  3.06 us (2%)
    ppermute x4, waiting for transfers between devices, to_chip(): lax.ppermute(value, 'ctx', [pair for pair in pairs if 0 <= pair[1] < count])  28.3 us
    all_to_all x4, starting transfers between devices, exchanged(): lax.all_to_all(value, 'ctx', 0, 0, axis_index_groups=groups, tiled=True)  20.9 us
    all_to_all x1, waiting for transfers between devices, on_device(): key_terms = lax.all_to_all(total, 'head', 0, 0, tiled=True)  17.5 us
    all_to_all x1, starting transfers between devices, on_device(): key_terms = lax.all_to_all(total, 'head', 0, 0, tiled=True)  16.2 us
    ppermute x4, starting transfers between devices, to_chip(): lax.ppermute(value, 'ctx', [pair for pair in pairs if 0 <= pair[1] < count])  14.5 us
    pallas_call x1, Pallas kernels, layer(): pl.pallas_call(layer_kernel, out_shape=(jax.ShapeDtypeStruct((rows, d_pac...  11.4 us
    ppermute x4, starting transfers between devices, swapped(): lax.ppermute(value, 'ctx', [(source, source ^ 1) for source in range(coun...  8.13 us
    all_to_all x4, waiting for transfers between devices, exchanged(): lax.all_to_all(value, 'ctx', 0, 0, axis_index_groups=groups, tiled=True)  6.18 us
  transfers between devices with their start and end apart: 13, of which 9 were waited for; matrix products, arithmetic and copies ran while one was open for 1% of the time, Pallas kernels for 1%

profile of v3, /device:TPU:24, one launch (start us, length us, event | category | flops | bytes accessed | tf_op | source)
XLA Modules:
  0.0 138.5 jit_solution(13080674742144732156)
XLA Ops:
  0.6 0.8 stack_reshape.6
  1.4 0.0 copy-start.9
  1.4 0.1 copy.16
  1.5 0.7 copy-done.9
  2.2 0.1 copy.17
  2.3 0.2 pad_maximum_fusion.2
  2.5 0.7 broadcast_in_dim.4
  3.2 0.0 copy-start.10
  3.2 6.0 %all-to-all-start = ((bf16[8,16,1024]{2,1,0:T(8,128)(2,1)}), bf16[8,16,1024]{2,1,0:T(8,128)(2,1)S(1)}, u32[]{:S(2)}, u32[]{:S(2)}) async-start(bf16[8,16,1024]{2,1,0:T(8,128)(2,1)} %bitcast.4), calls=%async_computation | async-start | bytes 524288 | tf_op jit(solution)/shard_map/all_to_all | solution.py:397
  9.2 0.0 copy-done.10
  9.2 0.1 copy.18
  9.3 0.0 copy-done.8
  9.4 6.4 %collective-permute-start.2 = (bf16[128,576]{1,0:T(8,128)(2,1)S(1)}, bf16[128,576]{1,0:T(8,128)(2,1)S(1)}, u32[]{:S(2)}, u32[]{:S(2)}) collective-permute-start(bf16[128,576]{1,0:T(8,128)(2,1)S(1)} %get-tuple-element.50), channel_id=1, source_target_pairs={{0,32},{16,48},{32,64},{48,80},{64,96},{80,112},{96,128},{112,144}... | collective-permute-start | bytes 442376 | tf_op jit(solution)/shard_map/ppermute | solution.py:394
  15.8 1.9 %collective-permute-start.1 = (bf16[128,576]{1,0:T(8,128)(2,1)S(1)}, bf16[128,576]{1,0:T(8,128)(2,1)S(1)}, u32[]{:S(2)}, u32[]{:S(2)}) collective-permute-start(bf16[128,576]{1,0:T(8,128)(2,1)S(1)} %get-tuple-element.50), channel_id=1, source_target_pairs={{0,64},{16,80},{32,96},{48,112},{64,128},{80,144},{96,160},{112,17... | collective-permute-start | bytes 442376 | tf_op jit(solution)/shard_map/ppermute | solution.py:394
  17.7 2.6 %collective-permute-done.2 = bf16[128,576]{1,0:T(8,128)(2,1)S(1)} collective-permute-done((bf16[128,576]{1,0:T(8,128)(2,1)S(1)}, bf16[128,576]{1,0:T(8,128)(2,1)S(1)}, u32[]{:S(2)}, u32[]{:S(2)}) %collective-permute-start.2) | collective-permute-done | bytes 147488 | tf_op jit(solution)/shard_map/ppermute | solution.py:394
  20.3 4.8 %collective-permute-done.1 = bf16[128,576]{1,0:T(8,128)(2,1)S(1)} collective-permute-done((bf16[128,576]{1,0:T(8,128)(2,1)S(1)}, bf16[128,576]{1,0:T(8,128)(2,1)S(1)}, u32[]{:S(2)}, u32[]{:S(2)}) %collective-permute-start.1) | collective-permute-done | bytes 147488 | tf_op jit(solution)/shard_map/ppermute | solution.py:394
  25.2 0.1 pad_maximum_fusion.keys_near
  25.2 0.0 copy-start.7
  25.3 0.0 all-to-all-done
  25.3 1.1 broadcast_in_dim.5
  26.4 0.0 copy-start
  26.4 4.6 %all-to-all-start.1 = ((bf16[4,8,16,1024]{3,2,1,0:T(8,128)(2,1)}), bf16[4,8,16,1024]{3,2,1,0:T(8,128)(2,1)S(1)}, u32[]{:S(2)}, u32[]{:S(2)}) async-start(bf16[4,8,16,1024]{3,2,1,0:T(8,128)(2,1)} %broadcast_in_dim.5), calls=%async_computation.1 | async-start | bytes 2097152 | tf_op jit(solution)/shard_map/all_to_all | solution.py:397
  31.0 0.0 copy-done.7
  31.0 1.9 %collective-permute-start.3 = (bf16[3,128,576]{2,1,0:T(8,128)(2,1)S(1)}, bf16[3,128,576]{2,1,0:T(8,128)(2,1)S(1)}, u32[]{:S(2)}, u32[]{:S(2)}) collective-permute-start(bf16[3,128,576]{2,1,0:T(8,128)(2,1)S(1)} %pad_maximum_fusion.keys_near), channel_id=1, source_target_pairs={{0,16},{16,0},{32,48},{48,32},{64,80},{80,64},{96,112},{112,96},{1... | collective-permute-start | bytes 1327112 | tf_op jit(solution)/shard_map/ppermute | solution.py:390
  33.0 0.0 copy-start.4
  33.0 0.0 copy-done
  33.0 0.0 copy-done.1
  33.0 0.0 copy-done.3
  33.0 0.6 copy-done.4
  33.6 0.2 shard_map.136
  33.8 0.0 copy-start.5
  33.8 0.7 copy-done.5
  34.5 2.4 %collective-permute-start = (bf16[128,1280]{1,0:T(8,128)(2,1)S(1)}, bf16[128,1280]{1,0:T(8,128)(2,1)S(1)}, u32[]{:S(2)}, u32[]{:S(2)}) collective-permute-start(bf16[128,1280]{1,0:T(8,128)(2,1)S(1)} %get-tuple-element.29), channel_id=1, source_target_pairs={{0,16},{16,0},{32,48},{48,32},{64,80},{80,64},{96,112},{112,96},{1... | collective-permute-start | bytes 983048 | tf_op jit(solution)/shard_map/ppermute | solution.py:390
  36.9 1.2 collective-permute-done.rows_lent
  38.2 0.0 collective-permute-done.3.keys_far
  38.2 5.1 %all-to-all-done.1 = bf16[4,8,16,1024]{3,2,1,0:T(8,128)(2,1)S(1)} async-done(((bf16[4,8,16,1024]{3,2,1,0:T(8,128)(2,1)}), bf16[4,8,16,1024]{3,2,1,0:T(8,128)(2,1)S(1)}, u32[]{:S(2)}, u32[]{:S(2)}) %all-to-all-start.1) | async-done | bytes 1048608 | tf_op jit(solution)/shard_map/all_to_all | solution.py:397
  43.2 0.0 copy-done.12
  43.2 0.0 copy-done.11
  43.2 1.0 copy-done.6
  44.2 11.4 %shard_map.137 = (bf16[128,768]{1,0:T(8,128)(2,1)}, bf16[128,768]{1,0:T(8,128)(2,1)}, bf16[3,128,576]{2,1,0:T(8,128)(2,1)}, bf16[3,128,576]{2,1,0:T(8,128)(2,1)}, bf16[4,4,2,16,1024]{4,3,2,1,0:T(8,128)(2,1)}) custom-call(s32[1]{0:T(128)} %bitcast.place, s32[32,128]{1,0:T(8,128)} %bitcast.35, bf16[128,1280]{1,0:T(8,128)(2,1)} %copy-done.5, ...), custom_call_target="tpu_custom_call" | custom-call | flops 5000000000 | bytes 8000000 | tf_op jit(solution)/shard_map/pallas_call | solution.py:282
  55.6 1.9 %collective-permute-start.4 = (bf16[3,128,576]{2,1,0:T(8,128)(2,1)}, bf16[3,128,576]{2,1,0:T(8,128)(2,1)S(1)}, u32[]{:S(2)}, u32[]{:S(2)}) collective-permute-start(bf16[3,128,576]{2,1,0:T(8,128)(2,1)} %get-tuple-element.34), channel_id=1, source_target_pairs={{0,16},{16,0},{32,48},{48,32},{64,80},{80,64},{96,112},{112,96},{1... | collective-permute-start | bytes 1327112 | tf_op jit(solution)/shard_map/ppermute | solution.py:390
  57.5 2.0 %collective-permute-done.4 = bf16[3,128,576]{2,1,0:T(8,128)(2,1)S(1)} collective-permute-done((bf16[3,128,576]{2,1,0:T(8,128)(2,1)}, bf16[3,128,576]{2,1,0:T(8,128)(2,1)S(1)}, u32[]{:S(2)}, u32[]{:S(2)}) %collective-permute-start.4) | collective-permute-done | bytes 442400 | tf_op jit(solution)/shard_map/ppermute | solution.py:390
  59.6 1.1 convert_add_fusion
  60.7 0.0 copy-start.13
  60.7 0.0 copy-start.2
  60.8 5.7 %all-to-all-start.2 = ((bf16[4,4,2,16,1024]{4,3,2,1,0:T(8,128)(2,1)}), bf16[4,4,2,16,1024]{4,3,2,1,0:T(8,128)(2,1)S(1)}, u32[]{:S(2)}, u32[]{:S(2)}) async-start(bf16[4,4,2,16,1024]{4,3,2,1,0:T(8,128)(2,1)} %get-tuple-element.35), calls=%async_computation.2 | async-start | bytes 2097152 | tf_op jit(solution)/shard_map/all_to_all | solution.py:397
  66.4 0.0 copy-done.13
  66.4 1.9 %collective-permute-start.6 = (bf16[128,768]{1,0:T(8,128)(2,1)S(1)}, bf16[128,768]{1,0:T(8,128)(2,1)S(1)}, u32[]{:S(2)}, u32[]{:S(2)}) collective-permute-start(bf16[128,768]{1,0:T(8,128)(2,1)S(1)} %copy-done.13), channel_id=1, source_target_pairs={{0,16},{16,0},{32,48},{48,32},{64,80},{80,64},{96,112},{112,96},{1... | collective-permute-start | bytes 589832 | tf_op jit(solution)/shard_map/ppermute | solution.py:390
  68.4 2.8 %collective-permute-start.5 = (bf16[128,576]{1,0:T(8,128)(2,1)S(1)}, bf16[128,576]{1,0:T(8,128)(2,1)S(1)}, u32[]{:S(2)}, u32[]{:S(2)}) collective-permute-start(bf16[128,576]{1,0:T(8,128)(2,1)S(1)} %fusion.4), channel_id=1, source_target_pairs={{32,0},{48,16},{64,32},{80,48},{96,64},{112,80},{128,96},{144,112}... | collective-permute-start | bytes 442376 | tf_op jit(solution)/shard_map/ppermute | solution.py:394
  71.1 0.0 collective-permute-done.6.returned
  71.1 0.0 copy-done.2
  71.2 0.8 shard_map.138
  71.9 10.5 %collective-permute-done.5 = bf16[128,576]{1,0:T(8,128)(2,1)S(1)} collective-permute-done((bf16[128,576]{1,0:T(8,128)(2,1)S(1)}, bf16[128,576]{1,0:T(8,128)(2,1)S(1)}, u32[]{:S(2)}, u32[]{:S(2)}) %collective-permute-start.5) | collective-permute-done | bytes 147488 | tf_op jit(solution)/shard_map/ppermute | solution.py:394
  82.5 1.1 all-to-all-done.2
  83.6 0.9 reduce_sum.12
  84.6 4.5 %all-to-all-start.3 = ((bf16[8,16,1024]{2,1,0:T(8,128)(2,1)}), bf16[8,16,1024]{2,1,0:T(8,128)(2,1)S(1)}, u32[]{:S(2)}, u32[]{:S(2)}) async-start(bf16[8,16,1024]{2,1,0:T(8,128)(2,1)} %bitcast.11), calls=%async_computation.3 | async-start | bytes 524288 | tf_op jit(solution)/shard_map/all_to_all | solution.py:397
  89.1 3.4 %collective-permute-start.7 = (bf16[128,576]{1,0:T(8,128)(2,1)S(1)}, bf16[128,576]{1,0:T(8,128)(2,1)S(1)}, u32[]{:S(2)}, u32[]{:S(2)}) collective-permute-start(bf16[128,576]{1,0:T(8,128)(2,1)S(1)} %fusion.3), channel_id=1, source_target_pairs={{32,0},{48,16},{64,32},{80,48},{96,64},{112,80},{128,96},{144,112}... | collective-permute-start | bytes 442376 | tf_op jit(solution)/shard_map/ppermute | solution.py:394
  92.5 10.3 %collective-permute-done.7 = bf16[128,576]{1,0:T(8,128)(2,1)S(1)} collective-permute-done((bf16[128,576]{1,0:T(8,128)(2,1)S(1)}, bf16[128,576]{1,0:T(8,128)(2,1)S(1)}, u32[]{:S(2)}, u32[]{:S(2)}) %collective-permute-start.7) | collective-permute-done | bytes 147488 | tf_op jit(solution)/shard_map/ppermute | solution.py:394
  102.8 0.7 fusion.1
  103.5 0.0 all-to-all-done.3
  103.5 16.2 %all-to-all-start.4 = ((bf16[16,8,576]{2,1,0:T(8,128)(2,1)}), bf16[16,8,576]{2,1,0:T(8,128)(2,1)S(1)}, u32[]{:S(2)}, u32[]{:S(2)}) async-start(bf16[16,8,576]{2,1,0:T(8,128)(2,1)} %bitcast.13), calls=%async_computation.4 | async-start | bytes 327680 | tf_op jit(solution)/shard_map/all_to_all | solution.py:433
  119.7 0.7 shard_map.140
  120.4 17.5 %all-to-all-done.4.shares = bf16[16,8,576]{2,1,0:T(8,128)(2,1)S(1)} async-done(((bf16[16,8,576]{2,1,0:T(8,128)(2,1)}), bf16[16,8,576]{2,1,0:T(8,128)(2,1)S(1)}, u32[]{:S(2)}, u32[]{:S(2)}) %all-to-all-start.4) | async-done | bytes 147488 | tf_op jit(solution)/shard_map/all_to_all | solution.py:433
  137.9 0.6 shard_map.139
  (11 shorter events, 0.1 us)
Async XLA Ops:
  1.4 0.8 copy-start.9
  3.2 6.0 %copy-start.10 = (bf16[128,64]{0,1:T(8,128)(2,1)S(1)}, bf16[128,64]{0,1:T(8,128)(2,1)}, u32[]{:S(2)}) copy-start(bf16[128,64]{0,1:T(8,128)(2,1)} %param.12) | copy-start | bytes 49156
  3.2 6.2 %copy-start.8 = (bf16[128,512]{1,0:T(8,128)(2,1)S(1)}, bf16[128,512]{1,0:T(8,128)(2,1)}, u32[]{:S(2)}) copy-start(bf16[128,512]{1,0:T(8,128)(2,1)} %param.11) | copy-start | bytes 393220
  3.2 22.1 %all-to-all-start = ((bf16[8,16,1024]{2,1,0:T(8,128)(2,1)}), bf16[8,16,1024]{2,1,0:T(8,128)(2,1)S(1)}, u32[]{:S(2)}, u32[]{:S(2)}) async-start(bf16[8,16,1024]{2,1,0:T(8,128)(2,1)} %bitcast.4), calls=%async_computation | async-start | bytes 524288 | tf_op jit(solution)/shard_map/all_to_all | solution.py:397
  9.4 10.9 %collective-permute-start.2 = (bf16[128,576]{1,0:T(8,128)(2,1)S(1)}, bf16[128,576]{1,0:T(8,128)(2,1)S(1)}, u32[]{:S(2)}, u32[]{:S(2)}) collective-permute-start(bf16[128,576]{1,0:T(8,128)(2,1)S(1)} %get-tuple-element.50), channel_id=1, source_target_pairs={{0,32},{16,48},{32,64},{48,80},{64,96},{80,112},{96,128},{112,144}... | collective-permute-start | bytes 442376 | tf_op jit(solution)/shard_map/ppermute | solution.py:394
  15.8 9.4 %collective-permute-start.1 = (bf16[128,576]{1,0:T(8,128)(2,1)S(1)}, bf16[128,576]{1,0:T(8,128)(2,1)S(1)}, u32[]{:S(2)}, u32[]{:S(2)}) collective-permute-start(bf16[128,576]{1,0:T(8,128)(2,1)S(1)} %get-tuple-element.50), channel_id=1, source_target_pairs={{0,64},{16,80},{32,96},{48,112},{64,128},{80,144},{96,160},{112,17... | collective-permute-start | bytes 442376 | tf_op jit(solution)/shard_map/ppermute | solution.py:394
  25.2 5.8 %copy-start.7 = (bf16[3,128,576]{2,1,0:T(8,128)(2,1)}, bf16[3,128,576]{2,1,0:T(8,128)(2,1)S(1)}, u32[]{:S(2)}) copy-start(bf16[3,128,576]{2,1,0:T(8,128)(2,1)S(1)} %pad_maximum_fusion.keys_near) | copy-start | bytes 1327108
  26.4 6.6 %copy-start = (bf16[128,1024]{1,0:T(8,128)(2,1)S(1)}, bf16[128,1024]{1,0:T(8,128)(2,1)}, u32[]{:S(2)}) copy-start(bf16[128,1024]{1,0:T(8,128)(2,1)} %queries.1) | copy-start | bytes 786436
  26.4 6.6 %copy-start.1 = (bf16[128,1024]{1,0:T(8,128)(2,1)S(1)}, bf16[128,1024]{1,0:T(8,128)(2,1)}, u32[]{:S(2)}) copy-start(bf16[128,1024]{1,0:T(8,128)(2,1)} %cotangent.1) | copy-start | bytes 786436
  26.4 6.6 %copy-start.3 = (bf16[128,512]{1,0:T(8,128)(2,1)S(1)}, bf16[128,512]{1,0:T(8,128)(2,1)}, u32[]{:S(2)}) copy-start(bf16[128,512]{1,0:T(8,128)(2,1)} %rotated.1) | copy-start | bytes 393220
  26.4 16.8 %all-to-all-start.1 = ((bf16[4,8,16,1024]{3,2,1,0:T(8,128)(2,1)}), bf16[4,8,16,1024]{3,2,1,0:T(8,128)(2,1)S(1)}, u32[]{:S(2)}, u32[]{:S(2)}) async-start(bf16[4,8,16,1024]{3,2,1,0:T(8,128)(2,1)} %broadcast_in_dim.5), calls=%async_computation.1 | async-start | bytes 2097152 | tf_op jit(solution)/shard_map/all_to_all | solution.py:397
  31.0 7.1 %collective-permute-start.3 = (bf16[3,128,576]{2,1,0:T(8,128)(2,1)S(1)}, bf16[3,128,576]{2,1,0:T(8,128)(2,1)S(1)}, u32[]{:S(2)}, u32[]{:S(2)}) collective-permute-start(bf16[3,128,576]{2,1,0:T(8,128)(2,1)S(1)} %pad_maximum_fusion.keys_near), channel_id=1, source_target_pairs={{0,16},{16,0},{32,48},{48,32},{64,80},{80,64},{96,112},{112,96},{1... | collective-permute-start | bytes 1327112 | tf_op jit(solution)/shard_map/ppermute | solution.py:390
  33.0 0.7 copy-start.4
  33.8 0.7 copy-start.5
  34.5 3.6 %collective-permute-start = (bf16[128,1280]{1,0:T(8,128)(2,1)S(1)}, bf16[128,1280]{1,0:T(8,128)(2,1)S(1)}, u32[]{:S(2)}, u32[]{:S(2)}) collective-permute-start(bf16[128,1280]{1,0:T(8,128)(2,1)S(1)} %get-tuple-element.29), channel_id=1, source_target_pairs={{0,16},{16,0},{32,48},{48,32},{64,80},{80,64},{96,112},{112,96},{1... | collective-permute-start | bytes 983048 | tf_op jit(solution)/shard_map/ppermute | solution.py:390
  38.2 5.1 %copy-start.12 = (bf16[128,1280]{1,0:T(8,128)(2,1)}, bf16[128,1280]{1,0:T(8,128)(2,1)S(1)}, u32[]{:S(2)}) copy-start(bf16[128,1280]{1,0:T(8,128)(2,1)S(1)} %collective-permute-done.rows_lent) | copy-start | bytes 983044
  38.2 5.1 %copy-start.11 = (bf16[3,128,576]{2,1,0:T(8,128)(2,1)}, bf16[3,128,576]{2,1,0:T(8,128)(2,1)S(1)}, u32[]{:S(2)}) copy-start(bf16[3,128,576]{2,1,0:T(8,128)(2,1)S(1)} %collective-permute-done.3.keys_far) | copy-start | bytes 1327108
  43.2 1.0 copy-start.6
  55.6 4.0 %collective-permute-start.4 = (bf16[3,128,576]{2,1,0:T(8,128)(2,1)}, bf16[3,128,576]{2,1,0:T(8,128)(2,1)S(1)}, u32[]{:S(2)}, u32[]{:S(2)}) collective-permute-start(bf16[3,128,576]{2,1,0:T(8,128)(2,1)} %get-tuple-element.34), channel_id=1, source_target_pairs={{0,16},{16,0},{32,48},{48,32},{64,80},{80,64},{96,112},{112,96},{1... | collective-permute-start | bytes 1327112 | tf_op jit(solution)/shard_map/ppermute | solution.py:390
  60.7 5.7 %copy-start.13 = (bf16[128,768]{1,0:T(8,128)(2,1)S(1)}, bf16[128,768]{1,0:T(8,128)(2,1)}, u32[]{:S(2)}) copy-start(bf16[128,768]{1,0:T(8,128)(2,1)} %get-tuple-element.38) | copy-start | bytes 589828
  60.7 10.4 %copy-start.2 = (bf16[128,768]{1,0:T(8,128)(2,1)S(1)}, bf16[128,768]{1,0:T(8,128)(2,1)}, u32[]{:S(2)}) copy-start(bf16[128,768]{1,0:T(8,128)(2,1)} %get-tuple-element.37.kept) | copy-start | bytes 589828
  60.8 22.9 %all-to-all-start.2 = ((bf16[4,4,2,16,1024]{4,3,2,1,0:T(8,128)(2,1)}), bf16[4,4,2,16,1024]{4,3,2,1,0:T(8,128)(2,1)S(1)}, u32[]{:S(2)}, u32[]{:S(2)}) async-start(bf16[4,4,2,16,1024]{4,3,2,1,0:T(8,128)(2,1)} %get-tuple-element.35), calls=%async_computation.2 | async-start | bytes 2097152 | tf_op jit(solution)/shard_map/all_to_all | solution.py:397
  66.4 4.7 %collective-permute-start.6 = (bf16[128,768]{1,0:T(8,128)(2,1)S(1)}, bf16[128,768]{1,0:T(8,128)(2,1)S(1)}, u32[]{:S(2)}, u32[]{:S(2)}) collective-permute-start(bf16[128,768]{1,0:T(8,128)(2,1)S(1)} %copy-done.13), channel_id=1, source_target_pairs={{0,16},{16,0},{32,48},{48,32},{64,80},{80,64},{96,112},{112,96},{1... | collective-permute-start | bytes 589832 | tf_op jit(solution)/shard_map/ppermute | solution.py:390
  68.4 14.1 %collective-permute-start.5 = (bf16[128,576]{1,0:T(8,128)(2,1)S(1)}, bf16[128,576]{1,0:T(8,128)(2,1)S(1)}, u32[]{:S(2)}, u32[]{:S(2)}) collective-permute-start(bf16[128,576]{1,0:T(8,128)(2,1)S(1)} %fusion.4), channel_id=1, source_target_pairs={{32,0},{48,16},{64,32},{80,48},{96,64},{112,80},{128,96},{144,112}... | collective-permute-start | bytes 442376 | tf_op jit(solution)/shard_map/ppermute | solution.py:394
  84.6 18.9 %all-to-all-start.3 = ((bf16[8,16,1024]{2,1,0:T(8,128)(2,1)}), bf16[8,16,1024]{2,1,0:T(8,128)(2,1)S(1)}, u32[]{:S(2)}, u32[]{:S(2)}) async-start(bf16[8,16,1024]{2,1,0:T(8,128)(2,1)} %bitcast.11), calls=%async_computation.3 | async-start | bytes 524288 | tf_op jit(solution)/shard_map/all_to_all | solution.py:397
  89.1 13.7 %collective-permute-start.7 = (bf16[128,576]{1,0:T(8,128)(2,1)S(1)}, bf16[128,576]{1,0:T(8,128)(2,1)S(1)}, u32[]{:S(2)}, u32[]{:S(2)}) collective-permute-start(bf16[128,576]{1,0:T(8,128)(2,1)S(1)} %fusion.3), channel_id=1, source_target_pairs={{32,0},{48,16},{64,32},{80,48},{96,64},{112,80},{128,96},{144,112}... | collective-permute-start | bytes 442376 | tf_op jit(solution)/shard_map/ppermute | solution.py:394
  103.5 34.4 %all-to-all-start.4 = ((bf16[16,8,576]{2,1,0:T(8,128)(2,1)}), bf16[16,8,576]{2,1,0:T(8,128)(2,1)S(1)}, u32[]{:S(2)}, u32[]{:S(2)}) async-start(bf16[16,8,576]{2,1,0:T(8,128)(2,1)} %bitcast.13), calls=%async_computation.4 | async-start | bytes 327680 | tf_op jit(solution)/shard_map/all_to_all | solution.py:433

commit v4 on v3

--- a/solution.py
+++ b/solution.py
@@ -339,6 +339,31 @@
     )(place, kept, returned)
 
 
+def slot_kernel(left, right, out, sems):
+    half = left.shape[1] // 2
+    copies = []
+    for slot in range(out.shape[0]):
+        here = pl.ds(slot % 2 * half, half)
+        for at, part in enumerate((left, right)):
+            target = out.at[slot, :, pl.ds(at * half, half)]
+            copies.append(pltpu.make_async_copy(part.at[:, here], target, sems.at[slot, at]))
+            copies[-1].start()
+    for copy in copies:
+        copy.wait()
+
+
+def slots(left, right, count):
+    return pl.pallas_call(
+        slot_kernel,
+        out_shape=jax.ShapeDtypeStruct((count,) + left.shape, left.dtype),
+        in_specs=[APART, APART],
+        out_specs=WHOLE,
+        scratch_shapes=[pltpu.SemaphoreType.DMA((count, 2))],
+        compiler_params=pltpu.CompilerParams(vmem_limit_bytes=56 * MIB),
+        cost_estimate=cost(100_000, 300_000),
+    )(left, right)
+
+
 def key_sum_kernel(shares, left, right):
     total = jnp.sum(shares[...].astype(jnp.float32), axis=0)
     left[...] = total[:, : left.shape[1]]
@@ -367,7 +392,6 @@
 def on_device(q_nope, q_rope, latent, k_rope, d_out, advantage, segment, w_uk, w_uv):
     rows, width = q_nope.shape
     piece = w_uk.shape[0]
-    half = width // 2
     count = lax.axis_size("ctx")
     ring = 4
     steps = count // (2 * ring)
@@ -396,10 +420,7 @@
     def exchanged(value, groups):
         return lax.all_to_all(value, "ctx", 0, 0, axis_index_groups=groups, tiled=True)
 
-    up = jnp.stack([w_uk.reshape(piece, 2, half), w_uv.reshape(piece, 2, half)], axis=2)
-    up = up.reshape(piece, 2, width).transpose(1, 0, 2)
-    up = jnp.broadcast_to(up[None], (steps, 2, piece, width)).reshape(2 * steps, piece, width)
-    column = exchanged(up, along_z)
+    column = exchanged(slots(w_uk, w_uv, 2 * steps), along_z)
     keys = jnp.concatenate([latent, k_rope], axis=1)
     near = jnp.stack([to_chip(keys, 2), to_chip(keys, 1), keys])
     column, near = lax.optimization_barrier((column, near))
@@ -416,16 +437,15 @@
     got = swapped(grad_given)
     sums = grad_kept.astype(jnp.float32) + got.astype(jnp.float32)
     far_sum = sums[0].astype(jnp.bfloat16)
-    d_weights, far_sum = lax.optimization_barrier((d_weights, far_sum))
     shares = exchanged(d_weights, along_y)
     near_sum = (sums[1] + to_chip(far_sum, -1).astype(jnp.float32)).astype(jnp.bfloat16)
-    returned = swapped(d_lent)
-    d_q_nope, d_q_rope = join_heads(place, d_kept, returned, width, q_rope.shape[1])
-    shares, near_sum, d_q_nope = lax.optimization_barrier((shares, near_sum, d_q_nope))
+    shares, near_sum = lax.optimization_barrier((shares, near_sum))
     d_column = jnp.sum(shares.astype(jnp.float32), axis=0).astype(jnp.bfloat16)
     d_shares = exchanged(d_column.reshape(2 * steps, piece, width), along_z)
     total = (sums[2] + to_chip(near_sum, -1).astype(jnp.float32)).astype(jnp.bfloat16)
-    d_shares, total = lax.optimization_barrier((d_shares, total))
+    returned = swapped(d_lent)
+    d_q_nope, d_q_rope = join_heads(place, d_kept, returned, width, q_rope.shape[1])
+    d_shares, total, d_q_nope = lax.optimization_barrier((d_shares, total, d_q_nope))
     d_uk, d_uv = summed(
         up_sum_kernel, d_shares.reshape(steps, 2, piece, width), piece, (width, width)
     )

time: 140 us -> 136 us (0.971)
  waiting for transfers between devices: 55.2 us -> 52.3 us
  local copies, waits for them, and re-layouts: 5.97 us -> 3.62 us
  Pallas kernels: 13.6 us -> 15.4 us
  starting transfers between devices: 59.7 us -> 61.4 us
    ppermute x4, waiting for transfers between devices: 3.28 us -> 1.24 us  [swapped(): lax.ppermute(value, 'ctx', [(source, source ^ 1) for source in range(coun...]
    pallas_call x0 -> x1, Pallas kernels: none -> 1.79 us  [slots(): pl.pallas_call(slot_kernel, out_shape=jax.ShapeDtypeStruct((count,) + lef...]
  transfers between devices with their start and end apart: 13 -> 13, of which waited for: 9 -> 8; matrix products, arithmetic and copies ran while one was open for 1% -> 1% of each run, Pallas kernels for 1% -> 1%
where the time goes in v4:
time: 136 us
  starting transfers between devices  61.4 us (45%)
  waiting for transfers between devices  52.3 us (38%)
  Pallas kernels  15.4 us (11%)
  local copies, waits for them, and re-layouts  3.62 us (3%)
  other arithmetic  1.88 us (1%)
    ppermute x4, waiting for transfers between devices, to_chip(): lax.ppermute(value, 'ctx', [pair for pair in pairs if 0 <= pair[1] < count])  27.9 us
    all_to_all x4, starting transfers between devices, exchanged(): lax.all_to_all(value, 'ctx', 0, 0, axis_index_groups=groups, tiled=True)  21.1 us
    all_to_all x1, waiting for transfers between devices, on_device(): key_terms = lax.all_to_all(total, 'head', 0, 0, tiled=True)  17.3 us
    all_to_all x1, starting transfers between devices, on_device(): key_terms = lax.all_to_all(total, 'head', 0, 0, tiled=True)  16.2 us
    ppermute x4, starting transfers between devices, to_chip(): lax.ppermute(value, 'ctx', [pair for pair in pairs if 0 <= pair[1] < count])  15.5 us
    pallas_call x1, Pallas kernels, layer(): pl.pallas_call(layer_kernel, out_shape=(jax.ShapeDtypeStruct((rows, d_pac...  11.4 us
    ppermute x4, starting transfers between devices, swapped(): lax.ppermute(value, 'ctx', [(source, source ^ 1) for source in range(coun...  8.62 us
    all_to_all x4, waiting for transfers between devices, exchanged(): lax.all_to_all(value, 'ctx', 0, 0, axis_index_groups=groups, tiled=True)  5.93 us
  transfers between devices with their start and end apart: 13, of which 8 were waited for; matrix products, arithmetic and copies ran while one was open for 1% of the time, Pallas kernels for 1%

profile of v4, /device:TPU:24, one launch (start us, length us, event | category | flops | bytes accessed | tf_op | source)
XLA Modules:
  0.0 135.5 jit_solution(17971068257652177760)
XLA Ops:
  0.6 1.8 %shard_map.137 = bf16[8,16,1024]{2,1,0:T(8,128)(2,1)} custom-call(bf16[16,1024]{1,0:T(8,128)(2,1)} %left.1, bf16[16,1024]{1,0:T(8,128)(2,1)} %right.1), custom_call_target="tpu_custom_call" | custom-call | flops 100000 | bytes 300000 | tf_op jit(solution)/shard_map/pallas_call | solution.py:356
  2.4 0.0 copy-start.10
  2.4 0.0 copy-start.9
  2.5 6.0 %all-to-all-start = ((bf16[8,16,1024]{2,1,0:T(8,128)(2,1)}), bf16[8,16,1024]{2,1,0:T(8,128)(2,1)S(1)}, u32[]{:S(2)}, u32[]{:S(2)}) async-start(bf16[8,16,1024]{2,1,0:T(8,128)(2,1)} %shard_map.137), calls=%async_computation | async-start | bytes 524288 | tf_op jit(solution)/shard_map/all_to_all | solution.py:421
  8.5 0.0 copy-done.10
  8.5 0.1 copy.15
  8.6 0.0 copy-done.9
  8.7 6.4 %collective-permute-start.2 = (bf16[128,576]{1,0:T(8,128)(2,1)S(1)}, bf16[128,576]{1,0:T(8,128)(2,1)S(1)}, u32[]{:S(2)}, u32[]{:S(2)}) collective-permute-start(bf16[128,576]{1,0:T(8,128)(2,1)S(1)} %get-tuple-element.46), channel_id=1, source_target_pairs={{0,32},{16,48},{32,64},{48,80},{64,96},{80,112},{96,128},{112,144}... | collective-permute-start | bytes 442376 | tf_op jit(solution)/shard_map/ppermute | solution.py:418
  15.1 1.9 %collective-permute-start.1 = (bf16[128,576]{1,0:T(8,128)(2,1)S(1)}, bf16[128,576]{1,0:T(8,128)(2,1)S(1)}, u32[]{:S(2)}, u32[]{:S(2)}) collective-permute-start(bf16[128,576]{1,0:T(8,128)(2,1)S(1)} %get-tuple-element.46), channel_id=1, source_target_pairs={{0,64},{16,80},{32,96},{48,112},{64,128},{80,144},{96,160},{112,17... | collective-permute-start | bytes 442376 | tf_op jit(solution)/shard_map/ppermute | solution.py:418
  17.0 2.6 %collective-permute-done.2 = bf16[128,576]{1,0:T(8,128)(2,1)S(1)} collective-permute-done((bf16[128,576]{1,0:T(8,128)(2,1)S(1)}, bf16[128,576]{1,0:T(8,128)(2,1)S(1)}, u32[]{:S(2)}, u32[]{:S(2)}) %collective-permute-start.2) | collective-permute-done | bytes 147488 | tf_op jit(solution)/shard_map/ppermute | solution.py:418
  19.6 4.8 %collective-permute-done.1 = bf16[128,576]{1,0:T(8,128)(2,1)S(1)} collective-permute-done((bf16[128,576]{1,0:T(8,128)(2,1)S(1)}, bf16[128,576]{1,0:T(8,128)(2,1)S(1)}, u32[]{:S(2)}, u32[]{:S(2)}) %collective-permute-start.1) | collective-permute-done | bytes 147488 | tf_op jit(solution)/shard_map/ppermute | solution.py:418
  24.4 0.1 pad_maximum_fusion.keys_near
  24.5 0.0 copy-start.7
  24.5 0.0 all-to-all-done
  24.5 1.1 broadcast_in_dim.2
  25.7 0.0 copy-start
  25.7 0.0 copy-start.1
  25.7 4.6 %all-to-all-start.1 = ((bf16[4,8,16,1024]{3,2,1,0:T(8,128)(2,1)}), bf16[4,8,16,1024]{3,2,1,0:T(8,128)(2,1)S(1)}, u32[]{:S(2)}, u32[]{:S(2)}) async-start(bf16[4,8,16,1024]{3,2,1,0:T(8,128)(2,1)} %broadcast_in_dim.2), calls=%async_computation.1 | async-start | bytes 2097152 | tf_op jit(solution)/shard_map/all_to_all | solution.py:421
  30.3 0.0 copy-done.7
  30.3 1.9 %collective-permute-start.3 = (bf16[3,128,576]{2,1,0:T(8,128)(2,1)S(1)}, bf16[3,128,576]{2,1,0:T(8,128)(2,1)S(1)}, u32[]{:S(2)}, u32[]{:S(2)}) collective-permute-start(bf16[3,128,576]{2,1,0:T(8,128)(2,1)S(1)} %pad_maximum_fusion.keys_near), channel_id=1, source_target_pairs={{0,16},{16,0},{32,48},{48,32},{64,80},{80,64},{96,112},{112,96},{1... | collective-permute-start | bytes 1327112 | tf_op jit(solution)/shard_map/ppermute | solution.py:414
  32.2 0.0 copy-start.4
  32.2 0.0 copy-done
  32.3 0.0 copy-done.1
  32.3 0.0 copy-done.3
  32.3 0.6 copy-done.4
  32.9 0.2 shard_map.136
  33.1 0.0 copy-start.5
  33.1 0.7 copy-done.5
  33.8 2.4 %collective-permute-start = (bf16[128,1280]{1,0:T(8,128)(2,1)S(1)}, bf16[128,1280]{1,0:T(8,128)(2,1)S(1)}, u32[]{:S(2)}, u32[]{:S(2)}) collective-permute-start(bf16[128,1280]{1,0:T(8,128)(2,1)S(1)} %get-tuple-element.27), channel_id=1, source_target_pairs={{0,16},{16,0},{32,48},{48,32},{64,80},{80,64},{96,112},{112,96},{1... | collective-permute-start | bytes 983048 | tf_op jit(solution)/shard_map/ppermute | solution.py:414
  36.2 1.2 collective-permute-done.rows_lent
  37.4 0.0 collective-permute-done.3.keys_far
  37.4 0.0 copy-start.11
  37.4 5.1 %all-to-all-done.1 = bf16[4,8,16,1024]{3,2,1,0:T(8,128)(2,1)S(1)} async-done(((bf16[4,8,16,1024]{3,2,1,0:T(8,128)(2,1)}), bf16[4,8,16,1024]{3,2,1,0:T(8,128)(2,1)S(1)}, u32[]{:S(2)}, u32[]{:S(2)}) %all-to-all-start.1) | async-done | bytes 1048608 | tf_op jit(solution)/shard_map/all_to_all | solution.py:421
  42.5 0.0 copy-start.6
  42.5 0.0 copy-done.12
  42.5 0.0 copy-done.11
  42.5 1.0 copy-done.6
  43.5 11.4 %shard_map.138 = (bf16[128,768]{1,0:T(8,128)(2,1)}, bf16[128,768]{1,0:T(8,128)(2,1)}, bf16[3,128,576]{2,1,0:T(8,128)(2,1)}, bf16[3,128,576]{2,1,0:T(8,128)(2,1)}, bf16[4,4,2,16,1024]{4,3,2,1,0:T(8,128)(2,1)}) custom-call(s32[1]{0:T(128)} %bitcast.place, s32[32,128]{1,0:T(8,128)} %bitcast.30, bf16[128,1280]{1,0:T(8,128)(2,1)} %copy-done.5, ...), custom_call_target="tpu_custom_call" | custom-call | flops 5000000000 | bytes 8000000 | tf_op jit(solution)/shard_map/pallas_call | solution.py:282
  54.9 1.9 %collective-permute-start.4 = (bf16[3,128,576]{2,1,0:T(8,128)(2,1)}, bf16[3,128,576]{2,1,0:T(8,128)(2,1)S(1)}, u32[]{:S(2)}, u32[]{:S(2)}) collective-permute-start(bf16[3,128,576]{2,1,0:T(8,128)(2,1)} %get-tuple-element.32), channel_id=1, source_target_pairs={{0,16},{16,0},{32,48},{48,32},{64,80},{80,64},{96,112},{112,96},{1... | collective-permute-start | bytes 1327112 | tf_op jit(solution)/shard_map/ppermute | solution.py:414
  56.8 0.0 copy-start.8
  56.8 5.7 %all-to-all-start.2 = ((bf16[4,4,2,16,1024]{4,3,2,1,0:T(8,128)(2,1)}), bf16[4,4,2,16,1024]{4,3,2,1,0:T(8,128)(2,1)S(1)}, u32[]{:S(2)}, u32[]{:S(2)}) async-start(bf16[4,4,2,16,1024]{4,3,2,1,0:T(8,128)(2,1)} %get-tuple-element.30), calls=%async_computation.2 | async-start | bytes 2097152 | tf_op jit(solution)/shard_map/all_to_all | solution.py:421
  62.5 0.0 collective-permute-done.4
  62.5 0.0 copy-done.8
  62.5 0.1 convert_add_fusion
  62.7 2.8 %collective-permute-start.5 = (bf16[128,576]{1,0:T(8,128)(2,1)S(1)}, bf16[128,576]{1,0:T(8,128)(2,1)S(1)}, u32[]{:S(2)}, u32[]{:S(2)}) collective-permute-start(bf16[128,576]{1,0:T(8,128)(2,1)S(1)} %fusion.4), channel_id=1, source_target_pairs={{32,0},{48,16},{64,32},{80,48},{96,64},{112,80},{128,96},{144,112}... | collective-permute-start | bytes 442376 | tf_op jit(solution)/shard_map/ppermute | solution.py:418
  65.4 12.7 %collective-permute-done.5 = bf16[128,576]{1,0:T(8,128)(2,1)S(1)} collective-permute-done((bf16[128,576]{1,0:T(8,128)(2,1)S(1)}, bf16[128,576]{1,0:T(8,128)(2,1)S(1)}, u32[]{:S(2)}, u32[]{:S(2)}) %collective-permute-start.5) | collective-permute-done | bytes 147488 | tf_op jit(solution)/shard_map/ppermute | solution.py:418
  78.2 0.9 all-to-all-done.2
  79.0 0.9 reduce_sum.12
  80.0 0.0 copy-start.13
  80.0 0.0 copy-start.2
  80.0 4.7 %all-to-all-start.3 = ((bf16[8,16,1024]{2,1,0:T(8,128)(2,1)}), bf16[8,16,1024]{2,1,0:T(8,128)(2,1)S(1)}, u32[]{:S(2)}, u32[]{:S(2)}) async-start(bf16[8,16,1024]{2,1,0:T(8,128)(2,1)} %bitcast.9), calls=%async_computation.3 | async-start | bytes 524288 | tf_op jit(solution)/shard_map/all_to_all | solution.py:421
  84.7 0.0 copy-done.13
  84.7 2.4 %collective-permute-start.7 = (bf16[128,768]{1,0:T(8,128)(2,1)S(1)}, bf16[128,768]{1,0:T(8,128)(2,1)S(1)}, u32[]{:S(2)}, u32[]{:S(2)}) collective-permute-start(bf16[128,768]{1,0:T(8,128)(2,1)S(1)} %copy-done.13), channel_id=1, source_target_pairs={{0,16},{16,0},{32,48},{48,32},{64,80},{80,64},{96,112},{112,96},{1... | collective-permute-start | bytes 589832 | tf_op jit(solution)/shard_map/ppermute | solution.py:414
  87.1 4.4 %collective-permute-start.6 = (bf16[128,576]{1,0:T(8,128)(2,1)S(1)}, bf16[128,576]{1,0:T(8,128)(2,1)S(1)}, u32[]{:S(2)}, u32[]{:S(2)}) collective-permute-start(bf16[128,576]{1,0:T(8,128)(2,1)S(1)} %fusion.3), channel_id=1, source_target_pairs={{32,0},{48,16},{64,32},{80,48},{96,64},{112,80},{128,96},{144,112}... | collective-permute-start | bytes 442376 | tf_op jit(solution)/shard_map/ppermute | solution.py:418
  91.5 0.0 collective-permute-done.7.returned
  91.5 0.0 copy-done.2
  91.5 0.8 shard_map.139
  92.3 7.7 %collective-permute-done.6 = bf16[128,576]{1,0:T(8,128)(2,1)S(1)} collective-permute-done((bf16[128,576]{1,0:T(8,128)(2,1)S(1)}, bf16[128,576]{1,0:T(8,128)(2,1)S(1)}, u32[]{:S(2)}, u32[]{:S(2)}) %collective-permute-start.6) | collective-permute-done | bytes 147488 | tf_op jit(solution)/shard_map/ppermute | solution.py:418
  100.0 0.7 fusion.1
  100.7 0.0 all-to-all-done.3
  100.7 16.2 %all-to-all-start.4 = ((bf16[16,8,576]{2,1,0:T(8,128)(2,1)}), bf16[16,8,576]{2,1,0:T(8,128)(2,1)S(1)}, u32[]{:S(2)}, u32[]{:S(2)}) async-start(bf16[16,8,576]{2,1,0:T(8,128)(2,1)} %bitcast.11), calls=%async_computation.4 | async-start | bytes 327680 | tf_op jit(solution)/shard_map/all_to_all | solution.py:453
  116.9 0.7 shard_map.141
  117.6 17.3 %all-to-all-done.4.shares = bf16[16,8,576]{2,1,0:T(8,128)(2,1)S(1)} async-done(((bf16[16,8,576]{2,1,0:T(8,128)(2,1)}), bf16[16,8,576]{2,1,0:T(8,128)(2,1)S(1)}, u32[]{:S(2)}, u32[]{:S(2)}) %all-to-all-start.4) | async-done | bytes 147488 | tf_op jit(solution)/shard_map/all_to_all | solution.py:453
  134.9 0.6 shard_map.140
  (5 shorter events, 0.1 us)
Async XLA Ops:
  2.4 6.1 %copy-start.10 = (bf16[128,64]{0,1:T(8,128)(2,1)S(1)}, bf16[128,64]{0,1:T(8,128)(2,1)}, u32[]{:S(2)}) copy-start(bf16[128,64]{0,1:T(8,128)(2,1)} %param.12) | copy-start | bytes 49156
  2.4 6.2 %copy-start.9 = (bf16[128,512]{1,0:T(8,128)(2,1)S(1)}, bf16[128,512]{1,0:T(8,128)(2,1)}, u32[]{:S(2)}) copy-start(bf16[128,512]{1,0:T(8,128)(2,1)} %param.11) | copy-start | bytes 393220
  2.5 22.1 %all-to-all-start = ((bf16[8,16,1024]{2,1,0:T(8,128)(2,1)}), bf16[8,16,1024]{2,1,0:T(8,128)(2,1)S(1)}, u32[]{:S(2)}, u32[]{:S(2)}) async-start(bf16[8,16,1024]{2,1,0:T(8,128)(2,1)} %shard_map.137), calls=%async_computation | async-start | bytes 524288 | tf_op jit(solution)/shard_map/all_to_all | solution.py:421
  8.7 10.9 %collective-permute-start.2 = (bf16[128,576]{1,0:T(8,128)(2,1)S(1)}, bf16[128,576]{1,0:T(8,128)(2,1)S(1)}, u32[]{:S(2)}, u32[]{:S(2)}) collective-permute-start(bf16[128,576]{1,0:T(8,128)(2,1)S(1)} %get-tuple-element.46), channel_id=1, source_target_pairs={{0,32},{16,48},{32,64},{48,80},{64,96},{80,112},{96,128},{112,144}... | collective-permute-start | bytes 442376 | tf_op jit(solution)/shard_map/ppermute | solution.py:418
  15.1 9.4 %collective-permute-start.1 = (bf16[128,576]{1,0:T(8,128)(2,1)S(1)}, bf16[128,576]{1,0:T(8,128)(2,1)S(1)}, u32[]{:S(2)}, u32[]{:S(2)}) collective-permute-start(bf16[128,576]{1,0:T(8,128)(2,1)S(1)} %get-tuple-element.46), channel_id=1, source_target_pairs={{0,64},{16,80},{32,96},{48,112},{64,128},{80,144},{96,160},{112,17... | collective-permute-start | bytes 442376 | tf_op jit(solution)/shard_map/ppermute | solution.py:418
  24.5 5.8 %copy-start.7 = (bf16[3,128,576]{2,1,0:T(8,128)(2,1)}, bf16[3,128,576]{2,1,0:T(8,128)(2,1)S(1)}, u32[]{:S(2)}) copy-start(bf16[3,128,576]{2,1,0:T(8,128)(2,1)S(1)} %pad_maximum_fusion.keys_near) | copy-start | bytes 1327108
  25.7 6.6 %copy-start = (bf16[128,1024]{1,0:T(8,128)(2,1)S(1)}, bf16[128,1024]{1,0:T(8,128)(2,1)}, u32[]{:S(2)}) copy-start(bf16[128,1024]{1,0:T(8,128)(2,1)} %queries.1) | copy-start | bytes 786436
  25.7 6.6 %copy-start.1 = (bf16[128,1024]{1,0:T(8,128)(2,1)S(1)}, bf16[128,1024]{1,0:T(8,128)(2,1)}, u32[]{:S(2)}) copy-start(bf16[128,1024]{1,0:T(8,128)(2,1)} %cotangent.1) | copy-start | bytes 786436
  25.7 6.6 %copy-start.3 = (bf16[128,512]{1,0:T(8,128)(2,1)S(1)}, bf16[128,512]{1,0:T(8,128)(2,1)}, u32[]{:S(2)}) copy-start(bf16[128,512]{1,0:T(8,128)(2,1)} %rotated.1) | copy-start | bytes 393220
  25.7 16.8 %all-to-all-start.1 = ((bf16[4,8,16,1024]{3,2,1,0:T(8,128)(2,1)}), bf16[4,8,16,1024]{3,2,1,0:T(8,128)(2,1)S(1)}, u32[]{:S(2)}, u32[]{:S(2)}) async-start(bf16[4,8,16,1024]{3,2,1,0:T(8,128)(2,1)} %broadcast_in_dim.2), calls=%async_computation.1 | async-start | bytes 2097152 | tf_op jit(solution)/shard_map/all_to_all | solution.py:421
  30.3 7.1 %collective-permute-start.3 = (bf16[3,128,576]{2,1,0:T(8,128)(2,1)S(1)}, bf16[3,128,576]{2,1,0:T(8,128)(2,1)S(1)}, u32[]{:S(2)}, u32[]{:S(2)}) collective-permute-start(bf16[3,128,576]{2,1,0:T(8,128)(2,1)S(1)} %pad_maximum_fusion.keys_near), channel_id=1, source_target_pairs={{0,16},{16,0},{32,48},{48,32},{64,80},{80,64},{96,112},{112,96},{1... | collective-permute-start | bytes 1327112 | tf_op jit(solution)/shard_map/ppermute | solution.py:414
  32.2 0.7 copy-start.4
  33.1 0.7 copy-start.5
  33.8 3.6 %collective-permute-start = (bf16[128,1280]{1,0:T(8,128)(2,1)S(1)}, bf16[128,1280]{1,0:T(8,128)(2,1)S(1)}, u32[]{:S(2)}, u32[]{:S(2)}) collective-permute-start(bf16[128,1280]{1,0:T(8,128)(2,1)S(1)} %get-tuple-element.27), channel_id=1, source_target_pairs={{0,16},{16,0},{32,48},{48,32},{64,80},{80,64},{96,112},{112,96},{1... | collective-permute-start | bytes 983048 | tf_op jit(solution)/shard_map/ppermute | solution.py:414
  37.4 5.1 %copy-start.12 = (bf16[128,1280]{1,0:T(8,128)(2,1)}, bf16[128,1280]{1,0:T(8,128)(2,1)S(1)}, u32[]{:S(2)}) copy-start(bf16[128,1280]{1,0:T(8,128)(2,1)S(1)} %collective-permute-done.rows_lent) | copy-start | bytes 983044
  37.4 5.1 %copy-start.11 = (bf16[3,128,576]{2,1,0:T(8,128)(2,1)}, bf16[3,128,576]{2,1,0:T(8,128)(2,1)S(1)}, u32[]{:S(2)}) copy-start(bf16[3,128,576]{2,1,0:T(8,128)(2,1)S(1)} %collective-permute-done.3.keys_far) | copy-start | bytes 1327108
  42.5 1.0 copy-start.6
  54.9 7.6 %collective-permute-start.4 = (bf16[3,128,576]{2,1,0:T(8,128)(2,1)}, bf16[3,128,576]{2,1,0:T(8,128)(2,1)S(1)}, u32[]{:S(2)}, u32[]{:S(2)}) collective-permute-start(bf16[3,128,576]{2,1,0:T(8,128)(2,1)} %get-tuple-element.32), channel_id=1, source_target_pairs={{0,16},{16,0},{32,48},{48,32},{64,80},{80,64},{96,112},{112,96},{1... | collective-permute-start | bytes 1327112 | tf_op jit(solution)/shard_map/ppermute | solution.py:414
  56.8 5.7 %copy-start.8 = (bf16[3,128,576]{2,1,0:T(8,128)(2,1)S(1)}, bf16[3,128,576]{2,1,0:T(8,128)(2,1)}, u32[]{:S(2)}) copy-start(bf16[3,128,576]{2,1,0:T(8,128)(2,1)} %get-tuple-element.31) | copy-start | bytes 1327108
  56.8 22.2 %all-to-all-start.2 = ((bf16[4,4,2,16,1024]{4,3,2,1,0:T(8,128)(2,1)}), bf16[4,4,2,16,1024]{4,3,2,1,0:T(8,128)(2,1)S(1)}, u32[]{:S(2)}, u32[]{:S(2)}) async-start(bf16[4,4,2,16,1024]{4,3,2,1,0:T(8,128)(2,1)} %get-tuple-element.30), calls=%async_computation.2 | async-start | bytes 2097152 | tf_op jit(solution)/shard_map/all_to_all | solution.py:421
  62.7 15.5 %collective-permute-start.5 = (bf16[128,576]{1,0:T(8,128)(2,1)S(1)}, bf16[128,576]{1,0:T(8,128)(2,1)S(1)}, u32[]{:S(2)}, u32[]{:S(2)}) collective-permute-start(bf16[128,576]{1,0:T(8,128)(2,1)S(1)} %fusion.4), channel_id=1, source_target_pairs={{32,0},{48,16},{64,32},{80,48},{96,64},{112,80},{128,96},{144,112}... | collective-permute-start | bytes 442376 | tf_op jit(solution)/shard_map/ppermute | solution.py:418
  80.0 4.7 %copy-start.13 = (bf16[128,768]{1,0:T(8,128)(2,1)S(1)}, bf16[128,768]{1,0:T(8,128)(2,1)}, u32[]{:S(2)}) copy-start(bf16[128,768]{1,0:T(8,128)(2,1)} %get-tuple-element.36) | copy-start | bytes 589828
  80.0 11.5 %copy-start.2 = (bf16[128,768]{1,0:T(8,128)(2,1)S(1)}, bf16[128,768]{1,0:T(8,128)(2,1)}, u32[]{:S(2)}) copy-start(bf16[128,768]{1,0:T(8,128)(2,1)} %get-tuple-element.35.kept) | copy-start | bytes 589828
  80.0 20.7 %all-to-all-start.3 = ((bf16[8,16,1024]{2,1,0:T(8,128)(2,1)}), bf16[8,16,1024]{2,1,0:T(8,128)(2,1)S(1)}, u32[]{:S(2)}, u32[]{:S(2)}) async-start(bf16[8,16,1024]{2,1,0:T(8,128)(2,1)} %bitcast.9), calls=%async_computation.3 | async-start | bytes 524288 | tf_op jit(solution)/shard_map/all_to_all | solution.py:421
  84.7 6.8 %collective-permute-start.7 = (bf16[128,768]{1,0:T(8,128)(2,1)S(1)}, bf16[128,768]{1,0:T(8,128)(2,1)S(1)}, u32[]{:S(2)}, u32[]{:S(2)}) collective-permute-start(bf16[128,768]{1,0:T(8,128)(2,1)S(1)} %copy-done.13), channel_id=1, source_target_pairs={{0,16},{16,0},{32,48},{48,32},{64,80},{80,64},{96,112},{112,96},{1... | collective-permute-start | bytes 589832 | tf_op jit(solution)/shard_map/ppermute | solution.py:414
  87.1 12.9 %collective-permute-start.6 = (bf16[128,576]{1,0:T(8,128)(2,1)S(1)}, bf16[128,576]{1,0:T(8,128)(2,1)S(1)}, u32[]{:S(2)}, u32[]{:S(2)}) collective-permute-start(bf16[128,576]{1,0:T(8,128)(2,1)S(1)} %fusion.3), channel_id=1, source_target_pairs={{32,0},{48,16},{64,32},{80,48},{96,64},{112,80},{128,96},{144,112}... | collective-permute-start | bytes 442376 | tf_op jit(solution)/shard_map/ppermute | solution.py:418
  100.7 34.2 %all-to-all-start.4 = ((bf16[16,8,576]{2,1,0:T(8,128)(2,1)}), bf16[16,8,576]{2,1,0:T(8,128)(2,1)S(1)}, u32[]{:S(2)}, u32[]{:S(2)}) async-start(bf16[16,8,576]{2,1,0:T(8,128)(2,1)} %bitcast.11), calls=%async_computation.4 | async-start | bytes 327680 | tf_op jit(solution)/shard_map/all_to_all | solution.py:453

commit v5 on v4

--- a/solution.py
+++ b/solution.py
@@ -438,21 +438,22 @@
     sums = grad_kept.astype(jnp.float32) + got.astype(jnp.float32)
     far_sum = sums[0].astype(jnp.bfloat16)
     shares = exchanged(d_weights, along_y)
-    near_sum = (sums[1] + to_chip(far_sum, -1).astype(jnp.float32)).astype(jnp.bfloat16)
-    shares, near_sum = lax.optimization_barrier((shares, near_sum))
+    near_sum = sums[1].astype(jnp.bfloat16)
+    total = sums[2] + to_chip(near_sum, -1).astype(jnp.float32)
+    total = (total + to_chip(far_sum, -2).astype(jnp.float32)).astype(jnp.bfloat16)
+    shares, total = lax.optimization_barrier((shares, total))
+    heads_over = lax.axis_size("head")
+    key_terms = lax.all_to_all(total, "head", 0, 0, tiled=True)
     d_column = jnp.sum(shares.astype(jnp.float32), axis=0).astype(jnp.bfloat16)
-    d_shares = exchanged(d_column.reshape(2 * steps, piece, width), along_z)
-    total = (sums[2] + to_chip(near_sum, -1).astype(jnp.float32)).astype(jnp.bfloat16)
+    key_terms, d_column = lax.optimization_barrier((key_terms, d_column))
     returned = swapped(d_lent)
     d_q_nope, d_q_rope = join_heads(place, d_kept, returned, width, q_rope.shape[1])
-    d_shares, total, d_q_nope = lax.optimization_barrier((d_shares, total, d_q_nope))
+    d_shares = exchanged(d_column.reshape(2 * steps, piece, width), along_z)
+    key_terms = key_terms.reshape(heads_over, rows // heads_over, LAT + ROPE)
+    d_latent, d_k_rope = summed(key_sum_kernel, key_terms, rows // heads_over, (LAT, ROPE))
     d_uk, d_uv = summed(
         up_sum_kernel, d_shares.reshape(steps, 2, piece, width), piece, (width, width)
     )
-    heads_over = lax.axis_size("head")
-    key_terms = lax.all_to_all(total, "head", 0, 0, tiled=True)
-    key_terms = key_terms.reshape(heads_over, rows // heads_over, LAT + ROPE)
-    d_latent, d_k_rope = summed(key_sum_kernel, key_terms, rows // heads_over, (LAT, ROPE))
     return (d_q_nope, d_q_rope, d_latent, d_k_rope, d_uk, d_uv)
 
 

time: 136 us -> 135 us (level)
  the two profiles are of different devices: /device:TPU:24 before, /device:TPU:1 now
where the time goes in v5:
time: 135 us; the launch traced here: 134 us
  starting transfers between devices  63.7 us (47%)
  waiting for transfers between devices  48.9 us (36%)
  Pallas kernels  15.4 us (11%)
  local copies, waits for them, and re-layouts  3.59 us (3%)
  other arithmetic  1.89 us (1%)
    all_to_all x4, starting transfers between devices, exchanged(): lax.all_to_all(value, 'ctx', 0, 0, axis_index_groups=groups, tiled=True)  31.3 us
    ppermute x4, waiting for transfers between devices, to_chip(): lax.ppermute(value, 'ctx', [pair for pair in pairs if 0 <= pair[1] < count])  23.4 us
    all_to_all x1, waiting for transfers between devices, on_device(): key_terms = lax.all_to_all(total, 'head', 0, 0, tiled=True)  13.7 us
    all_to_all x1, starting transfers between devices, on_device(): key_terms = lax.all_to_all(total, 'head', 0, 0, tiled=True)  12.8 us
    ppermute x4, starting transfers between devices, swapped(): lax.ppermute(value, 'ctx', [(source, source ^ 1) for source in range(coun...  12.1 us
    pallas_call x1, Pallas kernels, layer(): pl.pallas_call(layer_kernel, out_shape=(jax.ShapeDtypeStruct((rows, d_pac...  11.4 us
    all_to_all x4, waiting for transfers between devices, exchanged(): lax.all_to_all(value, 'ctx', 0, 0, axis_index_groups=groups, tiled=True)  8.75 us
    ppermute x4, starting transfers between devices, to_chip(): lax.ppermute(value, 'ctx', [pair for pair in pairs if 0 <= pair[1] < count])  7.53 us
  transfers between devices with their start and end apart: 13, of which 8 were waited for; matrix products, arithmetic and copies ran while one was open for 2% of the time, Pallas kernels for 1%

profile of v5, /device:TPU:1, one launch (start us, length us, event | category | flops | bytes accessed | tf_op | source)
XLA Modules:
  0.0 134.4 jit_solution(13747437119734732859)
XLA Ops:
  0.6 1.8 %shard_map.137 = bf16[8,16,1024]{2,1,0:T(8,128)(2,1)} custom-call(bf16[16,1024]{1,0:T(8,128)(2,1)} %left.1, bf16[16,1024]{1,0:T(8,128)(2,1)} %right.1), custom_call_target="tpu_custom_call" | custom-call | flops 100000 | bytes 300000 | tf_op jit(solution)/shard_map/pallas_call | solution.py:356
  2.4 0.0 copy-start.10
  2.4 0.0 copy-start.9
  2.5 10.3 %all-to-all-start = ((bf16[8,16,1024]{2,1,0:T(8,128)(2,1)}), bf16[8,16,1024]{2,1,0:T(8,128)(2,1)S(1)}, u32[]{:S(2)}, u32[]{:S(2)}) async-start(bf16[8,16,1024]{2,1,0:T(8,128)(2,1)} %shard_map.137), calls=%async_computation | async-start | bytes 524288 | tf_op jit(solution)/shard_map/all_to_all | solution.py:421
  12.8 0.0 copy-done.10
  12.8 0.1 copy.15
  12.9 0.0 copy-done.9
  13.0 1.3 collective-permute-start.2
  14.3 3.6 %collective-permute-start.1 = (bf16[128,576]{1,0:T(8,128)(2,1)S(1)}, bf16[128,576]{1,0:T(8,128)(2,1)S(1)}, u32[]{:S(2)}, u32[]{:S(2)}) collective-permute-start(bf16[128,576]{1,0:T(8,128)(2,1)S(1)} %get-tuple-element.48), channel_id=1, source_target_pairs={{0,64},{16,80},{32,96},{48,112},{64,128},{80,144},{96,160},{112,17... | collective-permute-start | bytes 442376 | tf_op jit(solution)/shard_map/ppermute | solution.py:418
  17.9 0.0 collective-permute-done.2
  18.0 3.2 %collective-permute-done.1 = bf16[128,576]{1,0:T(8,128)(2,1)S(1)} collective-permute-done((bf16[128,576]{1,0:T(8,128)(2,1)S(1)}, bf16[128,576]{1,0:T(8,128)(2,1)S(1)}, u32[]{:S(2)}, u32[]{:S(2)}) %collective-permute-start.1) | collective-permute-done | bytes 147488 | tf_op jit(solution)/shard_map/ppermute | solution.py:418
  21.2 0.1 pad_maximum_fusion.keys_near
  21.3 0.0 copy-start.8
  21.3 0.2 all-to-all-done
  21.5 1.1 broadcast_in_dim.2
  22.6 0.0 copy-start
  22.6 0.0 copy-start.1
  22.6 0.0 copy-start.3
  22.6 7.2 %all-to-all-start.1 = ((bf16[4,8,16,1024]{3,2,1,0:T(8,128)(2,1)}), bf16[4,8,16,1024]{3,2,1,0:T(8,128)(2,1)S(1)}, u32[]{:S(2)}, u32[]{:S(2)}) async-start(bf16[4,8,16,1024]{3,2,1,0:T(8,128)(2,1)} %broadcast_in_dim.2), calls=%async_computation.1 | async-start | bytes 2097152 | tf_op jit(solution)/shard_map/all_to_all | solution.py:421
  29.8 0.0 copy-done.8
  29.8 3.7 %collective-permute-start.3 = (bf16[3,128,576]{2,1,0:T(8,128)(2,1)S(1)}, bf16[3,128,576]{2,1,0:T(8,128)(2,1)S(1)}, u32[]{:S(2)}, u32[]{:S(2)}) collective-permute-start(bf16[3,128,576]{2,1,0:T(8,128)(2,1)S(1)} %pad_maximum_fusion.keys_near), channel_id=1, source_target_pairs={{0,16},{16,0},{32,48},{48,32},{64,80},{80,64},{96,112},{112,96},{1... | collective-permute-start | bytes 1327112 | tf_op jit(solution)/shard_map/ppermute | solution.py:414
  33.5 0.0 copy-start.4
  33.5 0.0 copy-done
  33.5 0.0 copy-done.1
  33.5 0.0 copy-done.3
  33.5 0.6 copy-done.4
  34.1 0.2 shard_map.136
  34.3 0.0 copy-start.5
  34.3 0.7 copy-done.5
  35.0 1.9 %collective-permute-start = (bf16[128,1280]{1,0:T(8,128)(2,1)S(1)}, bf16[128,1280]{1,0:T(8,128)(2,1)S(1)}, u32[]{:S(2)}, u32[]{:S(2)}) collective-permute-start(bf16[128,1280]{1,0:T(8,128)(2,1)S(1)} %get-tuple-element.26), channel_id=1, source_target_pairs={{0,16},{16,0},{32,48},{48,32},{64,80},{80,64},{96,112},{112,96},{1... | collective-permute-start | bytes 983048 | tf_op jit(solution)/shard_map/ppermute | solution.py:414
  37.0 1.6 %collective-permute-done.rows_lent = bf16[128,1280]{1,0:T(8,128)(2,1)S(1)} collective-permute-done((bf16[128,1280]{1,0:T(8,128)(2,1)S(1)}, bf16[128,1280]{1,0:T(8,128)(2,1)S(1)}, u32[]{:S(2)}, u32[]{:S(2)}) %collective-permute-start) | collective-permute-done | bytes 327712 | tf_op jit(solution)/shard_map/ppermute | solution.py:414
  38.6 0.0 copy-start.12
  38.6 0.0 collective-permute-done.3.keys_far
  38.6 0.0 copy-start.11
  38.6 4.6 %all-to-all-done.1 = bf16[4,8,16,1024]{3,2,1,0:T(8,128)(2,1)S(1)} async-done(((bf16[4,8,16,1024]{3,2,1,0:T(8,128)(2,1)}), bf16[4,8,16,1024]{3,2,1,0:T(8,128)(2,1)S(1)}, u32[]{:S(2)}, u32[]{:S(2)}) %all-to-all-start.1) | async-done | bytes 1048608 | tf_op jit(solution)/shard_map/all_to_all | solution.py:421
  43.1 0.0 copy-start.6
  43.1 0.0 copy-done.12
  43.1 0.0 copy-done.11
  43.1 1.0 copy-done.6
  44.1 11.4 %shard_map.138 = (bf16[128,768]{1,0:T(8,128)(2,1)}, bf16[128,768]{1,0:T(8,128)(2,1)}, bf16[3,128,576]{2,1,0:T(8,128)(2,1)}, bf16[3,128,576]{2,1,0:T(8,128)(2,1)}, bf16[4,4,2,16,1024]{4,3,2,1,0:T(8,128)(2,1)}) custom-call(s32[1]{0:T(128)} %bitcast.place, s32[32,128]{1,0:T(8,128)} %bitcast.30, bf16[128,1280]{1,0:T(8,128)(2,1)} %copy-done.5, ...), custom_call_target="tpu_custom_call" | custom-call | flops 5000000000 | bytes 8000000 | tf_op jit(solution)/shard_map/pallas_call | solution.py:282
  55.5 4.6 %collective-permute-start.5 = (bf16[3,128,576]{2,1,0:T(8,128)(2,1)}, bf16[3,128,576]{2,1,0:T(8,128)(2,1)S(1)}, u32[]{:S(2)}, u32[]{:S(2)}) collective-permute-start(bf16[3,128,576]{2,1,0:T(8,128)(2,1)} %get-tuple-element.35), channel_id=1, source_target_pairs={{0,16},{16,0},{32,48},{48,32},{64,80},{80,64},{96,112},{112,96},{1... | collective-permute-start | bytes 1327112 | tf_op jit(solution)/shard_map/ppermute | solution.py:414
  60.1 0.0 copy-start.7
  60.1 3.7 %all-to-all-start.2 = ((bf16[4,4,2,16,1024]{4,3,2,1,0:T(8,128)(2,1)}), bf16[4,4,2,16,1024]{4,3,2,1,0:T(8,128)(2,1)S(1)}, u32[]{:S(2)}, u32[]{:S(2)}) async-start(bf16[4,4,2,16,1024]{4,3,2,1,0:T(8,128)(2,1)} %get-tuple-element.33), calls=%async_computation.2 | async-start | bytes 2097152 | tf_op jit(solution)/shard_map/all_to_all | solution.py:421
  63.8 0.0 collective-permute-done.5
  63.8 0.0 copy-done.7
  63.8 0.1 fusion.4
  64.0 1.3 collective-permute-start.6
  65.3 1.3 collective-permute-start.7
  66.6 20.1 %collective-permute-done.6 = bf16[128,576]{1,0:T(8,128)(2,1)S(1)} collective-permute-done((bf16[128,576]{1,0:T(8,128)(2,1)S(1)}, bf16[128,576]{1,0:T(8,128)(2,1)S(1)}, u32[]{:S(2)}, u32[]{:S(2)}) %collective-permute-start.6) | collective-permute-done | bytes 147488 | tf_op jit(solution)/shard_map/ppermute | solution.py:418
  86.7 0.0 collective-permute-done.7
  86.7 0.7 fusion.2
  87.4 0.0 all-to-all-done.2
  87.4 12.8 %all-to-all-start.3 = ((bf16[16,8,576]{2,1,0:T(8,128)(2,1)}), bf16[16,8,576]{2,1,0:T(8,128)(2,1)S(1)}, u32[]{:S(2)}, u32[]{:S(2)}) async-start(bf16[16,8,576]{2,1,0:T(8,128)(2,1)} %bitcast.10), calls=%async_computation.3 | async-start | bytes 327680 | tf_op jit(solution)/shard_map/all_to_all | solution.py:446
  100.3 0.9 reduce_sum.12
  101.2 13.7 %all-to-all-done.3 = bf16[16,8,576]{2,1,0:T(8,128)(2,1)S(1)} async-done(((bf16[16,8,576]{2,1,0:T(8,128)(2,1)}), bf16[16,8,576]{2,1,0:T(8,128)(2,1)S(1)}, u32[]{:S(2)}, u32[]{:S(2)}) %all-to-all-start.3) | async-done | bytes 147488 | tf_op jit(solution)/shard_map/all_to_all | solution.py:446
  114.9 10.1 %all-to-all-start.4 = ((bf16[8,16,1024]{2,1,0:T(8,128)(2,1)}), bf16[8,16,1024]{2,1,0:T(8,128)(2,1)S(1)}, u32[]{:S(2)}, u32[]{:S(2)}) async-start(bf16[8,16,1024]{2,1,0:T(8,128)(2,1)} %bitcast.13), calls=%async_computation.4 | async-start | bytes 524288 | tf_op jit(solution)/shard_map/all_to_all | solution.py:421
  125.0 0.0 copy-done.13
  125.0 1.9 %collective-permute-start.4 = (bf16[128,768]{1,0:T(8,128)(2,1)S(1)}, bf16[128,768]{1,0:T(8,128)(2,1)S(1)}, u32[]{:S(2)}, u32[]{:S(2)}) collective-permute-start(bf16[128,768]{1,0:T(8,128)(2,1)S(1)} %copy-done.13), channel_id=1, source_target_pairs={{0,16},{16,0},{32,48},{48,32},{64,80},{80,64},{96,112},{112,96},{1... | collective-permute-start | bytes 589832 | tf_op jit(solution)/shard_map/ppermute | solution.py:414
  127.0 1.4 %collective-permute-done.4.returned = bf16[128,768]{1,0:T(8,128)(2,1)S(1)} collective-permute-done((bf16[128,768]{1,0:T(8,128)(2,1)S(1)}, bf16[128,768]{1,0:T(8,128)(2,1)S(1)}, u32[]{:S(2)}, u32[]{:S(2)}) %collective-permute-start.4) | collective-permute-done | bytes 196640 | tf_op jit(solution)/shard_map/ppermute | solution.py:414
  128.4 0.0 copy-done.2
  128.4 0.8 shard_map.139
  129.1 0.6 shard_map.140
  129.8 4.0 %all-to-all-done.4 = bf16[8,16,1024]{2,1,0:T(8,128)(2,1)S(1)} async-done(((bf16[8,16,1024]{2,1,0:T(8,128)(2,1)}), bf16[8,16,1024]{2,1,0:T(8,128)(2,1)S(1)}, u32[]{:S(2)}, u32[]{:S(2)}) %all-to-all-start.4) | async-done | bytes 262176 | tf_op jit(solution)/shard_map/all_to_all | solution.py:421
  133.8 0.7 shard_map.141
  (4 shorter events, 0.1 us)
Async XLA Ops:
  2.4 10.4 %copy-start.10 = (bf16[128,64]{0,1:T(8,128)(2,1)S(1)}, bf16[128,64]{0,1:T(8,128)(2,1)}, u32[]{:S(2)}) copy-start(bf16[128,64]{0,1:T(8,128)(2,1)} %param.12) | copy-start | bytes 49156
  2.4 10.5 %copy-start.9 = (bf16[128,512]{1,0:T(8,128)(2,1)S(1)}, bf16[128,512]{1,0:T(8,128)(2,1)}, u32[]{:S(2)}) copy-start(bf16[128,512]{1,0:T(8,128)(2,1)} %param.11) | copy-start | bytes 393220
  2.5 19.1 %all-to-all-start = ((bf16[8,16,1024]{2,1,0:T(8,128)(2,1)}), bf16[8,16,1024]{2,1,0:T(8,128)(2,1)S(1)}, u32[]{:S(2)}, u32[]{:S(2)}) async-start(bf16[8,16,1024]{2,1,0:T(8,128)(2,1)} %shard_map.137), calls=%async_computation | async-start | bytes 524288 | tf_op jit(solution)/shard_map/all_to_all | solution.py:421
  13.0 5.0 %collective-permute-start.2 = (bf16[128,576]{1,0:T(8,128)(2,1)S(1)}, bf16[128,576]{1,0:T(8,128)(2,1)S(1)}, u32[]{:S(2)}, u32[]{:S(2)}) collective-permute-start(bf16[128,576]{1,0:T(8,128)(2,1)S(1)} %get-tuple-element.48), channel_id=1, source_target_pairs={{0,32},{16,48},{32,64},{48,80},{64,96},{80,112},{96,128},{112,144}... | collective-permute-start | bytes 442376 | tf_op jit(solution)/shard_map/ppermute | solution.py:418
  14.3 6.9 %collective-permute-start.1 = (bf16[128,576]{1,0:T(8,128)(2,1)S(1)}, bf16[128,576]{1,0:T(8,128)(2,1)S(1)}, u32[]{:S(2)}, u32[]{:S(2)}) collective-permute-start(bf16[128,576]{1,0:T(8,128)(2,1)S(1)} %get-tuple-element.48), channel_id=1, source_target_pairs={{0,64},{16,80},{32,96},{48,112},{64,128},{80,144},{96,160},{112,17... | collective-permute-start | bytes 442376 | tf_op jit(solution)/shard_map/ppermute | solution.py:418
  21.3 8.5 %copy-start.8 = (bf16[3,128,576]{2,1,0:T(8,128)(2,1)}, bf16[3,128,576]{2,1,0:T(8,128)(2,1)S(1)}, u32[]{:S(2)}) copy-start(bf16[3,128,576]{2,1,0:T(8,128)(2,1)S(1)} %pad_maximum_fusion.keys_near) | copy-start | bytes 1327108
  22.6 10.9 %copy-start = (bf16[128,1024]{1,0:T(8,128)(2,1)S(1)}, bf16[128,1024]{1,0:T(8,128)(2,1)}, u32[]{:S(2)}) copy-start(bf16[128,1024]{1,0:T(8,128)(2,1)} %queries.1) | copy-start | bytes 786436
  22.6 10.9 %copy-start.1 = (bf16[128,1024]{1,0:T(8,128)(2,1)S(1)}, bf16[128,1024]{1,0:T(8,128)(2,1)}, u32[]{:S(2)}) copy-start(bf16[128,1024]{1,0:T(8,128)(2,1)} %cotangent.1) | copy-start | bytes 786436
  22.6 10.9 %copy-start.3 = (bf16[128,512]{1,0:T(8,128)(2,1)S(1)}, bf16[128,512]{1,0:T(8,128)(2,1)}, u32[]{:S(2)}) copy-start(bf16[128,512]{1,0:T(8,128)(2,1)} %rotated.1) | copy-start | bytes 393220
  22.6 20.5 %all-to-all-start.1 = ((bf16[4,8,16,1024]{3,2,1,0:T(8,128)(2,1)}), bf16[4,8,16,1024]{3,2,1,0:T(8,128)(2,1)S(1)}, u32[]{:S(2)}, u32[]{:S(2)}) async-start(bf16[4,8,16,1024]{3,2,1,0:T(8,128)(2,1)} %broadcast_in_dim.2), calls=%async_computation.1 | async-start | bytes 2097152 | tf_op jit(solution)/shard_map/all_to_all | solution.py:421
  29.8 8.8 %collective-permute-start.3 = (bf16[3,128,576]{2,1,0:T(8,128)(2,1)S(1)}, bf16[3,128,576]{2,1,0:T(8,128)(2,1)S(1)}, u32[]{:S(2)}, u32[]{:S(2)}) collective-permute-start(bf16[3,128,576]{2,1,0:T(8,128)(2,1)S(1)} %pad_maximum_fusion.keys_near), channel_id=1, source_target_pairs={{0,16},{16,0},{32,48},{48,32},{64,80},{80,64},{96,112},{112,96},{1... | collective-permute-start | bytes 1327112 | tf_op jit(solution)/shard_map/ppermute | solution.py:414
  33.5 0.7 copy-start.4
  34.3 0.7 copy-start.5
  35.0 3.5 %collective-permute-start = (bf16[128,1280]{1,0:T(8,128)(2,1)S(1)}, bf16[128,1280]{1,0:T(8,128)(2,1)S(1)}, u32[]{:S(2)}, u32[]{:S(2)}) collective-permute-start(bf16[128,1280]{1,0:T(8,128)(2,1)S(1)} %get-tuple-element.26), channel_id=1, source_target_pairs={{0,16},{16,0},{32,48},{48,32},{64,80},{80,64},{96,112},{112,96},{1... | collective-permute-start | bytes 983048 | tf_op jit(solution)/shard_map/ppermute | solution.py:414
  38.6 4.6 %copy-start.12 = (bf16[128,1280]{1,0:T(8,128)(2,1)}, bf16[128,1280]{1,0:T(8,128)(2,1)S(1)}, u32[]{:S(2)}) copy-start(bf16[128,1280]{1,0:T(8,128)(2,1)S(1)} %collective-permute-done.rows_lent) | copy-start | bytes 983044
  38.6 4.6 %copy-start.11 = (bf16[3,128,576]{2,1,0:T(8,128)(2,1)}, bf16[3,128,576]{2,1,0:T(8,128)(2,1)S(1)}, u32[]{:S(2)}) copy-start(bf16[3,128,576]{2,1,0:T(8,128)(2,1)S(1)} %collective-permute-done.3.keys_far) | copy-start | bytes 1327108
  43.1 1.0 copy-start.6
  55.5 8.3 %collective-permute-start.5 = (bf16[3,128,576]{2,1,0:T(8,128)(2,1)}, bf16[3,128,576]{2,1,0:T(8,128)(2,1)S(1)}, u32[]{:S(2)}, u32[]{:S(2)}) collective-permute-start(bf16[3,128,576]{2,1,0:T(8,128)(2,1)} %get-tuple-element.35), channel_id=1, source_target_pairs={{0,16},{16,0},{32,48},{48,32},{64,80},{80,64},{96,112},{112,96},{1... | collective-permute-start | bytes 1327112 | tf_op jit(solution)/shard_map/ppermute | solution.py:414
  60.1 3.7 %copy-start.7 = (bf16[3,128,576]{2,1,0:T(8,128)(2,1)S(1)}, bf16[3,128,576]{2,1,0:T(8,128)(2,1)}, u32[]{:S(2)}) copy-start(bf16[3,128,576]{2,1,0:T(8,128)(2,1)} %get-tuple-element.34) | copy-start | bytes 1327108
  60.1 27.3 %all-to-all-start.2 = ((bf16[4,4,2,16,1024]{4,3,2,1,0:T(8,128)(2,1)}), bf16[4,4,2,16,1024]{4,3,2,1,0:T(8,128)(2,1)S(1)}, u32[]{:S(2)}, u32[]{:S(2)}) async-start(bf16[4,4,2,16,1024]{4,3,2,1,0:T(8,128)(2,1)} %get-tuple-element.33), calls=%async_computation.2 | async-start | bytes 2097152 | tf_op jit(solution)/shard_map/all_to_all | solution.py:421
  64.0 22.7 %collective-permute-start.6 = (bf16[128,576]{1,0:T(8,128)(2,1)S(1)}, bf16[128,576]{1,0:T(8,128)(2,1)S(1)}, u32[]{:S(2)}, u32[]{:S(2)}) collective-permute-start(bf16[128,576]{1,0:T(8,128)(2,1)S(1)} %get-tuple-element.46), channel_id=1, source_target_pairs={{32,0},{48,16},{64,32},{80,48},{96,64},{112,80},{128,96},{144,112}... | collective-permute-start | bytes 442376 | tf_op jit(solution)/shard_map/ppermute | solution.py:418
  65.3 21.4 %collective-permute-start.7 = (bf16[128,576]{1,0:T(8,128)(2,1)S(1)}, bf16[128,576]{1,0:T(8,128)(2,1)S(1)}, u32[]{:S(2)}, u32[]{:S(2)}) collective-permute-start(bf16[128,576]{1,0:T(8,128)(2,1)S(1)} %get-tuple-element.47), channel_id=1, source_target_pairs={{64,0},{80,16},{96,32},{112,48},{128,64},{144,80},{160,96},{176,11... | collective-permute-start | bytes 442376 | tf_op jit(solution)/shard_map/ppermute | solution.py:418
  87.4 27.5 %all-to-all-start.3 = ((bf16[16,8,576]{2,1,0:T(8,128)(2,1)}), bf16[16,8,576]{2,1,0:T(8,128)(2,1)S(1)}, u32[]{:S(2)}, u32[]{:S(2)}) async-start(bf16[16,8,576]{2,1,0:T(8,128)(2,1)} %bitcast.10), calls=%async_computation.3 | async-start | bytes 327680 | tf_op jit(solution)/shard_map/all_to_all | solution.py:446
  114.9 10.1 %copy-start.13 = (bf16[128,768]{1,0:T(8,128)(2,1)S(1)}, bf16[128,768]{1,0:T(8,128)(2,1)}, u32[]{:S(2)}) copy-start(bf16[128,768]{1,0:T(8,128)(2,1)} %get-tuple-element.30) | copy-start | bytes 589828
  114.9 13.5 %copy-start.2 = (bf16[128,768]{1,0:T(8,128)(2,1)S(1)}, bf16[128,768]{1,0:T(8,128)(2,1)}, u32[]{:S(2)}) copy-start(bf16[128,768]{1,0:T(8,128)(2,1)} %get-tuple-element.29.kept) | copy-start | bytes 589828
  114.9 18.8 %all-to-all-start.4 = ((bf16[8,16,1024]{2,1,0:T(8,128)(2,1)}), bf16[8,16,1024]{2,1,0:T(8,128)(2,1)S(1)}, u32[]{:S(2)}, u32[]{:S(2)}) async-start(bf16[8,16,1024]{2,1,0:T(8,128)(2,1)} %bitcast.13), calls=%async_computation.4 | async-start | bytes 524288 | tf_op jit(solution)/shard_map/all_to_all | solution.py:421
  125.0 3.3 %collective-permute-start.4 = (bf16[128,768]{1,0:T(8,128)(2,1)S(1)}, bf16[128,768]{1,0:T(8,128)(2,1)S(1)}, u32[]{:S(2)}, u32[]{:S(2)}) collective-permute-start(bf16[128,768]{1,0:T(8,128)(2,1)S(1)} %copy-done.13), channel_id=1, source_target_pairs={{0,16},{16,0},{32,48},{48,32},{64,80},{80,64},{96,112},{112,96},{1... | collective-permute-start | bytes 589832 | tf_op jit(solution)/shard_map/ppermute | solution.py:414
